TPU v7x, 256 devices: a whole 4x4x8 slice. The times are simulated.
256 devices in a mesh: replica: 64 (over y, x_hi, z), mp: 4 (over x_lo, core).
Axes of the slice: x: 4 (x_hi: 2, x_lo: 2; x = x_hi * 2 + x_lo), y: 4, z: 8, core: 2. Of those that a mesh axis runs over, the one named last changes fastest.
Arguments:
- local_weights: bfloat16 [64, 4, 16, 16384], P('replica', None, None, 'mp')
- outer_weights: float32 [4, 16, 16384], P(None, None, 'mp')
- momentum: float32 [4, 16, 16384], P(None, None, 'mp'), may hold values from -1.8 to 1.8
- plan: int32 [4], replicated, may hold values from 0 to 3, each once
Outputs:
- new_outer: float32 [2, 16, 16384], P(None, None, 'mp')
- new_moment: float32 [2, 16, 16384], P(None, None, 'mp')
- merged: bfloat16 [64, 2, 16, 16384], P('replica', None, None, 'mp')
Inputs may be any that keep to these rules, and one draw needn't show every extreme that they name: `plan`: each fragment number appears once; the first 2 entries name the fragments synchronized now.
All inputs are finite; a program needn't handle non-finite values. Where the computation divides by a largest or mean magnitude, that divisor is 1e-20 or more.
Results may differ from a plain program's by a relative error of at most 0.001.
Values sent between devices are 32-bit elements; how exact they have to be, the bound alone decides.
No kernel may reach another device: no remote copies, remote signals or barrier semaphores. Data moves between devices by JAX's collectives and lax.ppermute only.
A program may use at most 192 MiB of HBM per device.

v0:
```python
import jax
import jax.numpy as jnp
from jax import lax
from jax.sharding import PartitionSpec as P

SYNCED = 2
BLOCK = 128


EPS = 1e-06
CLIP = 0.2
MU = 0.9
LR = 0.7
MIX = 0.5


def dequantized(diff):
    shape = diff.shape
    blocks = diff.reshape(shape[:-1] + (shape[-1] // BLOCK, BLOCK))
    scale = jnp.max(jnp.abs(blocks), axis=-1, keepdims=True) + EPS
    coded = lax.optimization_barrier((blocks / scale).astype(jnp.bfloat16))
    return (coded.astype(jnp.float32) * scale).reshape(shape)


def refresh(local_part, outer_part, moment_part):
    frag_count, rows, cols = outer_part.shape
    workers = lax.axis_size("replica")
    entries = rows * cols * lax.axis_size("mp")
    coded = dequantized(outer_part - local_part[0].astype(jnp.float32))
    pseudo = lax.psum(coded, "replica") / workers
    squares = lax.psum(jnp.sum(pseudo * pseudo, axis=(1, 2)), "mp")
    factor = jnp.minimum(1.0, CLIP / jnp.sqrt(squares / entries + EPS))[:, None, None]
    grad = pseudo * factor
    moment_next = MU * moment_part + grad
    outer_next = outer_part - LR * (MU * moment_next + grad)
    mixed = (MIX * local_part.astype(jnp.float32) + (1.0 - MIX) * outer_next[None]).astype(
        jnp.bfloat16
    )
    return (outer_next, moment_next, mixed)


def shards(local_weights, outer_weights, momentum, plan):
    chosen = plan[:SYNCED]
    local_sel = jnp.take(local_weights, chosen, axis=1)
    outer_sel = jnp.take(outer_weights, chosen, axis=0)
    moment_sel = jnp.take(momentum, chosen, axis=0)
    outer_list = []
    moment_list = []
    mixed_list = []
    for number in range(SYNCED):
        outer_one, moment_one, mixed_one = refresh(
            local_sel[:, number : number + 1],
            outer_sel[number : number + 1],
            moment_sel[number : number + 1],
        )
        outer_list.append(outer_one)
        moment_list.append(moment_one)
        mixed_list.append(mixed_one)
    return (
        jnp.concatenate(outer_list, axis=0),
        jnp.concatenate(moment_list, axis=0),
        jnp.concatenate(mixed_list, axis=1),
    )


def solution(mesh):
    return jax.shard_map(
        shards,
        mesh=mesh,
        in_specs=(P("replica", None, None, "mp"), P(None, None, "mp"), P(None, None, "mp"), P()),
        out_specs=(P(None, None, "mp"), P(None, None, "mp"), P("replica", None, None, "mp")),
        check_vma=False,
    )
```

profile of v0, /device:TPU:1, one launch (start us, length us, event | category | flops | bytes accessed | tf_op | source)
XLA Modules:
  0.0 728.1 jit_solution(7669302046812629465)
XLA Ops:
  7.2 0.8 compare_and_fusion
  8.0 1.6 gather_fusion
  9.7 0.6 gather_fusion.2
  10.3 0.6 gather_fusion.1
  10.9 0.1 bitcast_select_fusion
  11.0 0.1 broadcast_select_fusion
  11.2 0.1 copy.7
  11.2 0.1 fusion.10
  11.4 0.1 fusion.11
  11.5 0.1 convert_multiply_fusion.1
  11.7 0.8 reshape.151
  12.4 0.1 copy.8
  12.5 0.1 fusion.8
  12.6 0.1 fusion.9
  12.8 0.1 convert_multiply_fusion
  12.9 0.8 reshape.153
  13.7 649.7 %all-reduce.4.cloned.1.call-done = (f32[1,16,4096]{2,1,0:T(8,128)}, f32[1,16,4096]{2,1,0:T(8,128)}) async-done(((f32[1,16,4096]{2,1,0:T(8,128)}, f32[1,16,4096]{2,1,0:T(8,128)}), (f32[1,16,4096]{2,1,0:T(8,128)}, f32[1,16,4096]{2,1,0:T(8,128)})) %all-reduce.4.cloned.1.call-update) | async-done | bytes 524304 | tf_op jit(solution)/shard_map/psum | solution.py:30
  663.4 1.8 multiply_reduce_fusion
  665.2 52.0 %all-reduce.1 = (f32[1]{0:T(128)}, f32[1]{0:T(128)}) all-reduce(f32[1]{0:T(128)} %bitcast.6, f32[1]{0:T(128)} %bitcast.3), channel_id=1, replica_groups=mesh['replica'=64,'mp'=4] {'mp'}, use_global_device_ids=true, to_apply=%region_7.9 | all-reduce | flops 2 | bytes 16 | tf_op jit(solution)/shard_map/psum | solution.py:31
  718.6 0.2 fusion.3
  718.8 0.1 fusion.13
  718.9 0.8 pad_maximum_fusion.1
  719.7 0.7 pad_maximum_fusion.2
  720.4 0.8 pad_maximum_fusion
  (14 shorter events, 0.1 us)
Async XLA Ops:
  7.2 2.5 copy-start
  7.2 3.1 copy-start.3
  7.2 656.2 %all-reduce.4.cloned.1.call-start = ((), (), s32[]{:S(2)}) async-start(), calls=%async_computation | async-start | bytes 1048576 | tf_op jit(solution)/shard_map/psum | solution.py:30
  663.4 55.2 %copy-start.1 = (f32[1,16,4096]{2,1,0:T(8,128)S(1)}, f32[1,16,4096]{2,1,0:T(8,128)}, u32[]{:S(2)}) copy-start(f32[1,16,4096]{2,1,0:T(8,128)} %get-tuple-element.4) | copy-start | bytes 786436
  663.4 55.2 %copy-start.2 = (f32[1,16,4096]{2,1,0:T(8,128)S(1)}, f32[1,16,4096]{2,1,0:T(8,128)}, u32[]{:S(2)}) copy-start(f32[1,16,4096]{2,1,0:T(8,128)} %get-tuple-element.5) | copy-start | bytes 786436
Sparse Core Ops, SparseCore 0:
  13.8 649.5 all-reduce.3
where the time goes:
time: 728 us
  waiting for transfers between devices  650 us (89%)
  blocking collectives  52 us (7%)
  between operations  15.6 us (2%)
    psum x1, waiting for transfers between devices, refresh(): pseudo = lax.psum(coded, 'replica') / workers  650 us
    psum x1, blocking collectives, refresh(): squares = lax.psum(jnp.sum(pseudo * pseudo, axis=(1, 2)), 'mp')  52 us
  transfers between devices with their start and end apart: 1, of which 1 were waited for; matrix products, arithmetic and copies ran while one was open for 0% of the time, Pallas kernels for 0%

commit v1 on v0

v1 whole, which is shorter than its diff:
```python
import jax
import jax.numpy as jnp
from jax import lax
from jax.experimental import pallas as pl
from jax.experimental.pallas import tpu as pltpu
from jax.sharding import PartitionSpec as P

SYNCED = 2
BLOCK = 128
EPS = 1e-06
CLIP = 0.2
MU = 0.9
LR = 0.7
MIX = 0.5
VMEM = 40 * 1024 * 1024


def encode_kernel(plan_ref, local_ref, outer_ref, out_ref):
    for b in range(out_ref.shape[0]):
        cols = slice(b * BLOCK, (b + 1) * BLOCK)
        diff = outer_ref[0, :, cols] - local_ref[0, 0, :, cols].astype(jnp.float32)
        scale = jnp.max(jnp.abs(diff), axis=-1, keepdims=True) + EPS
        out_ref[b] = (diff / scale).astype(jnp.bfloat16).astype(jnp.float32) * scale


def encode(plan, local, outer):
    _, frags, rows, cols = local.shape
    blocks = cols // BLOCK
    return pl.pallas_call(
        encode_kernel,
        out_shape=jax.ShapeDtypeStruct((SYNCED * blocks, rows, BLOCK), jnp.float32),
        grid_spec=pltpu.PrefetchScalarGridSpec(
            num_scalar_prefetch=1,
            grid=(SYNCED,),
            in_specs=[
                pl.BlockSpec((1, 1, rows, cols), lambda i, plan: (0, plan[i], 0, 0)),
                pl.BlockSpec((1, rows, cols), lambda i, plan: (plan[i], 0, 0)),
            ],
            out_specs=pl.BlockSpec((blocks, rows, BLOCK), lambda i, plan: (i, 0, 0)),
        ),
        compiler_params=pltpu.CompilerParams(vmem_limit_bytes=VMEM),
        name="encode",
    )(plan, local, outer)


def add_kernel(workers, parts_ref, out_ref):
    total = jnp.sum(parts_ref[...], axis=0) / workers
    out_ref[...] = jnp.broadcast_to(total[None], out_ref.shape)


def add(parts, workers):
    return pl.pallas_call(
        lambda parts_ref, out_ref: add_kernel(workers, parts_ref, out_ref),
        out_shape=jax.ShapeDtypeStruct(parts.shape, jnp.float32),
        compiler_params=pltpu.CompilerParams(vmem_limit_bytes=VMEM),
        name="add",
    )(parts)


def squares_kernel(pseudo_ref, out_ref):
    half = pseudo_ref.shape[0] // SYNCED
    out_ref[...] = jnp.zeros_like(out_ref)
    for f in range(SYNCED):
        part = pseudo_ref[f * half : (f + 1) * half]
        out_ref[f : f + 1] = jnp.broadcast_to(jnp.sum(part * part), (1, BLOCK))


def squares(pseudo):
    return pl.pallas_call(
        squares_kernel,
        out_shape=jax.ShapeDtypeStruct((8, BLOCK), jnp.float32),
        compiler_params=pltpu.CompilerParams(vmem_limit_bytes=VMEM),
        name="squares",
    )(pseudo)


def update_kernel(entries, plan_ref, pseudo_ref, squares_ref, local_ref, outer_ref, moment_ref, new_outer_ref, new_moment_ref, merged_ref):
    f = pl.program_id(0)
    mean = squares_ref[pl.ds(f, 1)] / entries
    factor = jnp.minimum(1.0, CLIP / jnp.sqrt(mean + EPS))
    for b in range(pseudo_ref.shape[0]):
        cols = slice(b * BLOCK, (b + 1) * BLOCK)
        grad = pseudo_ref[b] * factor
        outer = outer_ref[0, :, cols]
        moment_next = MU * moment_ref[0, :, cols] + grad
        outer_next = outer - LR * (MU * moment_next + grad)
        new_moment_ref[0, :, cols] = moment_next
        new_outer_ref[0, :, cols] = outer_next
        local = local_ref[0, 0, :, cols].astype(jnp.float32)
        merged_ref[0, 0, :, cols] = (MIX * local + (1.0 - MIX) * outer_next).astype(jnp.bfloat16)


def update(plan, pseudo, squares_sum, local, outer, moment, entries):
    _, frags, rows, cols = local.shape
    blocks = cols // BLOCK
    chosen = pl.BlockSpec((1, rows, cols), lambda i, plan: (plan[i], 0, 0))
    placed = pl.BlockSpec((1, rows, cols), lambda i, plan: (i, 0, 0))
    return pl.pallas_call(
        lambda *refs: update_kernel(entries, *refs),
        out_shape=(
            jax.ShapeDtypeStruct((SYNCED, rows, cols), jnp.float32),
            jax.ShapeDtypeStruct((SYNCED, rows, cols), jnp.float32),
            jax.ShapeDtypeStruct((1, SYNCED, rows, cols), jnp.bfloat16),
        ),
        grid_spec=pltpu.PrefetchScalarGridSpec(
            num_scalar_prefetch=1,
            grid=(SYNCED,),
            in_specs=[
                pl.BlockSpec((blocks, rows, BLOCK), lambda i, plan: (i, 0, 0)),
                pl.BlockSpec((8, BLOCK), lambda i, plan: (0, 0)),
                pl.BlockSpec((1, 1, rows, cols), lambda i, plan: (0, plan[i], 0, 0)),
                chosen,
                chosen,
            ],
            out_specs=[
                placed,
                placed,
                pl.BlockSpec((1, 1, rows, cols), lambda i, plan: (0, i, 0, 0)),
            ],
        ),
        compiler_params=pltpu.CompilerParams(vmem_limit_bytes=VMEM),
        name="update",
    )(plan, pseudo, squares_sum, local, outer, moment)


def shards(local, outer, moment, plan):
    _, frags, rows, cols = local.shape
    workers = lax.axis_size("replica")
    entries = rows * cols * lax.axis_size("mp")
    pieces = encode(plan, local, outer)
    per_worker = pieces.shape[0] // workers
    parts = lax.all_to_all(pieces, "replica", 0, 0, tiled=True)
    means = add(parts, workers)
    pseudo = lax.all_to_all(means, "replica", 0, 0, tiled=True)
    squares_sum = lax.psum(squares(pseudo), "mp")
    return update(plan, pseudo, squares_sum, local, outer, moment, entries)


def solution(mesh):
    return jax.shard_map(
        shards,
        mesh=mesh,
        in_specs=(P("replica", None, None, "mp"), P(None, None, "mp"), P(None, None, "mp"), P()),
        out_specs=(P(None, None, "mp"), P(None, None, "mp"), P("replica", None, None, "mp")),
        check_vma=False,
    )
```

time: 728 us -> 71.9 us (0.10)
  waiting for transfers between devices: 650 us -> 0 us
  between operations: 15.6 us -> 0.7 us
  blocking collectives: 52 us -> 65.1 us
    psum x1 -> x0, waiting for transfers between devices: 650 us -> none  [refresh(): pseudo = lax.psum(coded, 'replica') / workers]
    all_to_all x0 -> x2, blocking collectives: none -> 55.4 us  [the longest x1 32.3 us: shards(): parts = lax.all_to_all(pieces, 'replica', 0, 0, tiled=True)]
    psum x1, blocking collectives: 52 us -> 9.71 us  [shards(): squares_sum = lax.psum(squares(pseudo), 'mp')]
  transfers between devices with their start and end apart: 1 -> 0, of which waited for: 1 -> 0; matrix products, arithmetic and copies ran while one was open for 0% -> 0% of each run, Pallas kernels for 0% -> 0%
where the time goes in v1:
time: 71.9 us; the launch traced here: 71.6 us
  blocking collectives  65.1 us (91%)
  local copies, waits for them, and re-layouts  2.94 us (4%)
  Pallas kernels  2.85 us (4%)
    all_to_all x1, blocking collectives, shards(): parts = lax.all_to_all(pieces, 'replica', 0, 0, tiled=True)  32.3 us
    all_to_all x1, blocking collectives, shards(): pseudo = lax.all_to_all(means, 'replica', 0, 0, tiled=True)  23.1 us
    psum x1, blocking collectives, shards(): squares_sum = lax.psum(squares(pseudo), 'mp')  9.71 us
    unnamed x14, local copies, waits for them, and re-layouts  2.94 us
    pallas_call x1, Pallas kernels, update(): pl.pallas_call(lambda *refs: update_kernel(entries, *refs), out_shape=(ja...  1.68 us

profile of v1, /device:TPU:1, one launch (start us, length us, event | category | flops | bytes accessed | tf_op | source)
XLA Modules:
  0.0 71.6 jit_solution(4748928155208496616)
XLA Ops:
  0.6 0.0 copy-start
  0.6 1.2 %copy-done = f32[4,16,4096]{2,1,0:T(8,128)S(1)} copy-done((f32[4,16,4096]{2,1,0:T(8,128)S(1)}, f32[4,16,4096]{2,1,0:T(8,128)}, u32[]{:S(2)}) %copy-start) | copy-done | bytes 1048600
  1.9 0.0 copy-start.2
  1.9 1.0 %copy-done.2 = bf16[1,4,16,4096]{3,2,1,0:T(8,128)(2,1)S(1)} copy-done((bf16[1,4,16,4096]{3,2,1,0:T(8,128)(2,1)S(1)}, bf16[1,4,16,4096]{3,2,1,0:T(8,128)(2,1)}, u32[]{:S(2)}) %copy-start.2) | copy-done | bytes 524312
  2.9 0.0 copy-start.5
  2.9 0.7 copy-done.5
  3.6 0.9 %encode.1 = f32[64,16,128]{2,1,0:T(8,128)S(1)} custom-call(s32[4]{0:T(128)S(1)} %copy-done.5, bf16[1,4,16,4096]{3,2,1,0:T(8,128)(2,1)S(1)} %copy-done.2, f32[4,16,4096]{2,1,0:T(8,128)S(1)} %copy-done), custom_call_target="tpu_custom_call" | custom-call | tf_op jit(solution)/shard_map/encode/pallas_call | solution.py:29
  4.5 32.3 %all_to_all.10.parts_ref = f32[64,16,128]{2,1,0:T(8,128)S(1)} all-to-all(f32[64,16,128]{2,1,0:T(8,128)S(1)} %encode.1), channel_id=1, replica_groups=mesh['replica'=64,'mp'=4] {'replica'}, dimensions={0} | all-to-all | bytes 1048576 | tf_op jit(solution)/shard_map/all_to_all | solution.py:132
  36.8 0.0 copy-start.4
  36.8 0.1 add.3
  36.9 0.0 copy-start.1
  36.9 23.1 %all_to_all.11.pseudo_ref.refs_1_ = f32[64,16,128]{2,1,0:T(8,128)S(1)} all-to-all(f32[64,16,128]{2,1,0:T(8,128)S(1)} %add.3), channel_id=1, replica_groups=mesh['replica'=64,'mp'=4] {'replica'}, dimensions={0} | all-to-all | bytes 1048576 | tf_op jit(solution)/shard_map/all_to_all | solution.py:134
  60.0 0.0 copy-start.3
  60.0 0.2 squares.1
  60.2 0.0 copy-start.6
  60.2 9.7 %psum.7.refs_2_ = f32[8,128]{1,0:T(8,128)S(1)} all-reduce(f32[8,128]{1,0:T(8,128)S(1)} %squares.1), channel_id=1, replica_groups=mesh['replica'=64,'mp'=4] {'mp'}, use_global_device_ids=true, to_apply=%region_0.0 | all-reduce | flops 1024 | bytes 8192 | tf_op jit(solution)/shard_map/psum | solution.py:135
  69.9 0.0 copy-done.4
  69.9 0.0 copy-done.1
  69.9 0.0 copy-done.3
  69.9 0.0 copy-done.6
  69.9 1.7 %update.1 = (f32[2,16,4096]{2,1,0:T(8,128)}, f32[2,16,4096]{2,1,0:T(8,128)}, bf16[1,2,16,4096]{3,2,1,0:T(8,128)(2,1)}) custom-call(s32[4]{0:T(128)S(1)} %copy-done.6, f32[64,16,128]{2,1,0:T(8,128)S(1)} %all_to_all.11.pseudo_ref.refs_1_, f32[8,128]{1,0:T(8,128)S(1)} %psum.7.refs_2_, bf16[1,4,16,4096]{3,2,1,0:T(8,128)(2,1)S(1)} %copy-done.3, ...), custom_call_target="tpu_custom_call" | custom-call | tf_op jit(solution)/shard_map/update/pallas_call | solution.py:98
Async XLA Ops:
  0.6 1.2 %copy-start = (f32[4,16,4096]{2,1,0:T(8,128)S(1)}, f32[4,16,4096]{2,1,0:T(8,128)}, u32[]{:S(2)}) copy-start(f32[4,16,4096]{2,1,0:T(8,128)} %refs_4_.1) | copy-start | bytes 3145732
  1.9 1.0 %copy-start.2 = (bf16[1,4,16,4096]{3,2,1,0:T(8,128)(2,1)S(1)}, bf16[1,4,16,4096]{3,2,1,0:T(8,128)(2,1)}, u32[]{:S(2)}) copy-start(bf16[1,4,16,4096]{3,2,1,0:T(8,128)(2,1)} %refs_3_.1) | copy-start | bytes 1572868
  2.9 0.7 copy-start.5
  36.8 33.1 %copy-start.4 = (f32[4,16,4096]{2,1,0:T(8,128)S(1)}, f32[4,16,4096]{2,1,0:T(8,128)}, u32[]{:S(2)}) copy-start(f32[4,16,4096]{2,1,0:T(8,128)} %refs_5_.1) | copy-start | bytes 3145732
  36.9 33.0 %copy-start.1 = (f32[4,16,4096]{2,1,0:T(8,128)S(1)}, f32[4,16,4096]{2,1,0:T(8,128)}, u32[]{:S(2)}) copy-start(f32[4,16,4096]{2,1,0:T(8,128)} %refs_4_.1) | copy-start | bytes 3145732
  60.0 9.9 %copy-start.3 = (bf16[1,4,16,4096]{3,2,1,0:T(8,128)(2,1)S(1)}, bf16[1,4,16,4096]{3,2,1,0:T(8,128)(2,1)}, u32[]{:S(2)}) copy-start(bf16[1,4,16,4096]{3,2,1,0:T(8,128)(2,1)} %refs_3_.1) | copy-start | bytes 1572868
  60.2 9.7 %copy-start.6 = (s32[4]{0:T(128)S(1)}, s32[4]{0:T(128)}, u32[]{:S(2)}) copy-start(s32[4]{0:T(128)} %refs_0_.1) | copy-start | bytes 52

commit v2 on v0

v2 whole, which is shorter than its diff:
```python
import jax
import jax.numpy as jnp
from jax import lax
from jax.experimental import pallas as pl
from jax.experimental.pallas import tpu as pltpu
from jax.sharding import PartitionSpec as P

SYNCED = 2
BLOCK = 128
EPS = 1e-06
CLIP = 0.2
MU = 0.9
LR = 0.7
MIX = 0.5

QUARTERS = 4
SCOPED = 32 * 1024 * 1024
HBM = pl.BlockSpec(memory_space=pltpu.HBM)
VMEM = pl.BlockSpec(memory_space=pltpu.VMEM)
PARAMS = pltpu.CompilerParams(vmem_limit_bytes=SCOPED)


def my_y(workers):
    return lax.axis_index("replica") // (workers // QUARTERS)


def place(y, k, width):
    quarter = jnp.bitwise_xor(y, k)
    per_fragment = QUARTERS // SYNCED
    return quarter // per_fragment, pl.ds(pl.multiple_of((quarter % per_fragment) * width, width), width)


def encode_kernel(workers, plan_hbm, local_hbm, outer_hbm, moment_hbm, *refs):
    out_refs, (outer_ref, local_ref, moment_ref, plan_ref, plan_sem, sems) = refs[:QUARTERS], refs[QUARTERS:]
    width = outer_ref.shape[-1]
    plan_copy = pltpu.make_async_copy(plan_hbm, plan_ref, plan_sem)
    plan_copy.start()
    y = my_y(workers)
    plan_copy.wait()
    order = (1, 2, 3, 0)
    copies = {}
    for k in order:
        number, cols = place(y, k, width)
        f = plan_ref[number]
        copies[k] = (
            pltpu.make_async_copy(outer_hbm.at[f, :, cols], outer_ref.at[k], sems.at[0, k]),
            pltpu.make_async_copy(local_hbm.at[0, f, :, cols], local_ref.at[k], sems.at[1, k]),
            pltpu.make_async_copy(moment_hbm.at[f, :, cols], moment_ref.at[k], sems.at[2, k]),
        )
        copies[k][0].start()
        copies[k][1].start()
    for k in order:
        copies[k][2].start()
    for k in order:
        copies[k][0].wait()
        copies[k][1].wait()
        for b in range(width // BLOCK):
            at = slice(b * BLOCK, (b + 1) * BLOCK)
            diff = outer_ref[k, :, at] - local_ref[k, :, at].astype(jnp.float32)
            scale = jnp.max(jnp.abs(diff), axis=-1, keepdims=True) + EPS
            out_refs[k][b] = (diff / scale).astype(jnp.bfloat16).astype(jnp.float32) * scale
    for k in order:
        copies[k][2].wait()


def encode(plan, local, outer, moment, workers):
    _, frags, rows, cols = local.shape
    width = SYNCED * cols // QUARTERS
    piece = jax.ShapeDtypeStruct((width // BLOCK, rows, BLOCK), jnp.float32)
    kept = lambda dtype: jax.ShapeDtypeStruct((QUARTERS, rows, width), dtype)
    return pl.pallas_call(
        lambda *refs: encode_kernel(workers, *refs),
        out_shape=(piece,) * QUARTERS + (kept(jnp.float32), kept(local.dtype), kept(jnp.float32)),
        in_specs=[HBM] * 4,
        out_specs=(VMEM,) * (QUARTERS + 3),
        scratch_shapes=[
            pltpu.SMEM(plan.shape, jnp.int32),
            pltpu.SemaphoreType.DMA(()),
            pltpu.SemaphoreType.DMA((3, QUARTERS)),
        ],
        compiler_params=PARAMS,
        name="encode",
    )(plan, local, outer, moment)


def add_kernel(*refs):
    *parts, out_ref = refs
    out_ref[...] = (parts[0][...] + parts[1][...]) + (parts[2][...] + parts[3][...])


def add(parts):
    return pl.pallas_call(
        add_kernel,
        out_shape=jax.ShapeDtypeStruct(parts[0].shape, jnp.float32),
        in_specs=[VMEM] * QUARTERS,
        out_specs=VMEM,
        compiler_params=PARAMS,
        name="add",
    )(*parts)


def mean_kernel(workers, parts_ref, out_ref):
    total = jnp.sum(parts_ref[...], axis=0) / workers
    out_ref[...] = jnp.broadcast_to(total[None], out_ref.shape)


def mean(parts, workers):
    return pl.pallas_call(
        lambda *refs: mean_kernel(workers, *refs),
        out_shape=jax.ShapeDtypeStruct(parts.shape, jnp.float32),
        in_specs=[VMEM],
        out_specs=VMEM,
        compiler_params=PARAMS,
        name="mean",
    )(parts)


def squares_kernel(workers, *refs):
    *quarters, out_ref = refs
    y = my_y(workers)
    row = lax.broadcasted_iota(jnp.int32, out_ref.shape, 0)
    total = jnp.zeros(out_ref.shape, jnp.float32)
    sums = [jnp.sum(q[...] * q[...]) for q in quarters]
    for k in range(0, QUARTERS, 2):
        number, _ = place(y, k, BLOCK)
        total = jnp.where(row == number, sums[k] + sums[k + 1], total)
    out_ref[...] = total


def squares(quarters, workers):
    return pl.pallas_call(
        lambda *refs: squares_kernel(workers, *refs),
        out_shape=jax.ShapeDtypeStruct((8, BLOCK), jnp.float32),
        in_specs=[VMEM] * QUARTERS,
        out_specs=VMEM,
        compiler_params=PARAMS,
        name="squares",
    )(*quarters)


def update_kernel(workers, entries, *refs):
    quarters, refs = refs[:QUARTERS], refs[QUARTERS:]
    squares_ref, outer_ref, local_ref, moment_ref, new_outer, new_moment, merged, outer_buf, moment_buf, merged_buf, factor_ref, sems = refs
    width = outer_ref.shape[-1]
    y = my_y(workers)
    factor_ref[...] = jnp.minimum(1.0, CLIP / jnp.sqrt(squares_ref[...] / entries + EPS))
    copies = []
    for k in range(QUARTERS):
        number, cols = place(y, k, width)
        factor = factor_ref[pl.ds(number, 1)]
        for b in range(width // BLOCK):
            at = slice(b * BLOCK, (b + 1) * BLOCK)
            grad = quarters[k][b] * factor
            moment_next = MU * moment_ref[k, :, at] + grad
            outer_next = outer_ref[k, :, at] - LR * (MU * moment_next + grad)
            moment_buf[k, :, at] = moment_next
            outer_buf[k, :, at] = outer_next
            merged_buf[k, :, at] = (
                MIX * local_ref[k, :, at].astype(jnp.float32) + (1.0 - MIX) * outer_next
            ).astype(jnp.bfloat16)
        copies += [
            pltpu.make_async_copy(moment_buf.at[k], new_moment.at[number, :, cols], sems.at[0, k]),
            pltpu.make_async_copy(outer_buf.at[k], new_outer.at[number, :, cols], sems.at[1, k]),
            pltpu.make_async_copy(merged_buf.at[k], merged.at[0, number, :, cols], sems.at[2, k]),
        ]
        for copy in copies[-3:]:
            copy.start()
    for copy in copies:
        copy.wait()


def update(quarters, squares_sum, outer_sel, local_sel, moment_sel, workers, entries):
    _, rows, width = outer_sel.shape
    cols = QUARTERS * width // SYNCED
    return pl.pallas_call(
        lambda *refs: update_kernel(workers, entries, *refs),
        out_shape=(
            jax.ShapeDtypeStruct((SYNCED, rows, cols), jnp.float32),
            jax.ShapeDtypeStruct((SYNCED, rows, cols), jnp.float32),
            jax.ShapeDtypeStruct((1, SYNCED, rows, cols), local_sel.dtype),
        ),
        in_specs=[VMEM] * (QUARTERS + 4),
        out_specs=(HBM,) * 3,
        scratch_shapes=[
            pltpu.VMEM(outer_sel.shape, jnp.float32),
            pltpu.VMEM(outer_sel.shape, jnp.float32),
            pltpu.VMEM(local_sel.shape, local_sel.dtype),
            pltpu.VMEM((8, BLOCK), jnp.float32),
            pltpu.SemaphoreType.DMA((3, QUARTERS)),
        ],
        compiler_params=PARAMS,
        name="update",
    )(*quarters, squares_sum, outer_sel, local_sel, moment_sel)


def shards(local, outer, moment, plan):
    _, frags, rows, cols = local.shape
    workers = lax.axis_size("replica")
    shares = lax.axis_size("mp")
    entries = rows * cols * shares
    inner = workers // QUARTERS
    groups = [list(range(g * inner, (g + 1) * inner)) for g in range(QUARTERS)]

    def along_y(array, k):
        return lax.ppermute(array, "replica", [(r, r ^ (k * inner)) for r in range(workers)])

    def inside(array):
        return lax.all_to_all(array, "replica", 0, 0, axis_index_groups=groups, tiled=True)

    *coded, outer_sel, local_sel, moment_sel = encode(plan, local, outer, moment, workers)
    mine = add([coded[0]] + [along_y(coded[k], k) for k in range(1, QUARTERS)])
    quarter = inside(mean(inside(mine), workers))
    quarters = [quarter] + [along_y(quarter, k) for k in range(1, QUARTERS)]
    squares_sum = squares(quarters, workers)
    for bit in (1, 2):
        squares_sum += lax.ppermute(squares_sum, "mp", [(m, m ^ bit) for m in range(shares)])
    return update(quarters, squares_sum, outer_sel, local_sel, moment_sel, workers, entries)


def solution(mesh):
    return jax.shard_map(
        shards,
        mesh=mesh,
        in_specs=(P("replica", None, None, "mp"), P(None, None, "mp"), P(None, None, "mp"), P()),
        out_specs=(P(None, None, "mp"), P(None, None, "mp"), P("replica", None, None, "mp")),
        check_vma=False,
    )
```

time: 728 us -> 68.8 us (0.09)
  waiting for transfers between devices: 650 us -> 14.9 us
  blocking collectives: 52 us -> 31.5 us
  between operations: 15.6 us -> 0.68 us
  starting transfers between devices: 0.04 us -> 13.8 us
    psum x1 -> x0, waiting for transfers between devices: 650 us -> none  [refresh(): pseudo = lax.psum(coded, 'replica') / workers]
    psum x1 -> x0, blocking collectives: 52 us -> none  [refresh(): squares = lax.psum(jnp.sum(pseudo * pseudo, axis=(1, 2)), 'mp')]
    all_to_all x0 -> x2, blocking collectives: none -> 31.5 us  [inside(): lax.all_to_all(array, 'replica', 0, 0, axis_index_groups=groups, tiled=True)]
    ppermute x0 -> x8, waiting for transfers between devices: none -> 14.9 us  [the longest x6 12 us: along_y(): lax.ppermute(array, 'replica', [(r, r ^ k * inner) for r in range(workers)])]
    ppermute x0 -> x8, starting transfers between devices: none -> 13.8 us  [the longest x6 8.09 us: along_y(): lax.ppermute(array, 'replica', [(r, r ^ k * inner) for r in range(workers)])]
  transfers between devices with their start and end apart: 1 -> 8, of which waited for: 1 -> 6; matrix products, arithmetic and copies ran while one was open for 0% -> 0% of each run, Pallas kernels for 0% -> 0%
where the time goes in v2:
time: 68.8 us; the launch traced here: 68.5 us
  blocking collectives  31.5 us (46%)
  waiting for transfers between devices  14.9 us (22%)
  starting transfers between devices  13.8 us (20%)
  local copies, waits for them, and re-layouts  4.14 us (6%)
  Pallas kernels  3.49 us (5%)
    all_to_all x2, blocking collectives, inside(): lax.all_to_all(array, 'replica', 0, 0, axis_index_groups=groups, tiled=True)  31.5 us
    ppermute x6, waiting for transfers between devices, along_y(): lax.ppermute(array, 'replica', [(r, r ^ k * inner) for r in range(workers)])  12 us
    ppermute x6, starting transfers between devices, along_y(): lax.ppermute(array, 'replica', [(r, r ^ k * inner) for r in range(workers)])  8.09 us
    ppermute x2, starting transfers between devices, shards(): lax.ppermute(squares_sum, 'mp', [(m, m ^ bit) for m in range(shares)])  5.66 us
    unnamed x8, local copies, waits for them, and re-layouts  4.14 us
    ppermute x2, waiting for transfers between devices, shards(): lax.ppermute(squares_sum, 'mp', [(m, m ^ bit) for m in range(shares)])  2.97 us
    pallas_call x1, Pallas kernels, encode(): pl.pallas_call(lambda *refs: encode_kernel(workers, *refs), out_shape=(pi...  2.06 us
  transfers between devices with their start and end apart: 8, of which 6 were waited for; matrix products, arithmetic and copies ran while one was open for 0% of the time, Pallas kernels for 0%

profile of v2, /device:TPU:1, one launch (start us, length us, event | category | flops | bytes accessed | tf_op | source)
XLA Modules:
  0.0 68.5 jit_solution(5385392701802947735)
XLA Ops:
  0.6 1.2 %copy-done = f32[4,16,4096]{2,1,0:T(8,128)S(1)} copy-done((f32[4,16,4096]{2,1,0:T(8,128)S(1)}, f32[4,16,4096]{2,1,0:T(8,128)}, u32[]{:S(2)}) %copy-start) | copy-done | bytes 1048600
  1.9 1.2 %copy-done.1 = f32[4,16,4096]{2,1,0:T(8,128)S(1)} copy-done((f32[4,16,4096]{2,1,0:T(8,128)S(1)}, f32[4,16,4096]{2,1,0:T(8,128)}, u32[]{:S(2)}) %copy-start.1) | copy-done | bytes 1048600
  3.1 1.0 %copy-done.2 = bf16[1,4,16,4096]{3,2,1,0:T(8,128)(2,1)S(1)} copy-done((bf16[1,4,16,4096]{3,2,1,0:T(8,128)(2,1)S(1)}, bf16[1,4,16,4096]{3,2,1,0:T(8,128)(2,1)}, u32[]{:S(2)}) %copy-start.2) | copy-done | bytes 524312
  4.1 0.7 copy-done.3
  4.8 2.1 %encode.1 = (f32[16,16,128]{2,1,0:T(8,128)S(1)}, f32[16,16,128]{2,1,0:T(8,128)S(1)}, f32[16,16,128]{2,1,0:T(8,128)S(1)}, f32[16,16,128]{2,1,0:T(8,128)S(1)}, f32...) custom-call(s32[4]{0:T(128)S(1)} %copy-done.3, ...), custom_call_target="tpu_custom_call" | custom-call | tf_op jit(solution)/shard_map/encode/pallas_call | solution.py:71
  6.8 2.2 %collective-permute-start = (f32[16,16,128]{2,1,0:T(8,128)S(1)}, f32[16,16,128]{2,1,0:T(8,128)S(1)}, u32[]{:S(2)}, u32[]{:S(2)}) collective-permute-start(f32[16,16,128]{2,1,0:T(8,128)S(1)} %get-tuple-element.11), channel_id=1, source_target_pairs={{0,64},{4,68},{8,72},{12,76},{16,80},{20,84},{24,88},{28,92},{32,9... | collective-permute-start | bytes 393224 | tf_op jit(solution)/shard_map/ppermute | solution.py:205
  9.1 2.6 %collective-permute-start.1 = (f32[16,16,128]{2,1,0:T(8,128)S(1)}, f32[16,16,128]{2,1,0:T(8,128)S(1)}, u32[]{:S(2)}, u32[]{:S(2)}) collective-permute-start(f32[16,16,128]{2,1,0:T(8,128)S(1)} %get-tuple-element.12), channel_id=1, source_target_pairs={{0,128},{4,132},{8,136},{12,140},{16,144},{20,148},{24,152},{28,15... | collective-permute-start | bytes 393224 | tf_op jit(solution)/shard_map/ppermute | solution.py:205
  11.7 0.0 collective-permute-start.2
  11.7 0.0 collective-permute-done.refs_1_
  11.7 5.7 %collective-permute-done.1.refs_2_ = f32[16,16,128]{2,1,0:T(8,128)S(1)} collective-permute-done((f32[16,16,128]{2,1,0:T(8,128)S(1)}, f32[16,16,128]{2,1,0:T(8,128)S(1)}, u32[]{:S(2)}, u32[]{:S(2)}) %collective-permute-start.1) | collective-permute-done | bytes 131104 | tf_op jit(solution)/shard_map/ppermute | solution.py:205
  17.4 2.5 %collective-permute-done.2.refs_3_ = f32[16,16,128]{2,1,0:T(8,128)S(1)} collective-permute-done((f32[16,16,128]{2,1,0:T(8,128)S(1)}, f32[16,16,128]{2,1,0:T(8,128)S(1)}, u32[]{:S(2)}, u32[]{:S(2)}) %collective-permute-start.2) | collective-permute-done | bytes 131104 | tf_op jit(solution)/shard_map/ppermute | solution.py:205
  19.9 19.5 %all_to_all.10.refs_0_ = f32[16,16,128]{2,1,0:T(8,128)S(1)} all-to-all(f32[16,16,128]{2,1,0:T(8,128)S(1)} %add.9), channel_id=1, replica_groups={{0,4,8,12,16,20,24,28,32,36,40,44,48,52,56,60},{64,68,72,76,80,84,88,92..., dimensions={0} | all-to-all | bytes 262144 | tf_op jit(solution)/shard_map/all_to_all | solution.py:208
  39.4 12.0 %all_to_all.11.refs_0_ = f32[16,16,128]{2,1,0:T(8,128)S(1)} all-to-all(f32[16,16,128]{2,1,0:T(8,128)S(1)} %mean.1), channel_id=1, replica_groups={{0,4,8,12,16,20,24,28,32,36,40,44,48,52,56,60},{64,68,72,76,80,84,88,92..., dimensions={0} | all-to-all | bytes 262144 | tf_op jit(solution)/shard_map/all_to_all | solution.py:208
  51.5 0.7 collective-permute-start.5
  52.1 0.1 collective-permute-start.4
  52.2 2.5 %collective-permute-start.3 = (f32[16,16,128]{2,1,0:T(8,128)S(1)}, f32[16,16,128]{2,1,0:T(8,128)S(1)}, u32[]{:S(2)}, u32[]{:S(2)}) collective-permute-start(f32[16,16,128]{2,1,0:T(8,128)S(1)} %all_to_all.11.refs_0_), channel_id=1, source_target_pairs={{0,64},{4,68},{8,72},{12,76},{16,80},{20,84},{24,88},{28,92},{32,9... | collective-permute-start | bytes 393224 | tf_op jit(solution)/shard_map/ppermute | solution.py:205
  54.7 3.2 %collective-permute-done.5.refs_3_ = f32[16,16,128]{2,1,0:T(8,128)S(1)} collective-permute-done((f32[16,16,128]{2,1,0:T(8,128)S(1)}, f32[16,16,128]{2,1,0:T(8,128)S(1)}, u32[]{:S(2)}, u32[]{:S(2)}) %collective-permute-start.5) | collective-permute-done | bytes 131104 | tf_op jit(solution)/shard_map/ppermute | solution.py:205
  57.9 0.6 collective-permute-done.3.refs_1_
  58.5 0.2 squares.1
  58.7 5.4 %collective-permute-start.6 = (f32[8,128]{1,0:T(8,128)S(1)}, f32[8,128]{1,0:T(8,128)S(1)}, u32[]{:S(2)}, u32[]{:S(2)}) collective-permute-start(f32[8,128]{1,0:T(8,128)S(1)} %squares.1), channel_id=1, source_target_pairs={{0,1},{1,0},{2,3},{3,2},{4,5},{5,4},{6,7},{7,6},{8,9},{9,8},{10,11... | collective-permute-start | bytes 12296 | tf_op jit(solution)/shard_map/ppermute | solution.py:216
  64.0 0.8 %collective-permute-done.6 = f32[8,128]{1,0:T(8,128)S(1)} collective-permute-done((f32[8,128]{1,0:T(8,128)S(1)}, f32[8,128]{1,0:T(8,128)S(1)}, u32[]{:S(2)}, u32[]{:S(2)}) %collective-permute-start.6) | collective-permute-done | bytes 4128 | tf_op jit(solution)/shard_map/ppermute | solution.py:216
  64.8 0.3 collective-permute-start.7
  65.2 2.1 %collective-permute-done.7 = f32[8,128]{1,0:T(8,128)S(1)} collective-permute-done((f32[8,128]{1,0:T(8,128)S(1)}, f32[8,128]{1,0:T(8,128)S(1)}, u32[]{:S(2)}, u32[]{:S(2)}) %collective-permute-start.7) | collective-permute-done | bytes 4128 | tf_op jit(solution)/shard_map/ppermute | solution.py:216
  67.3 1.2 %update.1 = (f32[2,16,4096]{2,1,0:T(8,128)}, f32[2,16,4096]{2,1,0:T(8,128)}, bf16[1,2,16,4096]{3,2,1,0:T(8,128)(2,1)}) custom-call(f32[16,16,128]{2,1,0:T(8,128)S(1)} %all_to_all.11.refs_0_, f32[16,16,128]{2,1,0:T(8,128)S(1)} %collective-permute-done.3.refs_1_, f32[16,16,128]{2,1,0:T(8,128)S(1)} %collective-permute-done.4.refs_2_, ...), custom_call_target="tpu_custom_call" | custom-call | tf_op jit(solution)/shard_map/update/pallas_call | solution.py:175
  (9 shorter events, 0.1 us)
Async XLA Ops:
  0.6 1.2 %copy-start = (f32[4,16,4096]{2,1,0:T(8,128)S(1)}, f32[4,16,4096]{2,1,0:T(8,128)}, u32[]{:S(2)}) copy-start(f32[4,16,4096]{2,1,0:T(8,128)} %refs_2_.1) | copy-start | bytes 3145732
  1.9 1.2 %copy-start.1 = (f32[4,16,4096]{2,1,0:T(8,128)S(1)}, f32[4,16,4096]{2,1,0:T(8,128)}, u32[]{:S(2)}) copy-start(f32[4,16,4096]{2,1,0:T(8,128)} %refs_3_.1) | copy-start | bytes 3145732
  3.1 1.0 %copy-start.2 = (bf16[1,4,16,4096]{3,2,1,0:T(8,128)(2,1)S(1)}, bf16[1,4,16,4096]{3,2,1,0:T(8,128)(2,1)}, u32[]{:S(2)}) copy-start(bf16[1,4,16,4096]{3,2,1,0:T(8,128)(2,1)} %refs_1_.1) | copy-start | bytes 1572868
  4.1 0.7 copy-start.3
  6.8 4.8 %collective-permute-start = (f32[16,16,128]{2,1,0:T(8,128)S(1)}, f32[16,16,128]{2,1,0:T(8,128)S(1)}, u32[]{:S(2)}, u32[]{:S(2)}) collective-permute-start(f32[16,16,128]{2,1,0:T(8,128)S(1)} %get-tuple-element.11), channel_id=1, source_target_pairs={{0,64},{4,68},{8,72},{12,76},{16,80},{20,84},{24,88},{28,92},{32,9... | collective-permute-start | bytes 393224 | tf_op jit(solution)/shard_map/ppermute | solution.py:205
  9.1 8.3 %collective-permute-start.1 = (f32[16,16,128]{2,1,0:T(8,128)S(1)}, f32[16,16,128]{2,1,0:T(8,128)S(1)}, u32[]{:S(2)}, u32[]{:S(2)}) collective-permute-start(f32[16,16,128]{2,1,0:T(8,128)S(1)} %get-tuple-element.12), channel_id=1, source_target_pairs={{0,128},{4,132},{8,136},{12,140},{16,144},{20,148},{24,152},{28,15... | collective-permute-start | bytes 393224 | tf_op jit(solution)/shard_map/ppermute | solution.py:205
  11.7 8.2 %collective-permute-start.2 = (f32[16,16,128]{2,1,0:T(8,128)S(1)}, f32[16,16,128]{2,1,0:T(8,128)S(1)}, u32[]{:S(2)}, u32[]{:S(2)}) collective-permute-start(f32[16,16,128]{2,1,0:T(8,128)S(1)} %get-tuple-element.13), channel_id=1, source_target_pairs={{0,192},{4,196},{8,200},{12,204},{16,208},{20,212},{24,216},{28,22... | collective-permute-start | bytes 393224 | tf_op jit(solution)/shard_map/ppermute | solution.py:205
  51.5 6.4 %collective-permute-start.5 = (f32[16,16,128]{2,1,0:T(8,128)S(1)}, f32[16,16,128]{2,1,0:T(8,128)S(1)}, u32[]{:S(2)}, u32[]{:S(2)}) collective-permute-start(f32[16,16,128]{2,1,0:T(8,128)S(1)} %all_to_all.11.refs_0_), channel_id=1, source_target_pairs={{0,192},{4,196},{8,200},{12,204},{16,208},{20,212},{24,216},{28,22... | collective-permute-start | bytes 393224 | tf_op jit(solution)/shard_map/ppermute | solution.py:205
  52.1 5.8 %collective-permute-start.4 = (f32[16,16,128]{2,1,0:T(8,128)S(1)}, f32[16,16,128]{2,1,0:T(8,128)S(1)}, u32[]{:S(2)}, u32[]{:S(2)}) collective-permute-start(f32[16,16,128]{2,1,0:T(8,128)S(1)} %all_to_all.11.refs_0_), channel_id=1, source_target_pairs={{0,128},{4,132},{8,136},{12,140},{16,144},{20,148},{24,152},{28,15... | collective-permute-start | bytes 393224 | tf_op jit(solution)/shard_map/ppermute | solution.py:205
  52.2 6.3 %collective-permute-start.3 = (f32[16,16,128]{2,1,0:T(8,128)S(1)}, f32[16,16,128]{2,1,0:T(8,128)S(1)}, u32[]{:S(2)}, u32[]{:S(2)}) collective-permute-start(f32[16,16,128]{2,1,0:T(8,128)S(1)} %all_to_all.11.refs_0_), channel_id=1, source_target_pairs={{0,64},{4,68},{8,72},{12,76},{16,80},{20,84},{24,88},{28,92},{32,9... | collective-permute-start | bytes 393224 | tf_op jit(solution)/shard_map/ppermute | solution.py:205
  58.7 6.2 %collective-permute-start.6 = (f32[8,128]{1,0:T(8,128)S(1)}, f32[8,128]{1,0:T(8,128)S(1)}, u32[]{:S(2)}, u32[]{:S(2)}) collective-permute-start(f32[8,128]{1,0:T(8,128)S(1)} %squares.1), channel_id=1, source_target_pairs={{0,1},{1,0},{2,3},{3,2},{4,5},{5,4},{6,7},{7,6},{8,9},{9,8},{10,11... | collective-permute-start | bytes 12296 | tf_op jit(solution)/shard_map/ppermute | solution.py:216
  64.8 2.5 %collective-permute-start.7 = (f32[8,128]{1,0:T(8,128)S(1)}, f32[8,128]{1,0:T(8,128)S(1)}, u32[]{:S(2)}, u32[]{:S(2)}) collective-permute-start(f32[8,128]{1,0:T(8,128)S(1)} %add.7), channel_id=1, source_target_pairs={{0,2},{1,3},{2,0},{3,1},{4,6},{5,7},{6,4},{7,5},{8,10},{9,11},{10,... | collective-permute-start | bytes 12296 | tf_op jit(solution)/shard_map/ppermute | solution.py:216

commit v3 on v2

--- a/solution.py
+++ b/solution.py
@@ -80,7 +80,7 @@
         ],
         compiler_params=PARAMS,
         name="encode",
-    )(plan, local, outer, moment)
+    )(*[pltpu.with_memory_space_constraint(a, pltpu.HBM) for a in (plan, local, outer, moment)])
 
 
 def add_kernel(*refs):

time: 68.8 us -> 64.7 us (0.940)
  local copies, waits for them, and re-layouts: 4.14 us -> 0 us
    unnamed x8 -> x0, local copies, waits for them, and re-layouts: 4.14 us -> none
where the time goes in v3:
time: 64.7 us; the launch traced here: 64.5 us
  blocking collectives  31.5 us (49%)
  waiting for transfers between devices  14.9 us (23%)
  starting transfers between devices  13.8 us (21%)
  Pallas kernels  3.66 us (6%)
  between operations  0.66 us (1%)
    all_to_all x2, blocking collectives, inside(): lax.all_to_all(array, 'replica', 0, 0, axis_index_groups=groups, tiled=True)  31.5 us
    ppermute x6, waiting for transfers between devices, along_y(): lax.ppermute(array, 'replica', [(r, r ^ k * inner) for r in range(workers)])  12 us
    ppermute x6, starting transfers between devices, along_y(): lax.ppermute(array, 'replica', [(r, r ^ k * inner) for r in range(workers)])  8.09 us
    ppermute x2, starting transfers between devices, shards(): lax.ppermute(squares_sum, 'mp', [(m, m ^ bit) for m in range(shares)])  5.66 us
    ppermute x2, waiting for transfers between devices, shards(): lax.ppermute(squares_sum, 'mp', [(m, m ^ bit) for m in range(shares)])  2.97 us
    pallas_call x1, Pallas kernels, encode(): pl.pallas_call(lambda *refs: encode_kernel(workers, *refs), out_shape=(pi...  2.22 us
  transfers between devices with their start and end apart: 8, of which 6 were waited for; matrix products, arithmetic and copies ran while one was open for 0% of the time, Pallas kernels for 0%

profile of v3, /device:TPU:1, one launch (start us, length us, event | category | flops | bytes accessed | tf_op | source)
XLA Modules:
  0.0 64.5 jit_solution(10044638450419347864)
XLA Ops:
  0.6 2.2 %encode.1 = (f32[16,16,128]{2,1,0:T(8,128)S(1)}, f32[16,16,128]{2,1,0:T(8,128)S(1)}, f32[16,16,128]{2,1,0:T(8,128)S(1)}, f32[16,16,128]{2,1,0:T(8,128)S(1)}, f32...) custom-call(s32[4]{0:T(128)} %refs_0_.1, bf16[1,4,16,4096]{3,2,1,0:T(8,128)(2,1)} %refs_1_.1, ...), custom_call_target="tpu_custom_call" | custom-call | tf_op jit(solution)/shard_map/encode/pallas_call | solution.py:71
  2.9 2.2 %collective-permute-start = (f32[16,16,128]{2,1,0:T(8,128)S(1)}, f32[16,16,128]{2,1,0:T(8,128)S(1)}, u32[]{:S(2)}, u32[]{:S(2)}) collective-permute-start(f32[16,16,128]{2,1,0:T(8,128)S(1)} %get-tuple-element.11), channel_id=1, source_target_pairs={{0,64},{4,68},{8,72},{12,76},{16,80},{20,84},{24,88},{28,92},{32,9... | collective-permute-start | bytes 393224 | tf_op jit(solution)/shard_map/ppermute | solution.py:205
  5.1 2.6 %collective-permute-start.1 = (f32[16,16,128]{2,1,0:T(8,128)S(1)}, f32[16,16,128]{2,1,0:T(8,128)S(1)}, u32[]{:S(2)}, u32[]{:S(2)}) collective-permute-start(f32[16,16,128]{2,1,0:T(8,128)S(1)} %get-tuple-element.12), channel_id=1, source_target_pairs={{0,128},{4,132},{8,136},{12,140},{16,144},{20,148},{24,152},{28,15... | collective-permute-start | bytes 393224 | tf_op jit(solution)/shard_map/ppermute | solution.py:205
  7.7 0.0 collective-permute-start.2
  7.7 0.0 collective-permute-done.refs_1_
  7.7 5.7 %collective-permute-done.1.refs_2_ = f32[16,16,128]{2,1,0:T(8,128)S(1)} collective-permute-done((f32[16,16,128]{2,1,0:T(8,128)S(1)}, f32[16,16,128]{2,1,0:T(8,128)S(1)}, u32[]{:S(2)}, u32[]{:S(2)}) %collective-permute-start.1) | collective-permute-done | bytes 131104 | tf_op jit(solution)/shard_map/ppermute | solution.py:205
  13.4 2.5 %collective-permute-done.2.refs_3_ = f32[16,16,128]{2,1,0:T(8,128)S(1)} collective-permute-done((f32[16,16,128]{2,1,0:T(8,128)S(1)}, f32[16,16,128]{2,1,0:T(8,128)S(1)}, u32[]{:S(2)}, u32[]{:S(2)}) %collective-permute-start.2) | collective-permute-done | bytes 131104 | tf_op jit(solution)/shard_map/ppermute | solution.py:205
  15.9 19.5 %all_to_all.10.refs_0_ = f32[16,16,128]{2,1,0:T(8,128)S(1)} all-to-all(f32[16,16,128]{2,1,0:T(8,128)S(1)} %add.9), channel_id=1, replica_groups={{0,4,8,12,16,20,24,28,32,36,40,44,48,52,56,60},{64,68,72,76,80,84,88,92..., dimensions={0} | all-to-all | bytes 262144 | tf_op jit(solution)/shard_map/all_to_all | solution.py:208
  35.5 12.0 %all_to_all.11.refs_0_ = f32[16,16,128]{2,1,0:T(8,128)S(1)} all-to-all(f32[16,16,128]{2,1,0:T(8,128)S(1)} %mean.1), channel_id=1, replica_groups={{0,4,8,12,16,20,24,28,32,36,40,44,48,52,56,60},{64,68,72,76,80,84,88,92..., dimensions={0} | all-to-all | bytes 262144 | tf_op jit(solution)/shard_map/all_to_all | solution.py:208
  47.5 0.7 %collective-permute-start.5 = (f32[16,16,128]{2,1,0:T(8,128)S(1)}, f32[16,16,128]{2,1,0:T(8,128)S(1)}, u32[]{:S(2)}, u32[]{:S(2)}) collective-permute-start(f32[16,16,128]{2,1,0:T(8,128)S(1)} %all_to_all.11.refs_0_), channel_id=1, source_target_pairs={{0,192},{4,196},{8,200},{12,204},{16,208},{20,212},{24,216},{28,22... | collective-permute-start | bytes 393224 | tf_op jit(solution)/shard_map/ppermute | solution.py:205
  48.1 0.1 collective-permute-start.4
  48.2 2.5 %collective-permute-start.3 = (f32[16,16,128]{2,1,0:T(8,128)S(1)}, f32[16,16,128]{2,1,0:T(8,128)S(1)}, u32[]{:S(2)}, u32[]{:S(2)}) collective-permute-start(f32[16,16,128]{2,1,0:T(8,128)S(1)} %all_to_all.11.refs_0_), channel_id=1, source_target_pairs={{0,64},{4,68},{8,72},{12,76},{16,80},{20,84},{24,88},{28,92},{32,9... | collective-permute-start | bytes 393224 | tf_op jit(solution)/shard_map/ppermute | solution.py:205
  50.7 3.2 %collective-permute-done.5.refs_3_ = f32[16,16,128]{2,1,0:T(8,128)S(1)} collective-permute-done((f32[16,16,128]{2,1,0:T(8,128)S(1)}, f32[16,16,128]{2,1,0:T(8,128)S(1)}, u32[]{:S(2)}, u32[]{:S(2)}) %collective-permute-start.5) | collective-permute-done | bytes 131104 | tf_op jit(solution)/shard_map/ppermute | solution.py:205
  53.9 0.0 collective-permute-done.4.refs_2_
  53.9 0.6 collective-permute-done.3.refs_1_
  54.5 0.2 squares.1
  54.7 5.4 %collective-permute-start.6 = (f32[8,128]{1,0:T(8,128)S(1)}, f32[8,128]{1,0:T(8,128)S(1)}, u32[]{:S(2)}, u32[]{:S(2)}) collective-permute-start(f32[8,128]{1,0:T(8,128)S(1)} %squares.1), channel_id=1, source_target_pairs={{0,1},{1,0},{2,3},{3,2},{4,5},{5,4},{6,7},{7,6},{8,9},{9,8},{10,11... | collective-permute-start | bytes 12296 | tf_op jit(solution)/shard_map/ppermute | solution.py:216
  60.0 0.8 %collective-permute-done.6 = f32[8,128]{1,0:T(8,128)S(1)} collective-permute-done((f32[8,128]{1,0:T(8,128)S(1)}, f32[8,128]{1,0:T(8,128)S(1)}, u32[]{:S(2)}, u32[]{:S(2)}) %collective-permute-start.6) | collective-permute-done | bytes 4128 | tf_op jit(solution)/shard_map/ppermute | solution.py:216
  60.9 0.3 collective-permute-start.7
  61.2 2.1 %collective-permute-done.7 = f32[8,128]{1,0:T(8,128)S(1)} collective-permute-done((f32[8,128]{1,0:T(8,128)S(1)}, f32[8,128]{1,0:T(8,128)S(1)}, u32[]{:S(2)}, u32[]{:S(2)}) %collective-permute-start.7) | collective-permute-done | bytes 4128 | tf_op jit(solution)/shard_map/ppermute | solution.py:216
  63.3 1.2 %update.1 = (f32[2,16,4096]{2,1,0:T(8,128)}, f32[2,16,4096]{2,1,0:T(8,128)}, bf16[1,2,16,4096]{3,2,1,0:T(8,128)(2,1)}) custom-call(f32[16,16,128]{2,1,0:T(8,128)S(1)} %all_to_all.11.refs_0_, f32[16,16,128]{2,1,0:T(8,128)S(1)} %collective-permute-done.3.refs_1_, f32[16,16,128]{2,1,0:T(8,128)S(1)} %collective-permute-done.4.refs_2_, ...), custom_call_target="tpu_custom_call" | custom-call | tf_op jit(solution)/shard_map/update/pallas_call | solution.py:175
  (4 shorter events, 0.1 us)
Async XLA Ops:
  2.9 4.8 %collective-permute-start = (f32[16,16,128]{2,1,0:T(8,128)S(1)}, f32[16,16,128]{2,1,0:T(8,128)S(1)}, u32[]{:S(2)}, u32[]{:S(2)}) collective-permute-start(f32[16,16,128]{2,1,0:T(8,128)S(1)} %get-tuple-element.11), channel_id=1, source_target_pairs={{0,64},{4,68},{8,72},{12,76},{16,80},{20,84},{24,88},{28,92},{32,9... | collective-permute-start | bytes 393224 | tf_op jit(solution)/shard_map/ppermute | solution.py:205
  5.1 8.3 %collective-permute-start.1 = (f32[16,16,128]{2,1,0:T(8,128)S(1)}, f32[16,16,128]{2,1,0:T(8,128)S(1)}, u32[]{:S(2)}, u32[]{:S(2)}) collective-permute-start(f32[16,16,128]{2,1,0:T(8,128)S(1)} %get-tuple-element.12), channel_id=1, source_target_pairs={{0,128},{4,132},{8,136},{12,140},{16,144},{20,148},{24,152},{28,15... | collective-permute-start | bytes 393224 | tf_op jit(solution)/shard_map/ppermute | solution.py:205
  7.7 8.2 %collective-permute-start.2 = (f32[16,16,128]{2,1,0:T(8,128)S(1)}, f32[16,16,128]{2,1,0:T(8,128)S(1)}, u32[]{:S(2)}, u32[]{:S(2)}) collective-permute-start(f32[16,16,128]{2,1,0:T(8,128)S(1)} %get-tuple-element.13), channel_id=1, source_target_pairs={{0,192},{4,196},{8,200},{12,204},{16,208},{20,212},{24,216},{28,22... | collective-permute-start | bytes 393224 | tf_op jit(solution)/shard_map/ppermute | solution.py:205
  47.5 6.4 %collective-permute-start.5 = (f32[16,16,128]{2,1,0:T(8,128)S(1)}, f32[16,16,128]{2,1,0:T(8,128)S(1)}, u32[]{:S(2)}, u32[]{:S(2)}) collective-permute-start(f32[16,16,128]{2,1,0:T(8,128)S(1)} %all_to_all.11.refs_0_), channel_id=1, source_target_pairs={{0,192},{4,196},{8,200},{12,204},{16,208},{20,212},{24,216},{28,22... | collective-permute-start | bytes 393224 | tf_op jit(solution)/shard_map/ppermute | solution.py:205
  48.1 5.8 %collective-permute-start.4 = (f32[16,16,128]{2,1,0:T(8,128)S(1)}, f32[16,16,128]{2,1,0:T(8,128)S(1)}, u32[]{:S(2)}, u32[]{:S(2)}) collective-permute-start(f32[16,16,128]{2,1,0:T(8,128)S(1)} %all_to_all.11.refs_0_), channel_id=1, source_target_pairs={{0,128},{4,132},{8,136},{12,140},{16,144},{20,148},{24,152},{28,15... | collective-permute-start | bytes 393224 | tf_op jit(solution)/shard_map/ppermute | solution.py:205
  48.2 6.3 %collective-permute-start.3 = (f32[16,16,128]{2,1,0:T(8,128)S(1)}, f32[16,16,128]{2,1,0:T(8,128)S(1)}, u32[]{:S(2)}, u32[]{:S(2)}) collective-permute-start(f32[16,16,128]{2,1,0:T(8,128)S(1)} %all_to_all.11.refs_0_), channel_id=1, source_target_pairs={{0,64},{4,68},{8,72},{12,76},{16,80},{20,84},{24,88},{28,92},{32,9... | collective-permute-start | bytes 393224 | tf_op jit(solution)/shard_map/ppermute | solution.py:205
  54.7 6.2 %collective-permute-start.6 = (f32[8,128]{1,0:T(8,128)S(1)}, f32[8,128]{1,0:T(8,128)S(1)}, u32[]{:S(2)}, u32[]{:S(2)}) collective-permute-start(f32[8,128]{1,0:T(8,128)S(1)} %squares.1), channel_id=1, source_target_pairs={{0,1},{1,0},{2,3},{3,2},{4,5},{5,4},{6,7},{7,6},{8,9},{9,8},{10,11... | collective-permute-start | bytes 12296 | tf_op jit(solution)/shard_map/ppermute | solution.py:216
  60.9 2.5 %collective-permute-start.7 = (f32[8,128]{1,0:T(8,128)S(1)}, f32[8,128]{1,0:T(8,128)S(1)}, u32[]{:S(2)}, u32[]{:S(2)}) collective-permute-start(f32[8,128]{1,0:T(8,128)S(1)} %add.7), channel_id=1, source_target_pairs={{0,2},{1,3},{2,0},{3,1},{4,6},{5,7},{6,4},{7,5},{8,10},{9,11},{10,... | collective-permute-start | bytes 12296 | tf_op jit(solution)/shard_map/ppermute | solution.py:216

commit v4 on v3

--- a/solution.py
+++ b/solution.py
@@ -20,6 +20,13 @@
 PARAMS = pltpu.CompilerParams(vmem_limit_bytes=SCOPED)
 
 
+SENT = (2, 3, 1)
+
+
+def in_hbm(*arrays):
+    return [pltpu.with_memory_space_constraint(array, pltpu.HBM) for array in arrays]
+
+
 def my_y(workers):
     return lax.axis_index("replica") // (workers // QUARTERS)
 
@@ -30,57 +37,104 @@
     return quarter // per_fragment, pl.ds(pl.multiple_of((quarter % per_fragment) * width, width), width)
 
 
-def encode_kernel(workers, plan_hbm, local_hbm, outer_hbm, moment_hbm, *refs):
-    out_refs, (outer_ref, local_ref, moment_ref, plan_ref, plan_sem, sems) = refs[:QUARTERS], refs[QUARTERS:]
+def coded(outer, local):
+    diff = outer - local.astype(jnp.float32)
+    scale = jnp.max(jnp.abs(diff), axis=-1, keepdims=True) + EPS
+    return (diff / scale).astype(jnp.bfloat16).astype(jnp.float32) * scale
+
+
+def encode_kernel(workers, plan_hbm, local_hbm, outer_hbm, *refs):
+    out_refs, (outer_ref, local_ref, plan_ref, plan_sem, sems) = refs[: len(SENT)], refs[len(SENT) :]
+    width = out_refs[0].shape[0] * BLOCK
+    frags = outer_ref.shape[0]
+    plan_copy = pltpu.make_async_copy(plan_hbm, plan_ref, plan_sem)
+    plan_copy.start()
+    copies = []
+    for f in range(frags):
+        copies.append(pltpu.make_async_copy(outer_hbm.at[f], outer_ref.at[f], sems.at[0, f]))
+        copies.append(pltpu.make_async_copy(local_hbm.at[0, f], local_ref.at[f], sems.at[1, f]))
+    for copy in copies:
+        copy.start()
+    y = my_y(workers)
+    plan_copy.wait()
+    for copy in copies:
+        copy.wait()
+    for k, out_ref in zip(SENT, out_refs):
+        number, cols = place(y, k, width)
+        f = plan_ref[number]
+        for b in range(width // BLOCK):
+            at = pl.ds(pl.multiple_of(cols.start + b * BLOCK, BLOCK), BLOCK)
+            out_ref[b] = coded(outer_ref[f, :, at], local_ref[f, :, at])
+
+
+def encode(plan, local, outer, workers):
+    _, frags, rows, cols = local.shape
+    width = SYNCED * cols // QUARTERS
+    piece = jax.ShapeDtypeStruct((width // BLOCK, rows, BLOCK), jnp.float32)
+    return pl.pallas_call(
+        lambda *refs: encode_kernel(workers, *refs),
+        out_shape=(piece,) * len(SENT),
+        in_specs=[HBM] * 3,
+        out_specs=(VMEM,) * len(SENT),
+        scratch_shapes=[
+            pltpu.VMEM(outer.shape, outer.dtype),
+            pltpu.VMEM(local.shape[1:], local.dtype),
+            pltpu.SMEM(plan.shape, jnp.int32),
+            pltpu.SemaphoreType.DMA(()),
+            pltpu.SemaphoreType.DMA((2, frags)),
+        ],
+        compiler_params=PARAMS,
+        name="encode",
+    )(*in_hbm(plan, local, outer))
+
+
+def select_kernel(workers, plan_hbm, local_hbm, outer_hbm, moment_hbm, own_ref, outer_ref, local_ref, moment_ref, plan_ref, plan_sem, sems):
     width = outer_ref.shape[-1]
     plan_copy = pltpu.make_async_copy(plan_hbm, plan_ref, plan_sem)
     plan_copy.start()
     y = my_y(workers)
     plan_copy.wait()
-    order = (1, 2, 3, 0)
-    copies = {}
-    for k in order:
+    copies = []
+    for k in range(QUARTERS):
         number, cols = place(y, k, width)
         f = plan_ref[number]
-        copies[k] = (
+        copies += [
             pltpu.make_async_copy(outer_hbm.at[f, :, cols], outer_ref.at[k], sems.at[0, k]),
             pltpu.make_async_copy(local_hbm.at[0, f, :, cols], local_ref.at[k], sems.at[1, k]),
             pltpu.make_async_copy(moment_hbm.at[f, :, cols], moment_ref.at[k], sems.at[2, k]),
-        )
-        copies[k][0].start()
-        copies[k][1].start()
-    for k in order:
-        copies[k][2].start()
-    for k in order:
-        copies[k][0].wait()
-        copies[k][1].wait()
-        for b in range(width // BLOCK):
-            at = slice(b * BLOCK, (b + 1) * BLOCK)
-            diff = outer_ref[k, :, at] - local_ref[k, :, at].astype(jnp.float32)
-            scale = jnp.max(jnp.abs(diff), axis=-1, keepdims=True) + EPS
-            out_refs[k][b] = (diff / scale).astype(jnp.bfloat16).astype(jnp.float32) * scale
-    for k in order:
-        copies[k][2].wait()
-
-
-def encode(plan, local, outer, moment, workers):
+        ]
+    for copy in copies:
+        copy.start()
+    for copy in copies:
+        copy.wait()
+    for b in range(width // BLOCK):
+        at = slice(b * BLOCK, (b + 1) * BLOCK)
+        own_ref[b] = coded(outer_ref[0, :, at], local_ref[0, :, at])
+
+
+def select(plan, local, outer, moment, workers):
     _, frags, rows, cols = local.shape
     width = SYNCED * cols // QUARTERS
-    piece = jax.ShapeDtypeStruct((width // BLOCK, rows, BLOCK), jnp.float32)
     kept = lambda dtype: jax.ShapeDtypeStruct((QUARTERS, rows, width), dtype)
     return pl.pallas_call(
-        lambda *refs: encode_kernel(workers, *refs),
-        out_shape=(piece,) * QUARTERS + (kept(jnp.float32), kept(local.dtype), kept(jnp.float32)),
+        lambda *refs: select_kernel(workers, *refs),
+        out_shape=(
+            jax.ShapeDtypeStruct((width // BLOCK, rows, BLOCK), jnp.float32),
+            kept(outer.dtype),
+            kept(local.dtype),
+            kept(moment.dtype),
+        ),
         in_specs=[HBM] * 4,
-        out_specs=(VMEM,) * (QUARTERS + 3),
+        out_specs=(VMEM,) * 4,
         scratch_shapes=[
             pltpu.SMEM(plan.shape, jnp.int32),
             pltpu.SemaphoreType.DMA(()),
             pltpu.SemaphoreType.DMA((3, QUARTERS)),
         ],
         compiler_params=PARAMS,
-        name="encode",
-    )(*[pltpu.with_memory_space_constraint(a, pltpu.HBM) for a in (plan, local, outer, moment)])
+        cost_estimate=pl.CostEstimate(flops=10**6, bytes_accessed=4 * 10**6, transcendentals=0),
+        name="select",
+    )(*in_hbm(plan, local, outer, moment))
 
 
 def add_kernel(*refs):
@@ -207,10 +261,13 @@
     def inside(array):
         return lax.all_to_all(array, "replica", 0, 0, axis_index_groups=groups, tiled=True)
 
-    *coded, outer_sel, local_sel, moment_sel = encode(plan, local, outer, moment, workers)
-    mine = add([coded[0]] + [along_y(coded[k], k) for k in range(1, QUARTERS)])
+    sent = encode(plan, local, outer, workers)
+    arrived = [along_y(array, k) for k, array in zip(SENT, sent)]
+    own, outer_sel, local_sel, moment_sel = select(plan, local, outer, moment, workers)
+    mine = add([own] + arrived)
     quarter = inside(mean(inside(mine), workers))
-    quarters = [quarter] + [along_y(quarter, k) for k in range(1, QUARTERS)]
+    received = {k: along_y(quarter, k) for k in reversed(SENT)}
+    quarters = [quarter] + [received[k] for k in range(1, QUARTERS)]
     squares_sum = squares(quarters, workers)
     for bit in (1, 2):
         squares_sum += lax.ppermute(squares_sum, "mp", [(m, m ^ bit) for m in range(shares)])

time: 64.7 us -> 62.1 us (0.960)
  waiting for transfers between devices: 14.9 us -> 12.4 us
  Pallas kernels: 3.66 us -> 5.37 us
  blocking collectives: 31.5 us -> 30 us
    ppermute x6, waiting for transfers between devices: 12 us -> 9.48 us  [along_y(): lax.ppermute(array, 'replica', [(r, r ^ k * inner) for r in range(workers)])]
    pallas_call x0 -> x1, Pallas kernels: none -> 2.28 us  [select(): pl.pallas_call(lambda *refs: select_kernel(workers, *refs), out_shape=(ja...]
    all_to_all x2, blocking collectives: 31.5 us -> 30 us  [inside(): lax.all_to_all(array, 'replica', 0, 0, axis_index_groups=groups, tiled=True)]
    ppermute x2, starting transfers between devices: 5.66 us -> 4.42 us  [shards(): lax.ppermute(squares_sum, 'mp', [(m, m ^ bit) for m in range(shares)])]
    ppermute x6, starting transfers between devices: 8.09 us -> 8.99 us  [along_y(): lax.ppermute(array, 'replica', [(r, r ^ k * inner) for r in range(workers)])]
  transfers between devices with their start and end apart: 8 -> 8, of which waited for: 6 -> 5; matrix products, arithmetic and copies ran while one was open for 0% -> 0% of each run, Pallas kernels for 0% -> 4%
where the time goes in v4:
time: 62.1 us; the launch traced here: 61.9 us
  blocking collectives  30 us (48%)
  starting transfers between devices  13.4 us (22%)
  waiting for transfers between devices  12.4 us (20%)
  Pallas kernels  5.37 us (9%)
  between operations  0.68 us (1%)
    all_to_all x2, blocking collectives, inside(): lax.all_to_all(array, 'replica', 0, 0, axis_index_groups=groups, tiled=True)  30 us
    ppermute x6, waiting for transfers between devices, along_y(): lax.ppermute(array, 'replica', [(r, r ^ k * inner) for r in range(workers)])  9.48 us
    ppermute x6, starting transfers between devices, along_y(): lax.ppermute(array, 'replica', [(r, r ^ k * inner) for r in range(workers)])  8.99 us
    ppermute x2, starting transfers between devices, shards(): lax.ppermute(squares_sum, 'mp', [(m, m ^ bit) for m in range(shares)])  4.42 us
    ppermute x2, waiting for transfers between devices, shards(): lax.ppermute(squares_sum, 'mp', [(m, m ^ bit) for m in range(shares)])  2.97 us
    pallas_call x1, Pallas kernels, select(): pl.pallas_call(lambda *refs: select_kernel(workers, *refs), out_shape=(ja...  2.28 us
    pallas_call x1, Pallas kernels, encode(): pl.pallas_call(lambda *refs: encode_kernel(workers, *refs), out_shape=(pi...  1.65 us
  transfers between devices with their start and end apart: 8, of which 5 were waited for; matrix products, arithmetic and copies ran while one was open for 0% of the time, Pallas kernels for 4%

profile of v4, /device:TPU:1, one launch (start us, length us, event | category | flops | bytes accessed | tf_op | source)
XLA Modules:
  0.0 61.9 jit_solution(14701548539340279782)
XLA Ops:
  0.6 1.6 %encode.1 = (f32[16,16,128]{2,1,0:T(8,128)S(1)}, f32[16,16,128]{2,1,0:T(8,128)S(1)}, f32[16,16,128]{2,1,0:T(8,128)S(1)}) custom-call(s32[4]{0:T(128)} %refs_0_.3, bf16[1,4,16,4096]{3,2,1,0:T(8,128)(2,1)} %refs_1_.3, f32[4,16,4096]{2,1,0:T(8,128)} %refs_2_.3), custom_call_target="tpu_custom_call" | custom-call | tf_op jit(solution)/shard_map/encode/pallas_call | solution.py:74
  2.3 3.8 %collective-permute-start = (f32[16,16,128]{2,1,0:T(8,128)S(1)}, f32[16,16,128]{2,1,0:T(8,128)S(1)}, u32[]{:S(2)}, u32[]{:S(2)}) collective-permute-start(f32[16,16,128]{2,1,0:T(8,128)S(1)} %get-tuple-element.11), channel_id=1, source_target_pairs={{0,128},{4,132},{8,136},{12,140},{16,144},{20,148},{24,152},{28,15... | collective-permute-start | bytes 393224 | tf_op jit(solution)/shard_map/ppermute | solution.py:259
  6.1 0.8 %collective-permute-start.1 = (f32[16,16,128]{2,1,0:T(8,128)S(1)}, f32[16,16,128]{2,1,0:T(8,128)S(1)}, u32[]{:S(2)}, u32[]{:S(2)}) collective-permute-start(f32[16,16,128]{2,1,0:T(8,128)S(1)} %get-tuple-element.12), channel_id=1, source_target_pairs={{0,192},{4,196},{8,200},{12,204},{16,208},{20,212},{24,216},{28,22... | collective-permute-start | bytes 393224 | tf_op jit(solution)/shard_map/ppermute | solution.py:259
  6.9 0.0 collective-permute-start.2
  6.9 2.3 %select.1 = (f32[16,16,128]{2,1,0:T(8,128)S(1)}, f32[4,16,2048]{2,1,0:T(8,128)S(1)}, bf16[4,16,2048]{2,1,0:T(8,128)(2,1)S(1)}, f32[4,16,2048]{2,1,0:T(8,128)S(1)}) custom-call(s32[4]{0:T(128)} %refs_0_.3, bf16[1,4,16,4096]{3,2,1,0:T(8,128)(2,1)} %refs_1_.3, f32[4,16,4096]{2,1,0:T(8,128)} %refs_2_.3, f32[4,16,4096]{2,1,0:T(8,128)} %refs_3_.1), custom_call_target="tpu_custom_call" | custom-call | flops 1000000 | bytes 4000000 | tf_op jit(solution)/shard_map/select/pallas_call | solution.py:119
  9.2 0.0 collective-permute-done.refs_1_
  9.2 4.6 %collective-permute-done.1.refs_2_ = f32[16,16,128]{2,1,0:T(8,128)S(1)} collective-permute-done((f32[16,16,128]{2,1,0:T(8,128)S(1)}, f32[16,16,128]{2,1,0:T(8,128)S(1)}, u32[]{:S(2)}, u32[]{:S(2)}) %collective-permute-start.1) | collective-permute-done | bytes 131104 | tf_op jit(solution)/shard_map/ppermute | solution.py:259
  13.8 0.0 collective-permute-done.2.refs_3_
  13.9 18.0 %all_to_all.10.refs_0_ = f32[16,16,128]{2,1,0:T(8,128)S(1)} all-to-all(f32[16,16,128]{2,1,0:T(8,128)S(1)} %add.9), channel_id=1, replica_groups={{0,4,8,12,16,20,24,28,32,36,40,44,48,52,56,60},{64,68,72,76,80,84,88,92..., dimensions={0} | all-to-all | bytes 262144 | tf_op jit(solution)/shard_map/all_to_all | solution.py:262
  31.9 12.0 %all_to_all.11.refs_0_ = f32[16,16,128]{2,1,0:T(8,128)S(1)} all-to-all(f32[16,16,128]{2,1,0:T(8,128)S(1)} %mean.1), channel_id=1, replica_groups={{0,4,8,12,16,20,24,28,32,36,40,44,48,52,56,60},{64,68,72,76,80,84,88,92..., dimensions={0} | all-to-all | bytes 262144 | tf_op jit(solution)/shard_map/all_to_all | solution.py:262
  43.9 3.8 %collective-permute-start.5 = (f32[16,16,128]{2,1,0:T(8,128)S(1)}, f32[16,16,128]{2,1,0:T(8,128)S(1)}, u32[]{:S(2)}, u32[]{:S(2)}) collective-permute-start(f32[16,16,128]{2,1,0:T(8,128)S(1)} %all_to_all.11.refs_0_), channel_id=1, source_target_pairs={{0,192},{4,196},{8,200},{12,204},{16,208},{20,212},{24,216},{28,22... | collective-permute-start | bytes 393224 | tf_op jit(solution)/shard_map/ppermute | solution.py:259
  47.7 0.0 collective-permute-start.4
  47.7 0.5 collective-permute-start.3
  48.3 2.7 %collective-permute-done.5.refs_3_ = f32[16,16,128]{2,1,0:T(8,128)S(1)} collective-permute-done((f32[16,16,128]{2,1,0:T(8,128)S(1)}, f32[16,16,128]{2,1,0:T(8,128)S(1)}, u32[]{:S(2)}, u32[]{:S(2)}) %collective-permute-start.5) | collective-permute-done | bytes 131104 | tf_op jit(solution)/shard_map/ppermute | solution.py:259
  51.0 2.1 %collective-permute-done.4.refs_2_ = f32[16,16,128]{2,1,0:T(8,128)S(1)} collective-permute-done((f32[16,16,128]{2,1,0:T(8,128)S(1)}, f32[16,16,128]{2,1,0:T(8,128)S(1)}, u32[]{:S(2)}, u32[]{:S(2)}) %collective-permute-start.4) | collective-permute-done | bytes 131104 | tf_op jit(solution)/shard_map/ppermute | solution.py:259
  53.1 0.0 collective-permute-done.3.refs_1_
  53.1 0.2 squares.1
  53.3 4.1 %collective-permute-start.6 = (f32[8,128]{1,0:T(8,128)S(1)}, f32[8,128]{1,0:T(8,128)S(1)}, u32[]{:S(2)}, u32[]{:S(2)}) collective-permute-start(f32[8,128]{1,0:T(8,128)S(1)} %squares.1), channel_id=1, source_target_pairs={{0,1},{1,0},{2,3},{3,2},{4,5},{5,4},{6,7},{7,6},{8,9},{9,8},{10,11... | collective-permute-start | bytes 12296 | tf_op jit(solution)/shard_map/ppermute | solution.py:273
  57.4 0.8 %collective-permute-done.6 = f32[8,128]{1,0:T(8,128)S(1)} collective-permute-done((f32[8,128]{1,0:T(8,128)S(1)}, f32[8,128]{1,0:T(8,128)S(1)}, u32[]{:S(2)}, u32[]{:S(2)}) %collective-permute-start.6) | collective-permute-done | bytes 4128 | tf_op jit(solution)/shard_map/ppermute | solution.py:273
  58.3 0.3 collective-permute-start.7
  58.6 2.1 %collective-permute-done.7 = f32[8,128]{1,0:T(8,128)S(1)} collective-permute-done((f32[8,128]{1,0:T(8,128)S(1)}, f32[8,128]{1,0:T(8,128)S(1)}, u32[]{:S(2)}, u32[]{:S(2)}) %collective-permute-start.7) | collective-permute-done | bytes 4128 | tf_op jit(solution)/shard_map/ppermute | solution.py:273
  60.7 1.2 %update.1 = (f32[2,16,4096]{2,1,0:T(8,128)}, f32[2,16,4096]{2,1,0:T(8,128)}, bf16[1,2,16,4096]{3,2,1,0:T(8,128)(2,1)}) custom-call(f32[16,16,128]{2,1,0:T(8,128)S(1)} %all_to_all.11.refs_0_, f32[16,16,128]{2,1,0:T(8,128)S(1)} %collective-permute-done.3.refs_1_, f32[16,16,128]{2,1,0:T(8,128)S(1)} %collective-permute-done.4.refs_2_, ...), custom_call_target="tpu_custom_call" | custom-call | tf_op jit(solution)/shard_map/update/pallas_call | solution.py:229
  (4 shorter events, 0.1 us)
Async XLA Ops:
  2.3 6.9 %collective-permute-start = (f32[16,16,128]{2,1,0:T(8,128)S(1)}, f32[16,16,128]{2,1,0:T(8,128)S(1)}, u32[]{:S(2)}, u32[]{:S(2)}) collective-permute-start(f32[16,16,128]{2,1,0:T(8,128)S(1)} %get-tuple-element.11), channel_id=1, source_target_pairs={{0,128},{4,132},{8,136},{12,140},{16,144},{20,148},{24,152},{28,15... | collective-permute-start | bytes 393224 | tf_op jit(solution)/shard_map/ppermute | solution.py:259
  6.1 7.7 %collective-permute-start.1 = (f32[16,16,128]{2,1,0:T(8,128)S(1)}, f32[16,16,128]{2,1,0:T(8,128)S(1)}, u32[]{:S(2)}, u32[]{:S(2)}) collective-permute-start(f32[16,16,128]{2,1,0:T(8,128)S(1)} %get-tuple-element.12), channel_id=1, source_target_pairs={{0,192},{4,196},{8,200},{12,204},{16,208},{20,212},{24,216},{28,22... | collective-permute-start | bytes 393224 | tf_op jit(solution)/shard_map/ppermute | solution.py:259
  6.9 6.9 %collective-permute-start.2 = (f32[16,16,128]{2,1,0:T(8,128)S(1)}, f32[16,16,128]{2,1,0:T(8,128)S(1)}, u32[]{:S(2)}, u32[]{:S(2)}) collective-permute-start(f32[16,16,128]{2,1,0:T(8,128)S(1)} %get-tuple-element.13), channel_id=1, source_target_pairs={{0,64},{4,68},{8,72},{12,76},{16,80},{20,84},{24,88},{28,92},{32,9... | collective-permute-start | bytes 393224 | tf_op jit(solution)/shard_map/ppermute | solution.py:259
  43.9 7.1 %collective-permute-start.5 = (f32[16,16,128]{2,1,0:T(8,128)S(1)}, f32[16,16,128]{2,1,0:T(8,128)S(1)}, u32[]{:S(2)}, u32[]{:S(2)}) collective-permute-start(f32[16,16,128]{2,1,0:T(8,128)S(1)} %all_to_all.11.refs_0_), channel_id=1, source_target_pairs={{0,192},{4,196},{8,200},{12,204},{16,208},{20,212},{24,216},{28,22... | collective-permute-start | bytes 393224 | tf_op jit(solution)/shard_map/ppermute | solution.py:259
  47.7 5.4 %collective-permute-start.4 = (f32[16,16,128]{2,1,0:T(8,128)S(1)}, f32[16,16,128]{2,1,0:T(8,128)S(1)}, u32[]{:S(2)}, u32[]{:S(2)}) collective-permute-start(f32[16,16,128]{2,1,0:T(8,128)S(1)} %all_to_all.11.refs_0_), channel_id=1, source_target_pairs={{0,128},{4,132},{8,136},{12,140},{16,144},{20,148},{24,152},{28,15... | collective-permute-start | bytes 393224 | tf_op jit(solution)/shard_map/ppermute | solution.py:259
  47.7 5.4 %collective-permute-start.3 = (f32[16,16,128]{2,1,0:T(8,128)S(1)}, f32[16,16,128]{2,1,0:T(8,128)S(1)}, u32[]{:S(2)}, u32[]{:S(2)}) collective-permute-start(f32[16,16,128]{2,1,0:T(8,128)S(1)} %all_to_all.11.refs_0_), channel_id=1, source_target_pairs={{0,64},{4,68},{8,72},{12,76},{16,80},{20,84},{24,88},{28,92},{32,9... | collective-permute-start | bytes 393224 | tf_op jit(solution)/shard_map/ppermute | solution.py:259
  53.3 4.9 %collective-permute-start.6 = (f32[8,128]{1,0:T(8,128)S(1)}, f32[8,128]{1,0:T(8,128)S(1)}, u32[]{:S(2)}, u32[]{:S(2)}) collective-permute-start(f32[8,128]{1,0:T(8,128)S(1)} %squares.1), channel_id=1, source_target_pairs={{0,1},{1,0},{2,3},{3,2},{4,5},{5,4},{6,7},{7,6},{8,9},{9,8},{10,11... | collective-permute-start | bytes 12296 | tf_op jit(solution)/shard_map/ppermute | solution.py:273
  58.3 2.5 %collective-permute-start.7 = (f32[8,128]{1,0:T(8,128)S(1)}, f32[8,128]{1,0:T(8,128)S(1)}, u32[]{:S(2)}, u32[]{:S(2)}) collective-permute-start(f32[8,128]{1,0:T(8,128)S(1)} %add.7), channel_id=1, source_target_pairs={{0,2},{1,3},{2,0},{3,1},{4,6},{5,7},{6,4},{7,5},{8,10},{9,11},{10,... | collective-permute-start | bytes 12296 | tf_op jit(solution)/shard_map/ppermute | solution.py:273

commit v5 on v4

--- a/solution.py
+++ b/solution.py
@@ -21,6 +21,7 @@
 
 
 SENT = (2, 3, 1)
+HELD = (0, 1, 3, 2)
 
 
 def in_hbm(*arrays):
@@ -49,22 +50,31 @@
     frags = outer_ref.shape[0]
     plan_copy = pltpu.make_async_copy(plan_hbm, plan_ref, plan_sem)
     plan_copy.start()
-    copies = []
+    def copies(f):
+        return (
+            pltpu.make_async_copy(outer_hbm.at[f], outer_ref.at[f], sems.at[0, f]),
+            pltpu.make_async_copy(local_hbm.at[0, f], local_ref.at[f], sems.at[1, f]),
+        )
+
     for f in range(frags):
-        copies.append(pltpu.make_async_copy(outer_hbm.at[f], outer_ref.at[f], sems.at[0, f]))
-        copies.append(pltpu.make_async_copy(local_hbm.at[0, f], local_ref.at[f], sems.at[1, f]))
-    for copy in copies:
-        copy.start()
+        for copy in copies(f):
+            copy.start()
     y = my_y(workers)
     plan_copy.wait()
-    for copy in copies:
-        copy.wait()
+    waited = set()
     for k, out_ref in zip(SENT, out_refs):
         number, cols = place(y, k, width)
         f = plan_ref[number]
+        if k // 2 not in waited:
+            waited.add(k // 2)
+            for copy in copies(f):
+                copy.wait()
         for b in range(width // BLOCK):
             at = pl.ds(pl.multiple_of(cols.start + b * BLOCK, BLOCK), BLOCK)
             out_ref[b] = coded(outer_ref[f, :, at], local_ref[f, :, at])
+    for number in range(SYNCED, frags):
+        for copy in copies(plan_ref[number]):
+            copy.wait()
 
 
 def encode(plan, local, outer, workers):
@@ -174,7 +184,7 @@
     y = my_y(workers)
     row = lax.broadcasted_iota(jnp.int32, out_ref.shape, 0)
     total = jnp.zeros(out_ref.shape, jnp.float32)
-    sums = [jnp.sum(q[...] * q[...]) for q in quarters]
+    sums = {k: jnp.sum(q[...] * q[...]) for k, q in zip(HELD, quarters)}
     for k in range(0, QUARTERS, 2):
         number, _ = place(y, k, BLOCK)
         total = jnp.where(row == number, sums[k] + sums[k + 1], total)
@@ -194,17 +204,18 @@
 
 def update_kernel(workers, entries, *refs):
     quarters, refs = refs[:QUARTERS], refs[QUARTERS:]
-    squares_ref, outer_ref, local_ref, moment_ref, new_outer, new_moment, merged, outer_buf, moment_buf, merged_buf, factor_ref, sems = refs
+    early_ref, back_ref, outer_ref, local_ref, moment_ref, new_outer, new_moment, merged, outer_buf, moment_buf, merged_buf, factor_ref, sems = refs
     width = outer_ref.shape[-1]
     y = my_y(workers)
-    factor_ref[...] = jnp.minimum(1.0, CLIP / jnp.sqrt(squares_ref[...] / entries + EPS))
+    total = jnp.where(lax.axis_index("mp") % 2 == 1, early_ref[...], back_ref[...])
+    factor_ref[...] = jnp.minimum(1.0, CLIP / jnp.sqrt(total / entries + EPS))
     copies = []
-    for k in range(QUARTERS):
+    for quarter_ref, k in zip(quarters, HELD):
         number, cols = place(y, k, width)
         factor = factor_ref[pl.ds(number, 1)]
         for b in range(width // BLOCK):
             at = slice(b * BLOCK, (b + 1) * BLOCK)
-            grad = quarters[k][b] * factor
+            grad = quarter_ref[b] * factor
             moment_next = MU * moment_ref[k, :, at] + grad
             outer_next = outer_ref[k, :, at] - LR * (MU * moment_next + grad)
             moment_buf[k, :, at] = moment_next
@@ -223,7 +234,7 @@
         copy.wait()
 
 
-def update(quarters, squares_sum, outer_sel, local_sel, moment_sel, workers, entries):
+def update(quarters, totals, outer_sel, local_sel, moment_sel, workers, entries):
     _, rows, width = outer_sel.shape
     cols = QUARTERS * width // SYNCED
     return pl.pallas_call(
@@ -233,7 +244,7 @@
             jax.ShapeDtypeStruct((SYNCED, rows, cols), jnp.float32),
             jax.ShapeDtypeStruct((1, SYNCED, rows, cols), local_sel.dtype),
         ),
-        in_specs=[VMEM] * (QUARTERS + 4),
+        in_specs=[VMEM] * (QUARTERS + 5),
         out_specs=(HBM,) * 3,
         scratch_shapes=[
             pltpu.VMEM(outer_sel.shape, jnp.float32),
@@ -244,7 +255,7 @@
         ],
         compiler_params=PARAMS,
         name="update",
-    )(*quarters, squares_sum, outer_sel, local_sel, moment_sel)
+    )(*quarters, *totals, outer_sel, local_sel, moment_sel)
 
 
 def shards(local, outer, moment, plan):
@@ -266,12 +277,16 @@
     own, outer_sel, local_sel, moment_sel = select(plan, local, outer, moment, workers)
     mine = add([own] + arrived)
     quarter = inside(mean(inside(mine), workers))
-    received = {k: along_y(quarter, k) for k in reversed(SENT)}
-    quarters = [quarter] + [received[k] for k in range(1, QUARTERS)]
-    squares_sum = squares(quarters, workers)
-    for bit in (1, 2):
-        squares_sum += lax.ppermute(squares_sum, "mp", [(m, m ^ bit) for m in range(shares)])
-    return update(quarters, squares_sum, outer_sel, local_sel, moment_sel, workers, entries)
+    received = {k: along_y(quarter, k) for k in SENT}
+    quarters = [quarter] + [received[k] for k in HELD[1:]]
+    return update(quarters, mp_totals(squares(quarters, workers)), outer_sel, local_sel, moment_sel, workers, entries)
+
+
+def mp_totals(mine):
+    from_late = [lax.ppermute(mine, "mp", pairs) for pairs in ([(0, 3), (2, 1)], [(0, 1), (2, 3)])]
+    from_early = lax.ppermute(mine, "mp", [(1, 3), (3, 1)])
+    total = (mine + from_early) + (from_late[0] + from_late[1])
+    return total, lax.ppermute(total, "mp", [(1, 0), (3, 2)])
 
 
 def solution(mesh):

time: 62.1 us -> 65.3 us (1.052)
  starting transfers between devices: 13.4 us -> 15.7 us
  waiting for transfers between devices: 12.4 us -> 13.6 us
    ppermute x2 -> x4, starting transfers between devices: 4.42 us -> 6.54 us  [the longest x2 2.58 us: mp_totals(): lax.ppermute(mine, 'mp', pairs)]
    ppermute x2 -> x4, waiting for transfers between devices: 2.97 us -> 4.87 us  [the longest x2 4.07 us: mp_totals(): lax.ppermute(mine, 'mp', pairs)]
    ppermute x6, waiting for transfers between devices: 9.48 us -> 8.73 us  [along_y(): lax.ppermute(array, 'replica', [(r, r ^ k * inner) for r in range(workers)])]
  transfers between devices with their start and end apart: 8 -> 10, of which waited for: 5 -> 7; matrix products, arithmetic and copies ran while one was open for 0% -> 0% of each run, Pallas kernels for 4% -> 4%
where the time goes in v5:
time: 65.3 us; the launch traced here: 65 us
  blocking collectives  29.7 us (45%)
  starting transfers between devices  15.7 us (24%)
  waiting for transfers between devices  13.6 us (21%)
  Pallas kernels  5.31 us (8%)
  between operations  0.71 us (1%)
    all_to_all x2, blocking collectives, inside(): lax.all_to_all(array, 'replica', 0, 0, axis_index_groups=groups, tiled=True)  29.7 us
    ppermute x6, starting transfers between devices, along_y(): lax.ppermute(array, 'replica', [(r, r ^ k * inner) for r in range(workers)])  9.14 us
    ppermute x6, waiting for transfers between devices, along_y(): lax.ppermute(array, 'replica', [(r, r ^ k * inner) for r in range(workers)])  8.73 us
    ppermute x2, waiting for transfers between devices, mp_totals(): lax.ppermute(mine, 'mp', pairs)  4.07 us
    ppermute x2, starting transfers between devices, mp_totals(): lax.ppermute(mine, 'mp', pairs)  2.58 us
    pallas_call x1, Pallas kernels, select(): pl.pallas_call(lambda *refs: select_kernel(workers, *refs), out_shape=(ja...  2.28 us
    ppermute x1, starting transfers between devices, mp_totals(): from_early = lax.ppermute(mine, 'mp', [(1, 3), (3, 1)])  2.22 us
    ppermute x1, starting transfers between devices, mp_totals(): return (total, lax.ppermute(total, 'mp', [(1, 0), (3, 2)]))  1.74 us
  transfers between devices with their start and end apart: 10, of which 7 were waited for; matrix products, arithmetic and copies ran while one was open for 0% of the time, Pallas kernels for 4%

profile of v5, /device:TPU:1, one launch (start us, length us, event | category | flops | bytes accessed | tf_op | source)
XLA Modules:
  0.0 65.0 jit_solution(14931050345875855603)
XLA Ops:
  0.6 1.6 %encode.1 = (f32[16,16,128]{2,1,0:T(8,128)S(1)}, f32[16,16,128]{2,1,0:T(8,128)S(1)}, f32[16,16,128]{2,1,0:T(8,128)S(1)}) custom-call(s32[4]{0:T(128)} %refs_0_.3, bf16[1,4,16,4096]{3,2,1,0:T(8,128)(2,1)} %refs_1_.3, f32[4,16,4096]{2,1,0:T(8,128)} %refs_2_.3), custom_call_target="tpu_custom_call" | custom-call | tf_op jit(solution)/shard_map/encode/pallas_call | solution.py:84
  2.2 4.0 %collective-permute-start = (f32[16,16,128]{2,1,0:T(8,128)S(1)}, f32[16,16,128]{2,1,0:T(8,128)S(1)}, u32[]{:S(2)}, u32[]{:S(2)}) collective-permute-start(f32[16,16,128]{2,1,0:T(8,128)S(1)} %get-tuple-element.11), channel_id=1, source_target_pairs={{0,128},{4,132},{8,136},{12,140},{16,144},{20,148},{24,152},{28,15... | collective-permute-start | bytes 393224 | tf_op jit(solution)/shard_map/ppermute | solution.py:270
  6.2 0.6 collective-permute-start.1
  6.8 0.0 collective-permute-start.2
  6.8 2.3 %select.1 = (f32[16,16,128]{2,1,0:T(8,128)S(1)}, f32[4,16,2048]{2,1,0:T(8,128)S(1)}, bf16[4,16,2048]{2,1,0:T(8,128)(2,1)S(1)}, f32[4,16,2048]{2,1,0:T(8,128)S(1)}) custom-call(s32[4]{0:T(128)} %refs_0_.3, bf16[1,4,16,4096]{3,2,1,0:T(8,128)(2,1)} %refs_1_.3, f32[4,16,4096]{2,1,0:T(8,128)} %refs_2_.3, f32[4,16,4096]{2,1,0:T(8,128)} %refs_3_.1), custom_call_target="tpu_custom_call" | custom-call | flops 1000000 | bytes 4000000 | tf_op jit(solution)/shard_map/select/pallas_call | solution.py:129
  9.1 0.0 collective-permute-done.refs_1_
  9.1 5.0 %collective-permute-done.1.refs_2_ = f32[16,16,128]{2,1,0:T(8,128)S(1)} collective-permute-done((f32[16,16,128]{2,1,0:T(8,128)S(1)}, f32[16,16,128]{2,1,0:T(8,128)S(1)}, u32[]{:S(2)}, u32[]{:S(2)}) %collective-permute-start.1) | collective-permute-done | bytes 131104 | tf_op jit(solution)/shard_map/ppermute | solution.py:270
  14.1 17.8 %all_to_all.10.refs_0_ = f32[16,16,128]{2,1,0:T(8,128)S(1)} all-to-all(f32[16,16,128]{2,1,0:T(8,128)S(1)} %add.16), channel_id=1, replica_groups={{0,4,8,12,16,20,24,28,32,36,40,44,48,52,56,60},{64,68,72,76,80,84,88,92..., dimensions={0} | all-to-all | bytes 262144 | tf_op jit(solution)/shard_map/all_to_all | solution.py:273
  32.0 11.9 %all_to_all.11.refs_0_ = f32[16,16,128]{2,1,0:T(8,128)S(1)} all-to-all(f32[16,16,128]{2,1,0:T(8,128)S(1)} %mean.1), channel_id=1, replica_groups={{0,4,8,12,16,20,24,28,32,36,40,44,48,52,56,60},{64,68,72,76,80,84,88,92..., dimensions={0} | all-to-all | bytes 262144 | tf_op jit(solution)/shard_map/all_to_all | solution.py:273
  43.9 2.0 %collective-permute-start.5 = (f32[16,16,128]{2,1,0:T(8,128)S(1)}, f32[16,16,128]{2,1,0:T(8,128)S(1)}, u32[]{:S(2)}, u32[]{:S(2)}) collective-permute-start(f32[16,16,128]{2,1,0:T(8,128)S(1)} %all_to_all.11.refs_0_), channel_id=1, source_target_pairs={{0,128},{4,132},{8,136},{12,140},{16,144},{20,148},{24,152},{28,15... | collective-permute-start | bytes 393224 | tf_op jit(solution)/shard_map/ppermute | solution.py:270
  45.9 2.3 %collective-permute-start.4 = (f32[16,16,128]{2,1,0:T(8,128)S(1)}, f32[16,16,128]{2,1,0:T(8,128)S(1)}, u32[]{:S(2)}, u32[]{:S(2)}) collective-permute-start(f32[16,16,128]{2,1,0:T(8,128)S(1)} %all_to_all.11.refs_0_), channel_id=1, source_target_pairs={{0,192},{4,196},{8,200},{12,204},{16,208},{20,212},{24,216},{28,22... | collective-permute-start | bytes 393224 | tf_op jit(solution)/shard_map/ppermute | solution.py:270
  48.2 0.2 collective-permute-start.3
  48.4 0.8 %collective-permute-done.5.refs_3_ = f32[16,16,128]{2,1,0:T(8,128)S(1)} collective-permute-done((f32[16,16,128]{2,1,0:T(8,128)S(1)}, f32[16,16,128]{2,1,0:T(8,128)S(1)}, u32[]{:S(2)}, u32[]{:S(2)}) %collective-permute-start.5) | collective-permute-done | bytes 131104 | tf_op jit(solution)/shard_map/ppermute | solution.py:270
  49.2 2.2 %collective-permute-done.4.refs_2_ = f32[16,16,128]{2,1,0:T(8,128)S(1)} collective-permute-done((f32[16,16,128]{2,1,0:T(8,128)S(1)}, f32[16,16,128]{2,1,0:T(8,128)S(1)}, u32[]{:S(2)}, u32[]{:S(2)}) %collective-permute-start.4) | collective-permute-done | bytes 131104 | tf_op jit(solution)/shard_map/ppermute | solution.py:270
  51.4 0.7 %collective-permute-done.3.refs_1_ = f32[16,16,128]{2,1,0:T(8,128)S(1)} collective-permute-done((f32[16,16,128]{2,1,0:T(8,128)S(1)}, f32[16,16,128]{2,1,0:T(8,128)S(1)}, u32[]{:S(2)}, u32[]{:S(2)}) %collective-permute-start.3) | collective-permute-done | bytes 131104 | tf_op jit(solution)/shard_map/ppermute | solution.py:270
  52.2 0.2 squares.1
  52.4 1.3 %collective-permute-start.8 = (f32[8,128]{1,0:T(8,128)S(1)}, f32[8,128]{1,0:T(8,128)S(1)}, u32[]{:S(2)}, u32[]{:S(2)}) collective-permute-start(f32[8,128]{1,0:T(8,128)S(1)} %squares.1), channel_id=1, source_target_pairs={{0,1},{2,3},{4,5},{6,7},{8,9},{10,11},{12,13},{14,15},{16,17},{18,... | collective-permute-start | bytes 12296 | tf_op jit(solution)/shard_map/ppermute | solution.py:286
  53.7 1.3 %collective-permute-start.7 = (f32[8,128]{1,0:T(8,128)S(1)}, f32[8,128]{1,0:T(8,128)S(1)}, u32[]{:S(2)}, u32[]{:S(2)}) collective-permute-start(f32[8,128]{1,0:T(8,128)S(1)} %squares.1), channel_id=1, source_target_pairs={{0,3},{2,1},{4,7},{6,5},{8,11},{10,9},{12,15},{14,13},{16,19},{18,... | collective-permute-start | bytes 12296 | tf_op jit(solution)/shard_map/ppermute | solution.py:286
  55.0 2.2 %collective-permute-start.6 = (f32[8,128]{1,0:T(8,128)S(1)}, f32[8,128]{1,0:T(8,128)S(1)}, u32[]{:S(2)}, u32[]{:S(2)}) collective-permute-start(f32[8,128]{1,0:T(8,128)S(1)} %squares.1), channel_id=1, source_target_pairs={{1,3},{3,1},{5,7},{7,5},{9,11},{11,9},{13,15},{15,13},{17,19},{19,... | collective-permute-start | bytes 12296 | tf_op jit(solution)/shard_map/ppermute | solution.py:287
  57.2 1.9 %collective-permute-done.8 = f32[8,128]{1,0:T(8,128)S(1)} collective-permute-done((f32[8,128]{1,0:T(8,128)S(1)}, f32[8,128]{1,0:T(8,128)S(1)}, u32[]{:S(2)}, u32[]{:S(2)}) %collective-permute-start.8) | collective-permute-done | bytes 4128 | tf_op jit(solution)/shard_map/ppermute | solution.py:286
  59.1 2.1 %collective-permute-done.7 = f32[8,128]{1,0:T(8,128)S(1)} collective-permute-done((f32[8,128]{1,0:T(8,128)S(1)}, f32[8,128]{1,0:T(8,128)S(1)}, u32[]{:S(2)}, u32[]{:S(2)}) %collective-permute-start.7) | collective-permute-done | bytes 4128 | tf_op jit(solution)/shard_map/ppermute | solution.py:286
  61.3 1.7 %collective-permute-start.9 = (f32[8,128]{1,0:T(8,128)S(1)}, f32[8,128]{1,0:T(8,128)S(1)}, u32[]{:S(2)}, u32[]{:S(2)}) collective-permute-start(f32[8,128]{1,0:T(8,128)S(1)} %add_add_fusion.refs_4_), channel_id=1, source_target_pairs={{1,0},{3,2},{5,4},{7,6},{9,8},{11,10},{13,12},{15,14},{17,16},{19,... | collective-permute-start | bytes 12296 | tf_op jit(solution)/shard_map/ppermute | solution.py:289
  63.0 0.8 %collective-permute-done.9.refs_5_ = f32[8,128]{1,0:T(8,128)S(1)} collective-permute-done((f32[8,128]{1,0:T(8,128)S(1)}, f32[8,128]{1,0:T(8,128)S(1)}, u32[]{:S(2)}, u32[]{:S(2)}) %collective-permute-start.9) | collective-permute-done | bytes 4128 | tf_op jit(solution)/shard_map/ppermute | solution.py:289
  63.8 1.2 %update.1 = (f32[2,16,4096]{2,1,0:T(8,128)}, f32[2,16,4096]{2,1,0:T(8,128)}, bf16[1,2,16,4096]{3,2,1,0:T(8,128)(2,1)}) custom-call(f32[16,16,128]{2,1,0:T(8,128)S(1)} %all_to_all.11.refs_0_, f32[16,16,128]{2,1,0:T(8,128)S(1)} %collective-permute-done.3.refs_1_, f32[16,16,128]{2,1,0:T(8,128)S(1)} %collective-permute-done.4.refs_2_, ...), custom_call_target="tpu_custom_call" | custom-call | tf_op jit(solution)/shard_map/update/pallas_call | solution.py:240
  (5 shorter events, 0.1 us)
Async XLA Ops:
  2.2 6.9 %collective-permute-start = (f32[16,16,128]{2,1,0:T(8,128)S(1)}, f32[16,16,128]{2,1,0:T(8,128)S(1)}, u32[]{:S(2)}, u32[]{:S(2)}) collective-permute-start(f32[16,16,128]{2,1,0:T(8,128)S(1)} %get-tuple-element.11), channel_id=1, source_target_pairs={{0,128},{4,132},{8,136},{12,140},{16,144},{20,148},{24,152},{28,15... | collective-permute-start | bytes 393224 | tf_op jit(solution)/shard_map/ppermute | solution.py:270
  6.2 7.9 %collective-permute-start.1 = (f32[16,16,128]{2,1,0:T(8,128)S(1)}, f32[16,16,128]{2,1,0:T(8,128)S(1)}, u32[]{:S(2)}, u32[]{:S(2)}) collective-permute-start(f32[16,16,128]{2,1,0:T(8,128)S(1)} %get-tuple-element.12), channel_id=1, source_target_pairs={{0,192},{4,196},{8,200},{12,204},{16,208},{20,212},{24,216},{28,22... | collective-permute-start | bytes 393224 | tf_op jit(solution)/shard_map/ppermute | solution.py:270
  6.8 7.3 %collective-permute-start.2 = (f32[16,16,128]{2,1,0:T(8,128)S(1)}, f32[16,16,128]{2,1,0:T(8,128)S(1)}, u32[]{:S(2)}, u32[]{:S(2)}) collective-permute-start(f32[16,16,128]{2,1,0:T(8,128)S(1)} %get-tuple-element.13), channel_id=1, source_target_pairs={{0,64},{4,68},{8,72},{12,76},{16,80},{20,84},{24,88},{28,92},{32,9... | collective-permute-start | bytes 393224 | tf_op jit(solution)/shard_map/ppermute | solution.py:270
  43.9 5.3 %collective-permute-start.5 = (f32[16,16,128]{2,1,0:T(8,128)S(1)}, f32[16,16,128]{2,1,0:T(8,128)S(1)}, u32[]{:S(2)}, u32[]{:S(2)}) collective-permute-start(f32[16,16,128]{2,1,0:T(8,128)S(1)} %all_to_all.11.refs_0_), channel_id=1, source_target_pairs={{0,128},{4,132},{8,136},{12,140},{16,144},{20,148},{24,152},{28,15... | collective-permute-start | bytes 393224 | tf_op jit(solution)/shard_map/ppermute | solution.py:270
  45.9 5.6 %collective-permute-start.4 = (f32[16,16,128]{2,1,0:T(8,128)S(1)}, f32[16,16,128]{2,1,0:T(8,128)S(1)}, u32[]{:S(2)}, u32[]{:S(2)}) collective-permute-start(f32[16,16,128]{2,1,0:T(8,128)S(1)} %all_to_all.11.refs_0_), channel_id=1, source_target_pairs={{0,192},{4,196},{8,200},{12,204},{16,208},{20,212},{24,216},{28,22... | collective-permute-start | bytes 393224 | tf_op jit(solution)/shard_map/ppermute | solution.py:270
  48.2 4.0 %collective-permute-start.3 = (f32[16,16,128]{2,1,0:T(8,128)S(1)}, f32[16,16,128]{2,1,0:T(8,128)S(1)}, u32[]{:S(2)}, u32[]{:S(2)}) collective-permute-start(f32[16,16,128]{2,1,0:T(8,128)S(1)} %all_to_all.11.refs_0_), channel_id=1, source_target_pairs={{0,64},{4,68},{8,72},{12,76},{16,80},{20,84},{24,88},{28,92},{32,9... | collective-permute-start | bytes 393224 | tf_op jit(solution)/shard_map/ppermute | solution.py:270
  52.4 6.8 %collective-permute-start.8 = (f32[8,128]{1,0:T(8,128)S(1)}, f32[8,128]{1,0:T(8,128)S(1)}, u32[]{:S(2)}, u32[]{:S(2)}) collective-permute-start(f32[8,128]{1,0:T(8,128)S(1)} %squares.1), channel_id=1, source_target_pairs={{0,1},{2,3},{4,5},{6,7},{8,9},{10,11},{12,13},{14,15},{16,17},{18,... | collective-permute-start | bytes 12296 | tf_op jit(solution)/shard_map/ppermute | solution.py:286
  53.7 7.6 %collective-permute-start.7 = (f32[8,128]{1,0:T(8,128)S(1)}, f32[8,128]{1,0:T(8,128)S(1)}, u32[]{:S(2)}, u32[]{:S(2)}) collective-permute-start(f32[8,128]{1,0:T(8,128)S(1)} %squares.1), channel_id=1, source_target_pairs={{0,3},{2,1},{4,7},{6,5},{8,11},{10,9},{12,15},{14,13},{16,19},{18,... | collective-permute-start | bytes 12296 | tf_op jit(solution)/shard_map/ppermute | solution.py:286
  55.0 6.3 %collective-permute-start.6 = (f32[8,128]{1,0:T(8,128)S(1)}, f32[8,128]{1,0:T(8,128)S(1)}, u32[]{:S(2)}, u32[]{:S(2)}) collective-permute-start(f32[8,128]{1,0:T(8,128)S(1)} %squares.1), channel_id=1, source_target_pairs={{1,3},{3,1},{5,7},{7,5},{9,11},{11,9},{13,15},{15,13},{17,19},{19,... | collective-permute-start | bytes 12296 | tf_op jit(solution)/shard_map/ppermute | solution.py:287
  61.3 2.5 %collective-permute-start.9 = (f32[8,128]{1,0:T(8,128)S(1)}, f32[8,128]{1,0:T(8,128)S(1)}, u32[]{:S(2)}, u32[]{:S(2)}) collective-permute-start(f32[8,128]{1,0:T(8,128)S(1)} %add_add_fusion.refs_4_), channel_id=1, source_target_pairs={{1,0},{3,2},{5,4},{7,6},{9,8},{11,10},{13,12},{15,14},{17,16},{19,... | collective-permute-start | bytes 12296 | tf_op jit(solution)/shard_map/ppermute | solution.py:289

commit v6 on v5

--- a/solution.py
+++ b/solution.py
@@ -204,11 +204,10 @@
 
 def update_kernel(workers, entries, *refs):
     quarters, refs = refs[:QUARTERS], refs[QUARTERS:]
-    early_ref, back_ref, outer_ref, local_ref, moment_ref, new_outer, new_moment, merged, outer_buf, moment_buf, merged_buf, factor_ref, sems = refs
+    squares_ref, outer_ref, local_ref, moment_ref, new_outer, new_moment, merged, outer_buf, moment_buf, merged_buf, factor_ref, sems = refs
     width = outer_ref.shape[-1]
     y = my_y(workers)
-    total = jnp.where(lax.axis_index("mp") % 2 == 1, early_ref[...], back_ref[...])
-    factor_ref[...] = jnp.minimum(1.0, CLIP / jnp.sqrt(total / entries + EPS))
+    factor_ref[...] = jnp.minimum(1.0, CLIP / jnp.sqrt(squares_ref[...] / entries + EPS))
     copies = []
     for quarter_ref, k in zip(quarters, HELD):
         number, cols = place(y, k, width)
@@ -234,7 +233,7 @@
         copy.wait()
 
 
-def update(quarters, totals, outer_sel, local_sel, moment_sel, workers, entries):
+def update(quarters, squares_sum, outer_sel, local_sel, moment_sel, workers, entries):
     _, rows, width = outer_sel.shape
     cols = QUARTERS * width // SYNCED
     return pl.pallas_call(
@@ -244,7 +243,7 @@
             jax.ShapeDtypeStruct((SYNCED, rows, cols), jnp.float32),
             jax.ShapeDtypeStruct((1, SYNCED, rows, cols), local_sel.dtype),
         ),
-        in_specs=[VMEM] * (QUARTERS + 5),
+        in_specs=[VMEM] * (QUARTERS + 4),
         out_specs=(HBM,) * 3,
         scratch_shapes=[
             pltpu.VMEM(outer_sel.shape, jnp.float32),
@@ -255,7 +254,7 @@
         ],
         compiler_params=PARAMS,
         name="update",
-    )(*quarters, *totals, outer_sel, local_sel, moment_sel)
+    )(*quarters, squares_sum, outer_sel, local_sel, moment_sel)
 
 
 def shards(local, outer, moment, plan):
@@ -279,14 +278,12 @@
     quarter = inside(mean(inside(mine), workers))
     received = {k: along_y(quarter, k) for k in SENT}
     quarters = [quarter] + [received[k] for k in HELD[1:]]
-    return update(quarters, mp_totals(squares(quarters, workers)), outer_sel, local_sel, moment_sel, workers, entries)
-
-
-def mp_totals(mine):
-    from_late = [lax.ppermute(mine, "mp", pairs) for pairs in ([(0, 3), (2, 1)], [(0, 1), (2, 3)])]
-    from_early = lax.ppermute(mine, "mp", [(1, 3), (3, 1)])
-    total = (mine + from_early) + (from_late[0] + from_late[1])
-    return total, lax.ppermute(total, "mp", [(1, 0), (3, 2)])
+    return update(quarters, mp_total(squares(quarters, workers)), outer_sel, local_sel, moment_sel, workers, entries)
+
+
+def mp_total(mine):
+    swap = {bit: lax.ppermute(mine, "mp", [(m, m ^ bit) for m in range(4)]) for bit in (2, 3, 1)}
+    return (mine + swap[1]) + (swap[3] + swap[2])
 
 
 def solution(mesh):

time: 65.3 us -> 61.9 us (0.948)
  waiting for transfers between devices: 13.6 us -> 10.3 us
  starting transfers between devices: 15.7 us -> 15 us
    ppermute x4 -> x3, waiting for transfers between devices: 4.87 us -> 1.64 us  [mp_total(): lax.ppermute(mine, 'mp', [(m, m ^ bit) for m in range(4)])]
    ppermute x4 -> x3, starting transfers between devices: 6.54 us -> 5.62 us  [mp_total(): lax.ppermute(mine, 'mp', [(m, m ^ bit) for m in range(4)])]
  transfers between devices with their start and end apart: 10 -> 9, of which waited for: 7 -> 5; matrix products, arithmetic and copies ran while one was open for 0% -> 0% of each run, Pallas kernels for 4% -> 4%
where the time goes in v6:
time: 61.9 us; the launch traced here: 61.7 us
  blocking collectives  30.3 us (49%)
  starting transfers between devices  15 us (24%)
  waiting for transfers between devices  10.3 us (17%)
  Pallas kernels  5.34 us (9%)
  between operations  0.68 us (1%)
    all_to_all x2, blocking collectives, inside(): lax.all_to_all(array, 'replica', 0, 0, axis_index_groups=groups, tiled=True)  30.3 us
    ppermute x6, starting transfers between devices, along_y(): lax.ppermute(array, 'replica', [(r, r ^ k * inner) for r in range(workers)])  9.39 us
    ppermute x6, waiting for transfers between devices, along_y(): lax.ppermute(array, 'replica', [(r, r ^ k * inner) for r in range(workers)])  8.71 us
    ppermute x3, starting transfers between devices, mp_total(): lax.ppermute(mine, 'mp', [(m, m ^ bit) for m in range(4)])  5.62 us
    pallas_call x1, Pallas kernels, select(): pl.pallas_call(lambda *refs: select_kernel(workers, *refs), out_shape=(ja...  2.28 us
    ppermute x3, waiting for transfers between devices, mp_total(): lax.ppermute(mine, 'mp', [(m, m ^ bit) for m in range(4)])  1.64 us
    pallas_call x1, Pallas kernels, encode(): pl.pallas_call(lambda *refs: encode_kernel(workers, *refs), out_shape=(pi...  1.62 us
  transfers between devices with their start and end apart: 9, of which 5 were waited for; matrix products, arithmetic and copies ran while one was open for 0% of the time, Pallas kernels for 4%

profile of v6, /device:TPU:1, one launch (start us, length us, event | category | flops | bytes accessed | tf_op | source)
XLA Modules:
  0.0 61.7 jit_solution(4269609082132015964)
XLA Ops:
  0.6 1.6 %encode.1 = (f32[16,16,128]{2,1,0:T(8,128)S(1)}, f32[16,16,128]{2,1,0:T(8,128)S(1)}, f32[16,16,128]{2,1,0:T(8,128)S(1)}) custom-call(s32[4]{0:T(128)} %refs_0_.3, bf16[1,4,16,4096]{3,2,1,0:T(8,128)(2,1)} %refs_1_.3, f32[4,16,4096]{2,1,0:T(8,128)} %refs_2_.3), custom_call_target="tpu_custom_call" | custom-call | tf_op jit(solution)/shard_map/encode/pallas_call | solution.py:84
  2.3 3.7 %collective-permute-start = (f32[16,16,128]{2,1,0:T(8,128)S(1)}, f32[16,16,128]{2,1,0:T(8,128)S(1)}, u32[]{:S(2)}, u32[]{:S(2)}) collective-permute-start(f32[16,16,128]{2,1,0:T(8,128)S(1)} %get-tuple-element.11), channel_id=1, source_target_pairs={{0,128},{4,132},{8,136},{12,140},{16,144},{20,148},{24,152},{28,15... | collective-permute-start | bytes 393224 | tf_op jit(solution)/shard_map/ppermute | solution.py:269
  6.0 0.9 %collective-permute-start.1 = (f32[16,16,128]{2,1,0:T(8,128)S(1)}, f32[16,16,128]{2,1,0:T(8,128)S(1)}, u32[]{:S(2)}, u32[]{:S(2)}) collective-permute-start(f32[16,16,128]{2,1,0:T(8,128)S(1)} %get-tuple-element.12), channel_id=1, source_target_pairs={{0,192},{4,196},{8,200},{12,204},{16,208},{20,212},{24,216},{28,22... | collective-permute-start | bytes 393224 | tf_op jit(solution)/shard_map/ppermute | solution.py:269
  6.9 0.0 collective-permute-start.2
  6.9 2.3 %select.1 = (f32[16,16,128]{2,1,0:T(8,128)S(1)}, f32[4,16,2048]{2,1,0:T(8,128)S(1)}, bf16[4,16,2048]{2,1,0:T(8,128)(2,1)S(1)}, f32[4,16,2048]{2,1,0:T(8,128)S(1)}) custom-call(s32[4]{0:T(128)} %refs_0_.3, bf16[1,4,16,4096]{3,2,1,0:T(8,128)(2,1)} %refs_1_.3, f32[4,16,4096]{2,1,0:T(8,128)} %refs_2_.3, f32[4,16,4096]{2,1,0:T(8,128)} %refs_3_.1), custom_call_target="tpu_custom_call" | custom-call | flops 1000000 | bytes 4000000 | tf_op jit(solution)/shard_map/select/pallas_call | solution.py:129
  9.2 0.0 collective-permute-done.refs_1_
  9.2 4.4 %collective-permute-done.1.refs_2_ = f32[16,16,128]{2,1,0:T(8,128)S(1)} collective-permute-done((f32[16,16,128]{2,1,0:T(8,128)S(1)}, f32[16,16,128]{2,1,0:T(8,128)S(1)}, u32[]{:S(2)}, u32[]{:S(2)}) %collective-permute-start.1) | collective-permute-done | bytes 131104 | tf_op jit(solution)/shard_map/ppermute | solution.py:269
  13.6 0.0 collective-permute-done.2.refs_3_
  13.6 18.3 %all_to_all.10.refs_0_ = f32[16,16,128]{2,1,0:T(8,128)S(1)} all-to-all(f32[16,16,128]{2,1,0:T(8,128)S(1)} %add.16), channel_id=1, replica_groups={{0,4,8,12,16,20,24,28,32,36,40,44,48,52,56,60},{64,68,72,76,80,84,88,92..., dimensions={0} | all-to-all | bytes 262144 | tf_op jit(solution)/shard_map/all_to_all | solution.py:272
  31.9 12.0 %all_to_all.11.refs_0_ = f32[16,16,128]{2,1,0:T(8,128)S(1)} all-to-all(f32[16,16,128]{2,1,0:T(8,128)S(1)} %mean.1), channel_id=1, replica_groups={{0,4,8,12,16,20,24,28,32,36,40,44,48,52,56,60},{64,68,72,76,80,84,88,92..., dimensions={0} | all-to-all | bytes 262144 | tf_op jit(solution)/shard_map/all_to_all | solution.py:272
  43.9 1.7 %collective-permute-start.5 = (f32[16,16,128]{2,1,0:T(8,128)S(1)}, f32[16,16,128]{2,1,0:T(8,128)S(1)}, u32[]{:S(2)}, u32[]{:S(2)}) collective-permute-start(f32[16,16,128]{2,1,0:T(8,128)S(1)} %all_to_all.11.refs_0_), channel_id=1, source_target_pairs={{0,128},{4,132},{8,136},{12,140},{16,144},{20,148},{24,152},{28,15... | collective-permute-start | bytes 393224 | tf_op jit(solution)/shard_map/ppermute | solution.py:269
  45.6 3.0 %collective-permute-start.4 = (f32[16,16,128]{2,1,0:T(8,128)S(1)}, f32[16,16,128]{2,1,0:T(8,128)S(1)}, u32[]{:S(2)}, u32[]{:S(2)}) collective-permute-start(f32[16,16,128]{2,1,0:T(8,128)S(1)} %all_to_all.11.refs_0_), channel_id=1, source_target_pairs={{0,192},{4,196},{8,200},{12,204},{16,208},{20,212},{24,216},{28,22... | collective-permute-start | bytes 393224 | tf_op jit(solution)/shard_map/ppermute | solution.py:269
  48.7 0.0 collective-permute-start.3
  48.7 0.5 collective-permute-done.5.refs_3_
  49.2 2.0 %collective-permute-done.4.refs_2_ = f32[16,16,128]{2,1,0:T(8,128)S(1)} collective-permute-done((f32[16,16,128]{2,1,0:T(8,128)S(1)}, f32[16,16,128]{2,1,0:T(8,128)S(1)}, u32[]{:S(2)}, u32[]{:S(2)}) %collective-permute-start.4) | collective-permute-done | bytes 131104 | tf_op jit(solution)/shard_map/ppermute | solution.py:269
  51.2 1.8 %collective-permute-done.3.refs_1_ = f32[16,16,128]{2,1,0:T(8,128)S(1)} collective-permute-done((f32[16,16,128]{2,1,0:T(8,128)S(1)}, f32[16,16,128]{2,1,0:T(8,128)S(1)}, u32[]{:S(2)}, u32[]{:S(2)}) %collective-permute-start.3) | collective-permute-done | bytes 131104 | tf_op jit(solution)/shard_map/ppermute | solution.py:269
  53.0 0.2 squares.1
  53.2 0.4 collective-permute-start.8
  53.6 5.2 %collective-permute-start.7 = (f32[8,128]{1,0:T(8,128)S(1)}, f32[8,128]{1,0:T(8,128)S(1)}, u32[]{:S(2)}, u32[]{:S(2)}) collective-permute-start(f32[8,128]{1,0:T(8,128)S(1)} %squares.1), channel_id=1, source_target_pairs={{0,3},{1,2},{2,1},{3,0},{4,7},{5,6},{6,5},{7,4},{8,11},{9,10},{10,... | collective-permute-start | bytes 12296 | tf_op jit(solution)/shard_map/ppermute | solution.py:285
  58.8 0.0 collective-permute-start.6
  58.8 0.0 collective-permute-done.8
  58.8 1.6 %collective-permute-done.7 = f32[8,128]{1,0:T(8,128)S(1)} collective-permute-done((f32[8,128]{1,0:T(8,128)S(1)}, f32[8,128]{1,0:T(8,128)S(1)}, u32[]{:S(2)}, u32[]{:S(2)}) %collective-permute-start.7) | collective-permute-done | bytes 4128 | tf_op jit(solution)/shard_map/ppermute | solution.py:285
  60.4 0.0 collective-permute-done.6
  60.5 1.2 %update.1 = (f32[2,16,4096]{2,1,0:T(8,128)}, f32[2,16,4096]{2,1,0:T(8,128)}, bf16[1,2,16,4096]{3,2,1,0:T(8,128)(2,1)}) custom-call(f32[16,16,128]{2,1,0:T(8,128)S(1)} %all_to_all.11.refs_0_, f32[16,16,128]{2,1,0:T(8,128)S(1)} %collective-permute-done.3.refs_1_, f32[16,16,128]{2,1,0:T(8,128)S(1)} %collective-permute-done.4.refs_2_, ...), custom_call_target="tpu_custom_call" | custom-call | tf_op jit(solution)/shard_map/update/pallas_call | solution.py:239
  (3 shorter events, 0.1 us)
Async XLA Ops:
  2.3 6.9 %collective-permute-start = (f32[16,16,128]{2,1,0:T(8,128)S(1)}, f32[16,16,128]{2,1,0:T(8,128)S(1)}, u32[]{:S(2)}, u32[]{:S(2)}) collective-permute-start(f32[16,16,128]{2,1,0:T(8,128)S(1)} %get-tuple-element.11), channel_id=1, source_target_pairs={{0,128},{4,132},{8,136},{12,140},{16,144},{20,148},{24,152},{28,15... | collective-permute-start | bytes 393224 | tf_op jit(solution)/shard_map/ppermute | solution.py:269
  6.0 7.6 %collective-permute-start.1 = (f32[16,16,128]{2,1,0:T(8,128)S(1)}, f32[16,16,128]{2,1,0:T(8,128)S(1)}, u32[]{:S(2)}, u32[]{:S(2)}) collective-permute-start(f32[16,16,128]{2,1,0:T(8,128)S(1)} %get-tuple-element.12), channel_id=1, source_target_pairs={{0,192},{4,196},{8,200},{12,204},{16,208},{20,212},{24,216},{28,22... | collective-permute-start | bytes 393224 | tf_op jit(solution)/shard_map/ppermute | solution.py:269
  6.9 6.7 %collective-permute-start.2 = (f32[16,16,128]{2,1,0:T(8,128)S(1)}, f32[16,16,128]{2,1,0:T(8,128)S(1)}, u32[]{:S(2)}, u32[]{:S(2)}) collective-permute-start(f32[16,16,128]{2,1,0:T(8,128)S(1)} %get-tuple-element.13), channel_id=1, source_target_pairs={{0,64},{4,68},{8,72},{12,76},{16,80},{20,84},{24,88},{28,92},{32,9... | collective-permute-start | bytes 393224 | tf_op jit(solution)/shard_map/ppermute | solution.py:269
  43.9 5.3 %collective-permute-start.5 = (f32[16,16,128]{2,1,0:T(8,128)S(1)}, f32[16,16,128]{2,1,0:T(8,128)S(1)}, u32[]{:S(2)}, u32[]{:S(2)}) collective-permute-start(f32[16,16,128]{2,1,0:T(8,128)S(1)} %all_to_all.11.refs_0_), channel_id=1, source_target_pairs={{0,128},{4,132},{8,136},{12,140},{16,144},{20,148},{24,152},{28,15... | collective-permute-start | bytes 393224 | tf_op jit(solution)/shard_map/ppermute | solution.py:269
  45.6 5.5 %collective-permute-start.4 = (f32[16,16,128]{2,1,0:T(8,128)S(1)}, f32[16,16,128]{2,1,0:T(8,128)S(1)}, u32[]{:S(2)}, u32[]{:S(2)}) collective-permute-start(f32[16,16,128]{2,1,0:T(8,128)S(1)} %all_to_all.11.refs_0_), channel_id=1, source_target_pairs={{0,192},{4,196},{8,200},{12,204},{16,208},{20,212},{24,216},{28,22... | collective-permute-start | bytes 393224 | tf_op jit(solution)/shard_map/ppermute | solution.py:269
  48.7 4.3 %collective-permute-start.3 = (f32[16,16,128]{2,1,0:T(8,128)S(1)}, f32[16,16,128]{2,1,0:T(8,128)S(1)}, u32[]{:S(2)}, u32[]{:S(2)}) collective-permute-start(f32[16,16,128]{2,1,0:T(8,128)S(1)} %all_to_all.11.refs_0_), channel_id=1, source_target_pairs={{0,64},{4,68},{8,72},{12,76},{16,80},{20,84},{24,88},{28,92},{32,9... | collective-permute-start | bytes 393224 | tf_op jit(solution)/shard_map/ppermute | solution.py:269
  53.2 5.6 %collective-permute-start.8 = (f32[8,128]{1,0:T(8,128)S(1)}, f32[8,128]{1,0:T(8,128)S(1)}, u32[]{:S(2)}, u32[]{:S(2)}) collective-permute-start(f32[8,128]{1,0:T(8,128)S(1)} %squares.1), channel_id=1, source_target_pairs={{0,2},{1,3},{2,0},{3,1},{4,6},{5,7},{6,4},{7,5},{8,10},{9,11},{10,... | collective-permute-start | bytes 12296 | tf_op jit(solution)/shard_map/ppermute | solution.py:285
  53.6 6.9 %collective-permute-start.7 = (f32[8,128]{1,0:T(8,128)S(1)}, f32[8,128]{1,0:T(8,128)S(1)}, u32[]{:S(2)}, u32[]{:S(2)}) collective-permute-start(f32[8,128]{1,0:T(8,128)S(1)} %squares.1), channel_id=1, source_target_pairs={{0,3},{1,2},{2,1},{3,0},{4,7},{5,6},{6,5},{7,4},{8,11},{9,10},{10,... | collective-permute-start | bytes 12296 | tf_op jit(solution)/shard_map/ppermute | solution.py:285
  58.8 1.6 %collective-permute-start.6 = (f32[8,128]{1,0:T(8,128)S(1)}, f32[8,128]{1,0:T(8,128)S(1)}, u32[]{:S(2)}, u32[]{:S(2)}) collective-permute-start(f32[8,128]{1,0:T(8,128)S(1)} %squares.1), channel_id=1, source_target_pairs={{0,1},{1,0},{2,3},{3,2},{4,5},{5,4},{6,7},{7,6},{8,9},{9,8},{10,11... | collective-permute-start | bytes 12296 | tf_op jit(solution)/shard_map/ppermute | solution.py:285

commit v7 on v6

--- a/solution.py
+++ b/solution.py
@@ -7,6 +7,7 @@
 
 SYNCED = 2
 BLOCK = 128
+TILE = 8
 EPS = 1e-06
 CLIP = 0.2
 MU = 0.9
@@ -21,7 +22,6 @@
 
 
 SENT = (2, 3, 1)
-HELD = (0, 1, 3, 2)
 
 
 def in_hbm(*arrays):
@@ -179,42 +179,76 @@
     )(parts)
 
 
-def squares_kernel(workers, *refs):
-    *quarters, out_ref = refs
-    y = my_y(workers)
-    row = lax.broadcasted_iota(jnp.int32, out_ref.shape, 0)
-    total = jnp.zeros(out_ref.shape, jnp.float32)
-    sums = {k: jnp.sum(q[...] * q[...]) for k, q in zip(HELD, quarters)}
-    for k in range(0, QUARTERS, 2):
-        number, _ = place(y, k, BLOCK)
-        total = jnp.where(row == number, sums[k] + sums[k + 1], total)
-    out_ref[...] = total
-
-
-def squares(quarters, workers):
-    return pl.pallas_call(
-        lambda *refs: squares_kernel(workers, *refs),
-        out_shape=jax.ShapeDtypeStruct((8, BLOCK), jnp.float32),
-        in_specs=[VMEM] * QUARTERS,
-        out_specs=VMEM,
+def squares_kernel(quarter_ref, out_ref, held_ref):
+    quarter = quarter_ref[...]
+    out_ref[...] = jnp.broadcast_to(jnp.sum(quarter * quarter), out_ref.shape)
+    held_ref[...] = quarter
+
+
+def squares(quarter):
+    return pl.pallas_call(
+        squares_kernel,
+        out_shape=(
+            jax.ShapeDtypeStruct((TILE, BLOCK), jnp.float32),
+            jax.ShapeDtypeStruct(quarter.shape, jnp.float32),
+        ),
+        in_specs=[VMEM],
+        out_specs=(VMEM, VMEM),
         compiler_params=PARAMS,
         name="squares",
-    )(*quarters)
-
-
-def update_kernel(workers, entries, *refs):
-    quarters, refs = refs[:QUARTERS], refs[QUARTERS:]
-    squares_ref, outer_ref, local_ref, moment_ref, new_outer, new_moment, merged, outer_buf, moment_buf, merged_buf, factor_ref, sems = refs
+    )(quarter)
+
+
+def pack_kernel(core_ref, cross_ref, side_ref, early_ref, mine_ref, quarter_ref, out_ref, total_ref):
+    pieces, rows, _ = quarter_ref.shape
+    total = (mine_ref[...] + core_ref[...]) + (cross_ref[...] + side_ref[...])
+    total_ref[...] = total
+    out_ref[pieces * rows :] = total
+    for b in range(pieces):
+        out_ref[b * rows : (b + 1) * rows] = quarter_ref[b]
+
+
+def pack(swaps, early, mine, quarter):
+    pieces, rows, _ = quarter.shape
+    operands = (*swaps, early, mine, quarter)
+    return pl.pallas_call(
+        pack_kernel,
+        out_shape=(
+            jax.ShapeDtypeStruct((pieces * rows + TILE, BLOCK), jnp.float32),
+            jax.ShapeDtypeStruct(mine.shape, jnp.float32),
+        ),
+        in_specs=[VMEM] * len(operands),
+        out_specs=(VMEM, VMEM),
+        compiler_params=PARAMS,
+        name="pack",
+    )(*operands)
+
+
+def update_kernel(workers, entries, own_ref, own_total_ref, far_ref, far_total_ref, third_ref, near_ref, outer_ref, local_ref, moment_ref, new_outer, new_moment, merged, outer_buf, moment_buf, merged_buf, sems):
+    pieces, rows, _ = own_ref.shape
     width = outer_ref.shape[-1]
     y = my_y(workers)
-    factor_ref[...] = jnp.minimum(1.0, CLIP / jnp.sqrt(squares_ref[...] / entries + EPS))
+    tail = slice(pieces * rows, pieces * rows + TILE)
+
+    def factor_of(total):
+        factor = jnp.minimum(1.0, CLIP / jnp.sqrt(total / entries + EPS))
+        return jnp.concatenate([factor] * (rows // TILE), axis=0)
+
+    near = factor_of(own_total_ref[...] + near_ref[tail])
+    far = factor_of(far_total_ref[...] + third_ref[tail])
+    packed = lambda ref: lambda b: ref[b * rows : (b + 1) * rows]
+    pieces_of = lambda ref: lambda b: ref[b]
     copies = []
-    for quarter_ref, k in zip(quarters, HELD):
+    for k, piece, factor in (
+        (0, pieces_of(own_ref), near),
+        (2, pieces_of(far_ref), far),
+        (3, packed(third_ref), far),
+        (1, packed(near_ref), near),
+    ):
         number, cols = place(y, k, width)
-        factor = factor_ref[pl.ds(number, 1)]
-        for b in range(width // BLOCK):
+        for b in range(pieces):
             at = slice(b * BLOCK, (b + 1) * BLOCK)
-            grad = quarter_ref[b] * factor
+            grad = piece(b) * factor
             moment_next = MU * moment_ref[k, :, at] + grad
             outer_next = outer_ref[k, :, at] - LR * (MU * moment_next + grad)
             moment_buf[k, :, at] = moment_next
@@ -233,7 +267,7 @@
         copy.wait()
 
 
-def update(quarters, squares_sum, outer_sel, local_sel, moment_sel, workers, entries):
+def update(means, outer_sel, local_sel, moment_sel, workers, entries):
     _, rows, width = outer_sel.shape
     cols = QUARTERS * width // SYNCED
     return pl.pallas_call(
@@ -243,18 +277,17 @@
             jax.ShapeDtypeStruct((SYNCED, rows, cols), jnp.float32),
             jax.ShapeDtypeStruct((1, SYNCED, rows, cols), local_sel.dtype),
         ),
-        in_specs=[VMEM] * (QUARTERS + 4),
+        in_specs=[VMEM] * (len(means) + 3),
         out_specs=(HBM,) * 3,
         scratch_shapes=[
             pltpu.VMEM(outer_sel.shape, jnp.float32),
             pltpu.VMEM(outer_sel.shape, jnp.float32),
             pltpu.VMEM(local_sel.shape, local_sel.dtype),
-            pltpu.VMEM((8, BLOCK), jnp.float32),
             pltpu.SemaphoreType.DMA((3, QUARTERS)),
         ],
         compiler_params=PARAMS,
         name="update",
-    )(*quarters, squares_sum, outer_sel, local_sel, moment_sel)
+    )(*means, outer_sel, local_sel, moment_sel)
 
 
 def shards(local, outer, moment, plan):
@@ -275,15 +308,13 @@
     arrived = [along_y(array, k) for k, array in zip(SENT, sent)]
     own, outer_sel, local_sel, moment_sel = select(plan, local, outer, moment, workers)
     mine = add([own] + arrived)
-    quarter = inside(mean(inside(mine), workers))
-    received = {k: along_y(quarter, k) for k in SENT}
-    quarters = [quarter] + [received[k] for k in HELD[1:]]
-    return update(quarters, mp_total(squares(quarters, workers)), outer_sel, local_sel, moment_sel, workers, entries)
-
-
-def mp_total(mine):
-    swap = {bit: lax.ppermute(mine, "mp", [(m, m ^ bit) for m in range(4)]) for bit in (2, 3, 1)}
-    return (mine + swap[1]) + (swap[3] + swap[2])
+    raw = inside(mean(inside(mine), workers))
+    own_squares, quarter = squares(raw)
+    far = along_y(raw, 2)
+    swaps = [lax.ppermute(own_squares, "mp", [(m, m ^ bit) for m in range(shares)]) for bit in (1, 3, 2)]
+    packed, total = pack(swaps, far, own_squares, quarter)
+    third, near, far_total = along_y(packed, 3), along_y(packed, 1), along_y(total, 2)
+    return update((quarter, total, far, far_total, third, near), outer_sel, local_sel, moment_sel, workers, entries)
 
 
 def solution(mesh):

time: 61.9 us -> 61.9 us (level); the launches traced: 61.7 us -> 61 us
  waiting for transfers between devices: 10.3 us -> 9.26 us
  starting transfers between devices: 15 us -> 15.7 us
    ppermute x6 -> x7, waiting for transfers between devices: 8.71 us -> 7.6 us  [along_y(): lax.ppermute(array, 'replica', [(r, r ^ k * inner) for r in range(workers)])]
    ppermute x6 -> x7, starting transfers between devices: 9.39 us -> 9.75 us  [along_y(): lax.ppermute(array, 'replica', [(r, r ^ k * inner) for r in range(workers)])]
  transfers between devices with their start and end apart: 9 -> 10, of which waited for: 5 -> 4; matrix products, arithmetic and copies ran while one was open for 0% -> 0% of each run, Pallas kernels for 4% -> 4%
where the time goes in v7:
time: 61.9 us; the launch traced here: 61 us
  blocking collectives  30.2 us (49%)
  starting transfers between devices  15.7 us (25%)
  waiting for transfers between devices  9.26 us (15%)
  Pallas kernels  5.17 us (8%)
  between operations  0.69 us (1%)
    all_to_all x2, blocking collectives, inside(): lax.all_to_all(array, 'replica', 0, 0, axis_index_groups=groups, tiled=True)  30.2 us
    ppermute x7, starting transfers between devices, along_y(): lax.ppermute(array, 'replica', [(r, r ^ k * inner) for r in range(workers)])  9.75 us
    ppermute x7, waiting for transfers between devices, along_y(): lax.ppermute(array, 'replica', [(r, r ^ k * inner) for r in range(workers)])  7.6 us
    ppermute x3, starting transfers between devices, shards(): lax.ppermute(own_squares, 'mp', [(m, m ^ bit) for m in range(shares)])  5.98 us
    pallas_call x1, Pallas kernels, select(): pl.pallas_call(lambda *refs: select_kernel(workers, *refs), out_shape=(ja...  2.28 us
    ppermute x3, waiting for transfers between devices, shards(): lax.ppermute(own_squares, 'mp', [(m, m ^ bit) for m in range(shares)])  1.67 us
    pallas_call x1, Pallas kernels, encode(): pl.pallas_call(lambda *refs: encode_kernel(workers, *refs), out_shape=(pi...  1.5 us
  transfers between devices with their start and end apart: 10, of which 4 were waited for; matrix products, arithmetic and copies ran while one was open for 0% of the time, Pallas kernels for 4%

profile of v7, /device:TPU:1, one launch (start us, length us, event | category | flops | bytes accessed | tf_op | source)
XLA Modules:
  0.0 61.0 jit_solution(13365508288719552424)
XLA Ops:
  0.6 1.5 %encode.1 = (f32[16,16,128]{2,1,0:T(8,128)S(1)}, f32[16,16,128]{2,1,0:T(8,128)S(1)}, f32[16,16,128]{2,1,0:T(8,128)S(1)}) custom-call(s32[4]{0:T(128)} %refs_0_.3, bf16[1,4,16,4096]{3,2,1,0:T(8,128)(2,1)} %refs_1_.3, f32[4,16,4096]{2,1,0:T(8,128)} %refs_2_.3), custom_call_target="tpu_custom_call" | custom-call | tf_op jit(solution)/shard_map/encode/pallas_call | solution.py:84
  2.1 3.8 %collective-permute-start = (f32[16,16,128]{2,1,0:T(8,128)S(1)}, f32[16,16,128]{2,1,0:T(8,128)S(1)}, u32[]{:S(2)}, u32[]{:S(2)}) collective-permute-start(f32[16,16,128]{2,1,0:T(8,128)S(1)} %get-tuple-element.15), channel_id=1, source_target_pairs={{0,128},{4,132},{8,136},{12,140},{16,144},{20,148},{24,152},{28,15... | collective-permute-start | bytes 393224 | tf_op jit(solution)/shard_map/ppermute | solution.py:302
  5.9 0.8 %collective-permute-start.1 = (f32[16,16,128]{2,1,0:T(8,128)S(1)}, f32[16,16,128]{2,1,0:T(8,128)S(1)}, u32[]{:S(2)}, u32[]{:S(2)}) collective-permute-start(f32[16,16,128]{2,1,0:T(8,128)S(1)} %get-tuple-element.16), channel_id=1, source_target_pairs={{0,192},{4,196},{8,200},{12,204},{16,208},{20,212},{24,216},{28,22... | collective-permute-start | bytes 393224 | tf_op jit(solution)/shard_map/ppermute | solution.py:302
  6.7 0.0 collective-permute-start.2
  6.7 2.3 %select.1 = (f32[16,16,128]{2,1,0:T(8,128)S(1)}, f32[4,16,2048]{2,1,0:T(8,128)S(1)}, bf16[4,16,2048]{2,1,0:T(8,128)(2,1)S(1)}, f32[4,16,2048]{2,1,0:T(8,128)S(1)}) custom-call(s32[4]{0:T(128)} %refs_0_.3, bf16[1,4,16,4096]{3,2,1,0:T(8,128)(2,1)} %refs_1_.3, f32[4,16,4096]{2,1,0:T(8,128)} %refs_2_.3, f32[4,16,4096]{2,1,0:T(8,128)} %refs_3_.1), custom_call_target="tpu_custom_call" | custom-call | flops 1000000 | bytes 4000000 | tf_op jit(solution)/shard_map/select/pallas_call | solution.py:129
  9.0 0.0 collective-permute-done.refs_1_
  9.0 4.5 %collective-permute-done.1.refs_2_ = f32[16,16,128]{2,1,0:T(8,128)S(1)} collective-permute-done((f32[16,16,128]{2,1,0:T(8,128)S(1)}, f32[16,16,128]{2,1,0:T(8,128)S(1)}, u32[]{:S(2)}, u32[]{:S(2)}) %collective-permute-start.1) | collective-permute-done | bytes 131104 | tf_op jit(solution)/shard_map/ppermute | solution.py:302
  13.5 0.0 collective-permute-done.2.refs_3_
  13.6 18.2 %all_to_all.10.refs_0_ = f32[16,16,128]{2,1,0:T(8,128)S(1)} all-to-all(f32[16,16,128]{2,1,0:T(8,128)S(1)} %add.1), channel_id=1, replica_groups={{0,4,8,12,16,20,24,28,32,36,40,44,48,52,56,60},{64,68,72,76,80,84,88,92..., dimensions={0} | all-to-all | bytes 262144 | tf_op jit(solution)/shard_map/all_to_all | solution.py:305
  31.8 12.0 %all_to_all.11.quarter_ref = f32[16,16,128]{2,1,0:T(8,128)S(1)} all-to-all(f32[16,16,128]{2,1,0:T(8,128)S(1)} %mean.1), channel_id=1, replica_groups={{0,4,8,12,16,20,24,28,32,36,40,44,48,52,56,60},{64,68,72,76,80,84,88,92..., dimensions={0} | all-to-all | bytes 262144 | tf_op jit(solution)/shard_map/all_to_all | solution.py:305
  43.8 1.8 %collective-permute-start.6 = (f32[16,16,128]{2,1,0:T(8,128)S(1)}, f32[16,16,128]{2,1,0:T(8,128)S(1)}, u32[]{:S(2)}, u32[]{:S(2)}) collective-permute-start(f32[16,16,128]{2,1,0:T(8,128)S(1)} %all_to_all.11.quarter_ref), channel_id=1, source_target_pairs={{0,128},{4,132},{8,136},{12,140},{16,144},{20,148},{24,152},{28,15... | collective-permute-start | bytes 393224 | tf_op jit(solution)/shard_map/ppermute | solution.py:302
  45.6 0.1 squares.1
  45.7 0.4 collective-permute-start.5
  46.1 5.6 %collective-permute-start.4 = (f32[8,128]{1,0:T(8,128)S(1)}, f32[8,128]{1,0:T(8,128)S(1)}, u32[]{:S(2)}, u32[]{:S(2)}) collective-permute-start(f32[8,128]{1,0:T(8,128)S(1)} %get-tuple-element.19.mine_ref), channel_id=1, source_target_pairs={{0,3},{1,2},{2,1},{3,0},{4,7},{5,6},{6,5},{7,4},{8,11},{9,10},{10,... | collective-permute-start | bytes 12296 | tf_op jit(solution)/shard_map/ppermute | solution.py:314
  51.7 0.0 collective-permute-start.3
  51.7 0.0 collective-permute-done.5.side_ref
  51.7 1.7 %collective-permute-done.4.cross_ref = f32[8,128]{1,0:T(8,128)S(1)} collective-permute-done((f32[8,128]{1,0:T(8,128)S(1)}, f32[8,128]{1,0:T(8,128)S(1)}, u32[]{:S(2)}, u32[]{:S(2)}) %collective-permute-start.4) | collective-permute-done | bytes 4128 | tf_op jit(solution)/shard_map/ppermute | solution.py:314
  53.4 0.0 collective-permute-done.6.early_ref.refs_2_
  53.4 1.3 %collective-permute-start.9 = (f32[264,128]{1,0:T(8,128)S(1)}, f32[264,128]{1,0:T(8,128)S(1)}, u32[]{:S(2)}, u32[]{:S(2)}) collective-permute-start(f32[264,128]{1,0:T(8,128)S(1)} %get-tuple-element.21), channel_id=1, source_target_pairs={{0,64},{4,68},{8,72},{12,76},{16,80},{20,84},{24,88},{28,92},{32,9... | collective-permute-start | bytes 405512 | tf_op jit(solution)/shard_map/ppermute | solution.py:302
  54.7 0.7 %collective-permute-start.8 = (f32[264,128]{1,0:T(8,128)S(1)}, f32[264,128]{1,0:T(8,128)S(1)}, u32[]{:S(2)}, u32[]{:S(2)}) collective-permute-start(f32[264,128]{1,0:T(8,128)S(1)} %get-tuple-element.21), channel_id=1, source_target_pairs={{0,192},{4,196},{8,200},{12,204},{16,208},{20,212},{24,216},{28,22... | collective-permute-start | bytes 405512 | tf_op jit(solution)/shard_map/ppermute | solution.py:302
  55.5 1.3 %collective-permute-start.7 = (f32[8,128]{1,0:T(8,128)S(1)}, f32[8,128]{1,0:T(8,128)S(1)}, u32[]{:S(2)}, u32[]{:S(2)}) collective-permute-start(f32[8,128]{1,0:T(8,128)S(1)} %get-tuple-element.20.refs_1_), channel_id=1, source_target_pairs={{0,128},{4,132},{8,136},{12,140},{16,144},{20,148},{24,152},{28,15... | collective-permute-start | bytes 12296 | tf_op jit(solution)/shard_map/ppermute | solution.py:302
  56.7 2.7 %collective-permute-done.7.refs_3_ = f32[8,128]{1,0:T(8,128)S(1)} collective-permute-done((f32[8,128]{1,0:T(8,128)S(1)}, f32[8,128]{1,0:T(8,128)S(1)}, u32[]{:S(2)}, u32[]{:S(2)}) %collective-permute-start.7) | collective-permute-done | bytes 4128 | tf_op jit(solution)/shard_map/ppermute | solution.py:302
  59.5 0.4 collective-permute-done.8.refs_4_
  59.8 1.2 %update.1 = (f32[2,16,4096]{2,1,0:T(8,128)}, f32[2,16,4096]{2,1,0:T(8,128)}, bf16[1,2,16,4096]{3,2,1,0:T(8,128)(2,1)}) custom-call(f32[16,16,128]{2,1,0:T(8,128)S(1)} %get-tuple-element.18.quarter_ref.refs_0_, f32[8,128]{1,0:T(8,128)S(1)} %get-tuple-element.20.refs_1_, f32[16,16,128]{2,1,0:T(8,128)S(1)} %collective-permute-done.6.early_ref.refs_2_, ...), custom_call_target="tpu_custom_call" | custom-call | tf_op jit(solution)/shard_map/update/pallas_call | solution.py:273
  (5 shorter events, 0.1 us)
Async XLA Ops:
  2.1 6.9 %collective-permute-start = (f32[16,16,128]{2,1,0:T(8,128)S(1)}, f32[16,16,128]{2,1,0:T(8,128)S(1)}, u32[]{:S(2)}, u32[]{:S(2)}) collective-permute-start(f32[16,16,128]{2,1,0:T(8,128)S(1)} %get-tuple-element.15), channel_id=1, source_target_pairs={{0,128},{4,132},{8,136},{12,140},{16,144},{20,148},{24,152},{28,15... | collective-permute-start | bytes 393224 | tf_op jit(solution)/shard_map/ppermute | solution.py:302
  5.9 7.6 %collective-permute-start.1 = (f32[16,16,128]{2,1,0:T(8,128)S(1)}, f32[16,16,128]{2,1,0:T(8,128)S(1)}, u32[]{:S(2)}, u32[]{:S(2)}) collective-permute-start(f32[16,16,128]{2,1,0:T(8,128)S(1)} %get-tuple-element.16), channel_id=1, source_target_pairs={{0,192},{4,196},{8,200},{12,204},{16,208},{20,212},{24,216},{28,22... | collective-permute-start | bytes 393224 | tf_op jit(solution)/shard_map/ppermute | solution.py:302
  6.7 6.8 %collective-permute-start.2 = (f32[16,16,128]{2,1,0:T(8,128)S(1)}, f32[16,16,128]{2,1,0:T(8,128)S(1)}, u32[]{:S(2)}, u32[]{:S(2)}) collective-permute-start(f32[16,16,128]{2,1,0:T(8,128)S(1)} %get-tuple-element.17), channel_id=1, source_target_pairs={{0,64},{4,68},{8,72},{12,76},{16,80},{20,84},{24,88},{28,92},{32,9... | collective-permute-start | bytes 393224 | tf_op jit(solution)/shard_map/ppermute | solution.py:302
  43.8 9.6 %collective-permute-start.6 = (f32[16,16,128]{2,1,0:T(8,128)S(1)}, f32[16,16,128]{2,1,0:T(8,128)S(1)}, u32[]{:S(2)}, u32[]{:S(2)}) collective-permute-start(f32[16,16,128]{2,1,0:T(8,128)S(1)} %all_to_all.11.quarter_ref), channel_id=1, source_target_pairs={{0,128},{4,132},{8,136},{12,140},{16,144},{20,148},{24,152},{28,15... | collective-permute-start | bytes 393224 | tf_op jit(solution)/shard_map/ppermute | solution.py:302
  45.7 6.0 %collective-permute-start.5 = (f32[8,128]{1,0:T(8,128)S(1)}, f32[8,128]{1,0:T(8,128)S(1)}, u32[]{:S(2)}, u32[]{:S(2)}) collective-permute-start(f32[8,128]{1,0:T(8,128)S(1)} %get-tuple-element.19.mine_ref), channel_id=1, source_target_pairs={{0,2},{1,3},{2,0},{3,1},{4,6},{5,7},{6,4},{7,5},{8,10},{9,11},{10,... | collective-permute-start | bytes 12296 | tf_op jit(solution)/shard_map/ppermute | solution.py:314
  46.1 7.2 %collective-permute-start.4 = (f32[8,128]{1,0:T(8,128)S(1)}, f32[8,128]{1,0:T(8,128)S(1)}, u32[]{:S(2)}, u32[]{:S(2)}) collective-permute-start(f32[8,128]{1,0:T(8,128)S(1)} %get-tuple-element.19.mine_ref), channel_id=1, source_target_pairs={{0,3},{1,2},{2,1},{3,0},{4,7},{5,6},{6,5},{7,4},{8,11},{9,10},{10,... | collective-permute-start | bytes 12296 | tf_op jit(solution)/shard_map/ppermute | solution.py:314
  51.7 1.7 %collective-permute-start.3 = (f32[8,128]{1,0:T(8,128)S(1)}, f32[8,128]{1,0:T(8,128)S(1)}, u32[]{:S(2)}, u32[]{:S(2)}) collective-permute-start(f32[8,128]{1,0:T(8,128)S(1)} %get-tuple-element.19.mine_ref), channel_id=1, source_target_pairs={{0,1},{1,0},{2,3},{3,2},{4,5},{5,4},{6,7},{7,6},{8,9},{9,8},{10,11... | collective-permute-start | bytes 12296 | tf_op jit(solution)/shard_map/ppermute | solution.py:314
  53.4 6.1 %collective-permute-start.9 = (f32[264,128]{1,0:T(8,128)S(1)}, f32[264,128]{1,0:T(8,128)S(1)}, u32[]{:S(2)}, u32[]{:S(2)}) collective-permute-start(f32[264,128]{1,0:T(8,128)S(1)} %get-tuple-element.21), channel_id=1, source_target_pairs={{0,64},{4,68},{8,72},{12,76},{16,80},{20,84},{24,88},{28,92},{32,9... | collective-permute-start | bytes 405512 | tf_op jit(solution)/shard_map/ppermute | solution.py:302
  54.7 5.1 %collective-permute-start.8 = (f32[264,128]{1,0:T(8,128)S(1)}, f32[264,128]{1,0:T(8,128)S(1)}, u32[]{:S(2)}, u32[]{:S(2)}) collective-permute-start(f32[264,128]{1,0:T(8,128)S(1)} %get-tuple-element.21), channel_id=1, source_target_pairs={{0,192},{4,196},{8,200},{12,204},{16,208},{20,212},{24,216},{28,22... | collective-permute-start | bytes 405512 | tf_op jit(solution)/shard_map/ppermute | solution.py:302
  55.5 4.0 %collective-permute-start.7 = (f32[8,128]{1,0:T(8,128)S(1)}, f32[8,128]{1,0:T(8,128)S(1)}, u32[]{:S(2)}, u32[]{:S(2)}) collective-permute-start(f32[8,128]{1,0:T(8,128)S(1)} %get-tuple-element.20.refs_1_), channel_id=1, source_target_pairs={{0,128},{4,132},{8,136},{12,140},{16,144},{20,148},{24,152},{28,15... | collective-permute-start | bytes 12296 | tf_op jit(solution)/shard_map/ppermute | solution.py:302

commit v8 on v7

--- a/solution.py
+++ b/solution.py
@@ -224,7 +224,7 @@
     )(*operands)
 
 
-def update_kernel(workers, entries, own_ref, own_total_ref, far_ref, far_total_ref, third_ref, near_ref, outer_ref, local_ref, moment_ref, new_outer, new_moment, merged, outer_buf, moment_buf, merged_buf, sems):
+def update_kernel(workers, entries, own_ref, own_total_ref, far_ref, near_ref, third_ref, far_total_ref, outer_ref, local_ref, moment_ref, new_outer, new_moment, merged, outer_buf, moment_buf, merged_buf, sems):
     pieces, rows, _ = own_ref.shape
     width = outer_ref.shape[-1]
     y = my_y(workers)
@@ -313,8 +313,8 @@
     far = along_y(raw, 2)
     swaps = [lax.ppermute(own_squares, "mp", [(m, m ^ bit) for m in range(shares)]) for bit in (1, 3, 2)]
     packed, total = pack(swaps, far, own_squares, quarter)
-    third, near, far_total = along_y(packed, 3), along_y(packed, 1), along_y(total, 2)
-    return update((quarter, total, far, far_total, third, near), outer_sel, local_sel, moment_sel, workers, entries)
+    near, third, far_total = along_y(packed, 1), along_y(packed, 3), along_y(total, 2)
+    return update((quarter, total, far, near, third, far_total), outer_sel, local_sel, moment_sel, workers, entries)
 
 
 def solution(mesh):

time: 61.9 us -> 62.8 us (1.015)
  the two profiles are of different devices: /device:TPU:1 before, /device:TPU:8 now
where the time goes in v8:
time: 62.8 us; the launch traced here: 62.6 us
  blocking collectives  34 us (54%)
  starting transfers between devices  12.9 us (21%)
  waiting for transfers between devices  9.77 us (16%)
  Pallas kernels  5.24 us (8%)
  between operations  0.67 us (1%)
    all_to_all x2, blocking collectives, inside(): lax.all_to_all(array, 'replica', 0, 0, axis_index_groups=groups, tiled=True)  34 us
    ppermute x7, starting transfers between devices, along_y(): lax.ppermute(array, 'replica', [(r, r ^ k * inner) for r in range(workers)])  10.6 us
    ppermute x7, waiting for transfers between devices, along_y(): lax.ppermute(array, 'replica', [(r, r ^ k * inner) for r in range(workers)])  8.24 us
    pallas_call x1, Pallas kernels, select(): pl.pallas_call(lambda *refs: select_kernel(workers, *refs), out_shape=(ja...  2.28 us
    ppermute x3, starting transfers between devices, shards(): lax.ppermute(own_squares, 'mp', [(m, m ^ bit) for m in range(shares)])  2.23 us
    pallas_call x1, Pallas kernels, encode(): pl.pallas_call(lambda *refs: encode_kernel(workers, *refs), out_shape=(pi...  1.57 us
    ppermute x3, waiting for transfers between devices, shards(): lax.ppermute(own_squares, 'mp', [(m, m ^ bit) for m in range(shares)])  1.53 us
  transfers between devices with their start and end apart: 10, of which 6 were waited for; matrix products, arithmetic and copies ran while one was open for 0% of the time, Pallas kernels for 4%

profile of v8, /device:TPU:8, one launch (start us, length us, event | category | flops | bytes accessed | tf_op | source)
XLA Modules:
  0.0 62.6 jit_solution(15696212864772763286)
XLA Ops:
  0.6 1.6 %encode.1 = (f32[16,16,128]{2,1,0:T(8,128)S(1)}, f32[16,16,128]{2,1,0:T(8,128)S(1)}, f32[16,16,128]{2,1,0:T(8,128)S(1)}) custom-call(s32[4]{0:T(128)} %refs_0_.3, bf16[1,4,16,4096]{3,2,1,0:T(8,128)(2,1)} %refs_1_.3, f32[4,16,4096]{2,1,0:T(8,128)} %refs_2_.3), custom_call_target="tpu_custom_call" | custom-call | tf_op jit(solution)/shard_map/encode/pallas_call | solution.py:84
  2.2 2.5 %collective-permute-start = (f32[16,16,128]{2,1,0:T(8,128)S(1)}, f32[16,16,128]{2,1,0:T(8,128)S(1)}, u32[]{:S(2)}, u32[]{:S(2)}) collective-permute-start(f32[16,16,128]{2,1,0:T(8,128)S(1)} %get-tuple-element.15), channel_id=1, source_target_pairs={{0,128},{4,132},{8,136},{12,140},{16,144},{20,148},{24,152},{28,15... | collective-permute-start | bytes 393224 | tf_op jit(solution)/shard_map/ppermute | solution.py:302
  4.8 1.2 %collective-permute-start.1 = (f32[16,16,128]{2,1,0:T(8,128)S(1)}, f32[16,16,128]{2,1,0:T(8,128)S(1)}, u32[]{:S(2)}, u32[]{:S(2)}) collective-permute-start(f32[16,16,128]{2,1,0:T(8,128)S(1)} %get-tuple-element.16), channel_id=1, source_target_pairs={{0,192},{4,196},{8,200},{12,204},{16,208},{20,212},{24,216},{28,22... | collective-permute-start | bytes 393224 | tf_op jit(solution)/shard_map/ppermute | solution.py:302
  5.9 1.1 %collective-permute-start.2 = (f32[16,16,128]{2,1,0:T(8,128)S(1)}, f32[16,16,128]{2,1,0:T(8,128)S(1)}, u32[]{:S(2)}, u32[]{:S(2)}) collective-permute-start(f32[16,16,128]{2,1,0:T(8,128)S(1)} %get-tuple-element.17), channel_id=1, source_target_pairs={{0,64},{4,68},{8,72},{12,76},{16,80},{20,84},{24,88},{28,92},{32,9... | collective-permute-start | bytes 393224 | tf_op jit(solution)/shard_map/ppermute | solution.py:302
  7.0 2.3 %select.1 = (f32[16,16,128]{2,1,0:T(8,128)S(1)}, f32[4,16,2048]{2,1,0:T(8,128)S(1)}, bf16[4,16,2048]{2,1,0:T(8,128)(2,1)S(1)}, f32[4,16,2048]{2,1,0:T(8,128)S(1)}) custom-call(s32[4]{0:T(128)} %refs_0_.3, bf16[1,4,16,4096]{3,2,1,0:T(8,128)(2,1)} %refs_1_.3, f32[4,16,4096]{2,1,0:T(8,128)} %refs_2_.3, f32[4,16,4096]{2,1,0:T(8,128)} %refs_3_.1), custom_call_target="tpu_custom_call" | custom-call | flops 1000000 | bytes 4000000 | tf_op jit(solution)/shard_map/select/pallas_call | solution.py:129
  9.3 0.5 collective-permute-done.refs_1_
  9.8 2.1 %collective-permute-done.1.refs_2_ = f32[16,16,128]{2,1,0:T(8,128)S(1)} collective-permute-done((f32[16,16,128]{2,1,0:T(8,128)S(1)}, f32[16,16,128]{2,1,0:T(8,128)S(1)}, u32[]{:S(2)}, u32[]{:S(2)}) %collective-permute-start.1) | collective-permute-done | bytes 131104 | tf_op jit(solution)/shard_map/ppermute | solution.py:302
  11.8 0.3 collective-permute-done.2.refs_3_
  12.2 20.9 %all_to_all.10.refs_0_ = f32[16,16,128]{2,1,0:T(8,128)S(1)} all-to-all(f32[16,16,128]{2,1,0:T(8,128)S(1)} %add.1), channel_id=1, replica_groups={{0,4,8,12,16,20,24,28,32,36,40,44,48,52,56,60},{64,68,72,76,80,84,88,92..., dimensions={0} | all-to-all | bytes 262144 | tf_op jit(solution)/shard_map/all_to_all | solution.py:305
  33.1 13.1 %all_to_all.11.quarter_ref = f32[16,16,128]{2,1,0:T(8,128)S(1)} all-to-all(f32[16,16,128]{2,1,0:T(8,128)S(1)} %mean.1), channel_id=1, replica_groups={{0,4,8,12,16,20,24,28,32,36,40,44,48,52,56,60},{64,68,72,76,80,84,88,92..., dimensions={0} | all-to-all | bytes 262144 | tf_op jit(solution)/shard_map/all_to_all | solution.py:305
  46.3 2.3 %collective-permute-start.6 = (f32[16,16,128]{2,1,0:T(8,128)S(1)}, f32[16,16,128]{2,1,0:T(8,128)S(1)}, u32[]{:S(2)}, u32[]{:S(2)}) collective-permute-start(f32[16,16,128]{2,1,0:T(8,128)S(1)} %all_to_all.11.quarter_ref), channel_id=1, source_target_pairs={{0,128},{4,132},{8,136},{12,140},{16,144},{20,148},{24,152},{28,15... | collective-permute-start | bytes 393224 | tf_op jit(solution)/shard_map/ppermute | solution.py:302
  48.6 0.1 squares.1
  48.7 0.7 %collective-permute-start.5 = (f32[8,128]{1,0:T(8,128)S(1)}, f32[8,128]{1,0:T(8,128)S(1)}, u32[]{:S(2)}, u32[]{:S(2)}) collective-permute-start(f32[8,128]{1,0:T(8,128)S(1)} %get-tuple-element.19.mine_ref), channel_id=1, source_target_pairs={{0,2},{1,3},{2,0},{3,1},{4,6},{5,7},{6,4},{7,5},{8,10},{9,11},{10,... | collective-permute-start | bytes 12296 | tf_op jit(solution)/shard_map/ppermute | solution.py:314
  49.4 0.0 collective-permute-start.4
  49.4 1.5 %collective-permute-start.3 = (f32[8,128]{1,0:T(8,128)S(1)}, f32[8,128]{1,0:T(8,128)S(1)}, u32[]{:S(2)}, u32[]{:S(2)}) collective-permute-start(f32[8,128]{1,0:T(8,128)S(1)} %get-tuple-element.19.mine_ref), channel_id=1, source_target_pairs={{0,1},{1,0},{2,3},{3,2},{4,5},{5,4},{6,7},{7,6},{8,9},{9,8},{10,11... | collective-permute-start | bytes 12296 | tf_op jit(solution)/shard_map/ppermute | solution.py:314
  51.0 1.5 %collective-permute-done.5.side_ref = f32[8,128]{1,0:T(8,128)S(1)} collective-permute-done((f32[8,128]{1,0:T(8,128)S(1)}, f32[8,128]{1,0:T(8,128)S(1)}, u32[]{:S(2)}, u32[]{:S(2)}) %collective-permute-start.5) | collective-permute-done | bytes 4128 | tf_op jit(solution)/shard_map/ppermute | solution.py:314
  52.4 0.0 collective-permute-done.4.cross_ref
  52.5 0.0 collective-permute-done.3.core_ref
  52.5 0.3 collective-permute-done.6.early_ref.refs_2_
  52.8 0.8 %collective-permute-start.8 = (f32[264,128]{1,0:T(8,128)S(1)}, f32[264,128]{1,0:T(8,128)S(1)}, u32[]{:S(2)}, u32[]{:S(2)}) collective-permute-start(f32[264,128]{1,0:T(8,128)S(1)} %get-tuple-element.21), channel_id=1, source_target_pairs={{0,192},{4,196},{8,200},{12,204},{16,208},{20,212},{24,216},{28,22... | collective-permute-start | bytes 405512 | tf_op jit(solution)/shard_map/ppermute | solution.py:302
  53.6 2.7 %collective-permute-start.7 = (f32[264,128]{1,0:T(8,128)S(1)}, f32[264,128]{1,0:T(8,128)S(1)}, u32[]{:S(2)}, u32[]{:S(2)}) collective-permute-start(f32[264,128]{1,0:T(8,128)S(1)} %get-tuple-element.21), channel_id=1, source_target_pairs={{0,64},{4,68},{8,72},{12,76},{16,80},{20,84},{24,88},{28,92},{32,9... | collective-permute-start | bytes 405512 | tf_op jit(solution)/shard_map/ppermute | solution.py:302
  56.3 0.0 collective-permute-start.9
  56.3 5.1 %collective-permute-done.9.refs_5_ = f32[8,128]{1,0:T(8,128)S(1)} collective-permute-done((f32[8,128]{1,0:T(8,128)S(1)}, f32[8,128]{1,0:T(8,128)S(1)}, u32[]{:S(2)}, u32[]{:S(2)}) %collective-permute-start.9) | collective-permute-done | bytes 4128 | tf_op jit(solution)/shard_map/ppermute | solution.py:302
  61.4 1.2 %update.1 = (f32[2,16,4096]{2,1,0:T(8,128)}, f32[2,16,4096]{2,1,0:T(8,128)}, bf16[1,2,16,4096]{3,2,1,0:T(8,128)(2,1)}) custom-call(f32[16,16,128]{2,1,0:T(8,128)S(1)} %get-tuple-element.18.quarter_ref.refs_0_, f32[8,128]{1,0:T(8,128)S(1)} %get-tuple-element.20.refs_1_, f32[16,16,128]{2,1,0:T(8,128)S(1)} %collective-permute-done.6.early_ref.refs_2_, ...), custom_call_target="tpu_custom_call" | custom-call | tf_op jit(solution)/shard_map/update/pallas_call | solution.py:273
  (5 shorter events, 0.1 us)
Async XLA Ops:
  2.2 7.6 %collective-permute-start = (f32[16,16,128]{2,1,0:T(8,128)S(1)}, f32[16,16,128]{2,1,0:T(8,128)S(1)}, u32[]{:S(2)}, u32[]{:S(2)}) collective-permute-start(f32[16,16,128]{2,1,0:T(8,128)S(1)} %get-tuple-element.15), channel_id=1, source_target_pairs={{0,128},{4,132},{8,136},{12,140},{16,144},{20,148},{24,152},{28,15... | collective-permute-start | bytes 393224 | tf_op jit(solution)/shard_map/ppermute | solution.py:302
  4.8 7.1 %collective-permute-start.1 = (f32[16,16,128]{2,1,0:T(8,128)S(1)}, f32[16,16,128]{2,1,0:T(8,128)S(1)}, u32[]{:S(2)}, u32[]{:S(2)}) collective-permute-start(f32[16,16,128]{2,1,0:T(8,128)S(1)} %get-tuple-element.16), channel_id=1, source_target_pairs={{0,192},{4,196},{8,200},{12,204},{16,208},{20,212},{24,216},{28,22... | collective-permute-start | bytes 393224 | tf_op jit(solution)/shard_map/ppermute | solution.py:302
  5.9 6.2 %collective-permute-start.2 = (f32[16,16,128]{2,1,0:T(8,128)S(1)}, f32[16,16,128]{2,1,0:T(8,128)S(1)}, u32[]{:S(2)}, u32[]{:S(2)}) collective-permute-start(f32[16,16,128]{2,1,0:T(8,128)S(1)} %get-tuple-element.17), channel_id=1, source_target_pairs={{0,64},{4,68},{8,72},{12,76},{16,80},{20,84},{24,88},{28,92},{32,9... | collective-permute-start | bytes 393224 | tf_op jit(solution)/shard_map/ppermute | solution.py:302
  46.3 6.5 %collective-permute-start.6 = (f32[16,16,128]{2,1,0:T(8,128)S(1)}, f32[16,16,128]{2,1,0:T(8,128)S(1)}, u32[]{:S(2)}, u32[]{:S(2)}) collective-permute-start(f32[16,16,128]{2,1,0:T(8,128)S(1)} %all_to_all.11.quarter_ref), channel_id=1, source_target_pairs={{0,128},{4,132},{8,136},{12,140},{16,144},{20,148},{24,152},{28,15... | collective-permute-start | bytes 393224 | tf_op jit(solution)/shard_map/ppermute | solution.py:302
  48.7 3.7 %collective-permute-start.5 = (f32[8,128]{1,0:T(8,128)S(1)}, f32[8,128]{1,0:T(8,128)S(1)}, u32[]{:S(2)}, u32[]{:S(2)}) collective-permute-start(f32[8,128]{1,0:T(8,128)S(1)} %get-tuple-element.19.mine_ref), channel_id=1, source_target_pairs={{0,2},{1,3},{2,0},{3,1},{4,6},{5,7},{6,4},{7,5},{8,10},{9,11},{10,... | collective-permute-start | bytes 12296 | tf_op jit(solution)/shard_map/ppermute | solution.py:314
  49.4 3.1 %collective-permute-start.4 = (f32[8,128]{1,0:T(8,128)S(1)}, f32[8,128]{1,0:T(8,128)S(1)}, u32[]{:S(2)}, u32[]{:S(2)}) collective-permute-start(f32[8,128]{1,0:T(8,128)S(1)} %get-tuple-element.19.mine_ref), channel_id=1, source_target_pairs={{0,3},{1,2},{2,1},{3,0},{4,7},{5,6},{6,5},{7,4},{8,11},{9,10},{10,... | collective-permute-start | bytes 12296 | tf_op jit(solution)/shard_map/ppermute | solution.py:314
  49.4 3.1 %collective-permute-start.3 = (f32[8,128]{1,0:T(8,128)S(1)}, f32[8,128]{1,0:T(8,128)S(1)}, u32[]{:S(2)}, u32[]{:S(2)}) collective-permute-start(f32[8,128]{1,0:T(8,128)S(1)} %get-tuple-element.19.mine_ref), channel_id=1, source_target_pairs={{0,1},{1,0},{2,3},{3,2},{4,5},{5,4},{6,7},{7,6},{8,9},{9,8},{10,11... | collective-permute-start | bytes 12296 | tf_op jit(solution)/shard_map/ppermute | solution.py:314
  52.8 8.7 %collective-permute-start.8 = (f32[264,128]{1,0:T(8,128)S(1)}, f32[264,128]{1,0:T(8,128)S(1)}, u32[]{:S(2)}, u32[]{:S(2)}) collective-permute-start(f32[264,128]{1,0:T(8,128)S(1)} %get-tuple-element.21), channel_id=1, source_target_pairs={{0,192},{4,196},{8,200},{12,204},{16,208},{20,212},{24,216},{28,22... | collective-permute-start | bytes 405512 | tf_op jit(solution)/shard_map/ppermute | solution.py:302
  53.6 7.8 %collective-permute-start.7 = (f32[264,128]{1,0:T(8,128)S(1)}, f32[264,128]{1,0:T(8,128)S(1)}, u32[]{:S(2)}, u32[]{:S(2)}) collective-permute-start(f32[264,128]{1,0:T(8,128)S(1)} %get-tuple-element.21), channel_id=1, source_target_pairs={{0,64},{4,68},{8,72},{12,76},{16,80},{20,84},{24,88},{28,92},{32,9... | collective-permute-start | bytes 405512 | tf_op jit(solution)/shard_map/ppermute | solution.py:302
  56.3 5.1 %collective-permute-start.9 = (f32[8,128]{1,0:T(8,128)S(1)}, f32[8,128]{1,0:T(8,128)S(1)}, u32[]{:S(2)}, u32[]{:S(2)}) collective-permute-start(f32[8,128]{1,0:T(8,128)S(1)} %get-tuple-element.20.refs_1_), channel_id=1, source_target_pairs={{0,128},{4,132},{8,136},{12,140},{16,144},{20,148},{24,152},{28,15... | collective-permute-start | bytes 12296 | tf_op jit(solution)/shard_map/ppermute | solution.py:302

commit v9 on v7

--- a/solution.py
+++ b/solution.py
@@ -61,20 +61,15 @@
             copy.start()
     y = my_y(workers)
     plan_copy.wait()
-    waited = set()
+    for f in range(frags):
+        for copy in copies(f):
+            copy.wait()
     for k, out_ref in zip(SENT, out_refs):
         number, cols = place(y, k, width)
         f = plan_ref[number]
-        if k // 2 not in waited:
-            waited.add(k // 2)
-            for copy in copies(f):
-                copy.wait()
         for b in range(width // BLOCK):
             at = pl.ds(pl.multiple_of(cols.start + b * BLOCK, BLOCK), BLOCK)
             out_ref[b] = coded(outer_ref[f, :, at], local_ref[f, :, at])
-    for number in range(SYNCED, frags):
-        for copy in copies(plan_ref[number]):
-            copy.wait()
 
 
 def encode(plan, local, outer, workers):

time: 61.9 us -> 62.1 us (level)
  no operation moved by 1% of the time
where the time goes in v9:
time: 62.1 us; the launch traced here: 61.5 us
  blocking collectives  30 us (48%)
  starting transfers between devices  15.8 us (25%)
  waiting for transfers between devices  9.71 us (16%)
  Pallas kernels  5.32 us (9%)
  between operations  0.69 us (1%)
    all_to_all x2, blocking collectives, inside(): lax.all_to_all(array, 'replica', 0, 0, axis_index_groups=groups, tiled=True)  30 us
    ppermute x7, starting transfers between devices, along_y(): lax.ppermute(array, 'replica', [(r, r ^ k * inner) for r in range(workers)])  9.83 us
    ppermute x7, waiting for transfers between devices, along_y(): lax.ppermute(array, 'replica', [(r, r ^ k * inner) for r in range(workers)])  8.04 us
    ppermute x3, starting transfers between devices, shards(): lax.ppermute(own_squares, 'mp', [(m, m ^ bit) for m in range(shares)])  5.98 us
    pallas_call x1, Pallas kernels, select(): pl.pallas_call(lambda *refs: select_kernel(workers, *refs), out_shape=(ja...  2.28 us
    ppermute x3, waiting for transfers between devices, shards(): lax.ppermute(own_squares, 'mp', [(m, m ^ bit) for m in range(shares)])  1.67 us
    pallas_call x1, Pallas kernels, encode(): pl.pallas_call(lambda *refs: encode_kernel(workers, *refs), out_shape=(pi...  1.65 us
  transfers between devices with their start and end apart: 10, of which 4 were waited for; matrix products, arithmetic and copies ran while one was open for 0% of the time, Pallas kernels for 4%

profile of v9, /device:TPU:1, one launch (start us, length us, event | category | flops | bytes accessed | tf_op | source)
XLA Modules:
  0.0 61.5 jit_solution(3506567904665531706)
XLA Ops:
  0.6 1.6 %encode.1 = (f32[16,16,128]{2,1,0:T(8,128)S(1)}, f32[16,16,128]{2,1,0:T(8,128)S(1)}, f32[16,16,128]{2,1,0:T(8,128)S(1)}) custom-call(s32[4]{0:T(128)} %refs_0_.3, bf16[1,4,16,4096]{3,2,1,0:T(8,128)(2,1)} %refs_1_.3, f32[4,16,4096]{2,1,0:T(8,128)} %refs_2_.3), custom_call_target="tpu_custom_call" | custom-call | tf_op jit(solution)/shard_map/encode/pallas_call | solution.py:79
  2.3 3.8 %collective-permute-start = (f32[16,16,128]{2,1,0:T(8,128)S(1)}, f32[16,16,128]{2,1,0:T(8,128)S(1)}, u32[]{:S(2)}, u32[]{:S(2)}) collective-permute-start(f32[16,16,128]{2,1,0:T(8,128)S(1)} %get-tuple-element.15), channel_id=1, source_target_pairs={{0,128},{4,132},{8,136},{12,140},{16,144},{20,148},{24,152},{28,15... | collective-permute-start | bytes 393224 | tf_op jit(solution)/shard_map/ppermute | solution.py:297
  6.1 0.8 %collective-permute-start.1 = (f32[16,16,128]{2,1,0:T(8,128)S(1)}, f32[16,16,128]{2,1,0:T(8,128)S(1)}, u32[]{:S(2)}, u32[]{:S(2)}) collective-permute-start(f32[16,16,128]{2,1,0:T(8,128)S(1)} %get-tuple-element.16), channel_id=1, source_target_pairs={{0,192},{4,196},{8,200},{12,204},{16,208},{20,212},{24,216},{28,22... | collective-permute-start | bytes 393224 | tf_op jit(solution)/shard_map/ppermute | solution.py:297
  6.9 0.0 collective-permute-start.2
  6.9 2.3 %select.1 = (f32[16,16,128]{2,1,0:T(8,128)S(1)}, f32[4,16,2048]{2,1,0:T(8,128)S(1)}, bf16[4,16,2048]{2,1,0:T(8,128)(2,1)S(1)}, f32[4,16,2048]{2,1,0:T(8,128)S(1)}) custom-call(s32[4]{0:T(128)} %refs_0_.3, bf16[1,4,16,4096]{3,2,1,0:T(8,128)(2,1)} %refs_1_.3, f32[4,16,4096]{2,1,0:T(8,128)} %refs_2_.3, f32[4,16,4096]{2,1,0:T(8,128)} %refs_3_.1), custom_call_target="tpu_custom_call" | custom-call | flops 1000000 | bytes 4000000 | tf_op jit(solution)/shard_map/select/pallas_call | solution.py:124
  9.2 0.0 collective-permute-done.refs_1_
  9.2 4.6 %collective-permute-done.1.refs_2_ = f32[16,16,128]{2,1,0:T(8,128)S(1)} collective-permute-done((f32[16,16,128]{2,1,0:T(8,128)S(1)}, f32[16,16,128]{2,1,0:T(8,128)S(1)}, u32[]{:S(2)}, u32[]{:S(2)}) %collective-permute-start.1) | collective-permute-done | bytes 131104 | tf_op jit(solution)/shard_map/ppermute | solution.py:297
  13.8 0.0 collective-permute-done.2.refs_3_
  13.9 18.0 %all_to_all.10.refs_0_ = f32[16,16,128]{2,1,0:T(8,128)S(1)} all-to-all(f32[16,16,128]{2,1,0:T(8,128)S(1)} %add.1), channel_id=1, replica_groups={{0,4,8,12,16,20,24,28,32,36,40,44,48,52,56,60},{64,68,72,76,80,84,88,92..., dimensions={0} | all-to-all | bytes 262144 | tf_op jit(solution)/shard_map/all_to_all | solution.py:300
  31.9 12.0 %all_to_all.11.quarter_ref = f32[16,16,128]{2,1,0:T(8,128)S(1)} all-to-all(f32[16,16,128]{2,1,0:T(8,128)S(1)} %mean.1), channel_id=1, replica_groups={{0,4,8,12,16,20,24,28,32,36,40,44,48,52,56,60},{64,68,72,76,80,84,88,92..., dimensions={0} | all-to-all | bytes 262144 | tf_op jit(solution)/shard_map/all_to_all | solution.py:300
  43.9 1.9 %collective-permute-start.6 = (f32[16,16,128]{2,1,0:T(8,128)S(1)}, f32[16,16,128]{2,1,0:T(8,128)S(1)}, u32[]{:S(2)}, u32[]{:S(2)}) collective-permute-start(f32[16,16,128]{2,1,0:T(8,128)S(1)} %all_to_all.11.quarter_ref), channel_id=1, source_target_pairs={{0,128},{4,132},{8,136},{12,140},{16,144},{20,148},{24,152},{28,15... | collective-permute-start | bytes 393224 | tf_op jit(solution)/shard_map/ppermute | solution.py:297
  45.8 0.1 squares.1
  45.9 0.4 collective-permute-start.5
  46.3 5.6 %collective-permute-start.4 = (f32[8,128]{1,0:T(8,128)S(1)}, f32[8,128]{1,0:T(8,128)S(1)}, u32[]{:S(2)}, u32[]{:S(2)}) collective-permute-start(f32[8,128]{1,0:T(8,128)S(1)} %get-tuple-element.19.mine_ref), channel_id=1, source_target_pairs={{0,3},{1,2},{2,1},{3,0},{4,7},{5,6},{6,5},{7,4},{8,11},{9,10},{10,... | collective-permute-start | bytes 12296 | tf_op jit(solution)/shard_map/ppermute | solution.py:309
  51.9 0.0 collective-permute-start.3
  51.9 0.0 collective-permute-done.5.side_ref
  51.9 1.7 %collective-permute-done.4.cross_ref = f32[8,128]{1,0:T(8,128)S(1)} collective-permute-done((f32[8,128]{1,0:T(8,128)S(1)}, f32[8,128]{1,0:T(8,128)S(1)}, u32[]{:S(2)}, u32[]{:S(2)}) %collective-permute-start.4) | collective-permute-done | bytes 4128 | tf_op jit(solution)/shard_map/ppermute | solution.py:309
  53.6 0.0 collective-permute-done.3.core_ref
  53.6 1.3 %collective-permute-start.9 = (f32[264,128]{1,0:T(8,128)S(1)}, f32[264,128]{1,0:T(8,128)S(1)}, u32[]{:S(2)}, u32[]{:S(2)}) collective-permute-start(f32[264,128]{1,0:T(8,128)S(1)} %get-tuple-element.21), channel_id=1, source_target_pairs={{0,64},{4,68},{8,72},{12,76},{16,80},{20,84},{24,88},{28,92},{32,9... | collective-permute-start | bytes 405512 | tf_op jit(solution)/shard_map/ppermute | solution.py:297
  54.9 0.5 collective-permute-start.8
  55.4 1.5 %collective-permute-start.7 = (f32[8,128]{1,0:T(8,128)S(1)}, f32[8,128]{1,0:T(8,128)S(1)}, u32[]{:S(2)}, u32[]{:S(2)}) collective-permute-start(f32[8,128]{1,0:T(8,128)S(1)} %get-tuple-element.20.refs_1_), channel_id=1, source_target_pairs={{0,128},{4,132},{8,136},{12,140},{16,144},{20,148},{24,152},{28,15... | collective-permute-start | bytes 12296 | tf_op jit(solution)/shard_map/ppermute | solution.py:297
  57.0 2.5 %collective-permute-done.7.refs_3_ = f32[8,128]{1,0:T(8,128)S(1)} collective-permute-done((f32[8,128]{1,0:T(8,128)S(1)}, f32[8,128]{1,0:T(8,128)S(1)}, u32[]{:S(2)}, u32[]{:S(2)}) %collective-permute-start.7) | collective-permute-done | bytes 4128 | tf_op jit(solution)/shard_map/ppermute | solution.py:297
  59.5 0.9 %collective-permute-done.8.refs_4_ = f32[264,128]{1,0:T(8,128)S(1)} collective-permute-done((f32[264,128]{1,0:T(8,128)S(1)}, f32[264,128]{1,0:T(8,128)S(1)}, u32[]{:S(2)}, u32[]{:S(2)}) %collective-permute-start.8) | collective-permute-done | bytes 135200 | tf_op jit(solution)/shard_map/ppermute | solution.py:297
  60.4 1.2 %update.1 = (f32[2,16,4096]{2,1,0:T(8,128)}, f32[2,16,4096]{2,1,0:T(8,128)}, bf16[1,2,16,4096]{3,2,1,0:T(8,128)(2,1)}) custom-call(f32[16,16,128]{2,1,0:T(8,128)S(1)} %get-tuple-element.18.quarter_ref.refs_0_, f32[8,128]{1,0:T(8,128)S(1)} %get-tuple-element.20.refs_1_, f32[16,16,128]{2,1,0:T(8,128)S(1)} %collective-permute-done.6.early_ref.refs_2_, ...), custom_call_target="tpu_custom_call" | custom-call | tf_op jit(solution)/shard_map/update/pallas_call | solution.py:268
  (5 shorter events, 0.1 us)
Async XLA Ops:
  2.3 6.9 %collective-permute-start = (f32[16,16,128]{2,1,0:T(8,128)S(1)}, f32[16,16,128]{2,1,0:T(8,128)S(1)}, u32[]{:S(2)}, u32[]{:S(2)}) collective-permute-start(f32[16,16,128]{2,1,0:T(8,128)S(1)} %get-tuple-element.15), channel_id=1, source_target_pairs={{0,128},{4,132},{8,136},{12,140},{16,144},{20,148},{24,152},{28,15... | collective-permute-start | bytes 393224 | tf_op jit(solution)/shard_map/ppermute | solution.py:297
  6.1 7.7 %collective-permute-start.1 = (f32[16,16,128]{2,1,0:T(8,128)S(1)}, f32[16,16,128]{2,1,0:T(8,128)S(1)}, u32[]{:S(2)}, u32[]{:S(2)}) collective-permute-start(f32[16,16,128]{2,1,0:T(8,128)S(1)} %get-tuple-element.16), channel_id=1, source_target_pairs={{0,192},{4,196},{8,200},{12,204},{16,208},{20,212},{24,216},{28,22... | collective-permute-start | bytes 393224 | tf_op jit(solution)/shard_map/ppermute | solution.py:297
  6.9 6.9 %collective-permute-start.2 = (f32[16,16,128]{2,1,0:T(8,128)S(1)}, f32[16,16,128]{2,1,0:T(8,128)S(1)}, u32[]{:S(2)}, u32[]{:S(2)}) collective-permute-start(f32[16,16,128]{2,1,0:T(8,128)S(1)} %get-tuple-element.17), channel_id=1, source_target_pairs={{0,64},{4,68},{8,72},{12,76},{16,80},{20,84},{24,88},{28,92},{32,9... | collective-permute-start | bytes 393224 | tf_op jit(solution)/shard_map/ppermute | solution.py:297
  43.9 9.7 %collective-permute-start.6 = (f32[16,16,128]{2,1,0:T(8,128)S(1)}, f32[16,16,128]{2,1,0:T(8,128)S(1)}, u32[]{:S(2)}, u32[]{:S(2)}) collective-permute-start(f32[16,16,128]{2,1,0:T(8,128)S(1)} %all_to_all.11.quarter_ref), channel_id=1, source_target_pairs={{0,128},{4,132},{8,136},{12,140},{16,144},{20,148},{24,152},{28,15... | collective-permute-start | bytes 393224 | tf_op jit(solution)/shard_map/ppermute | solution.py:297
  45.9 6.0 %collective-permute-start.5 = (f32[8,128]{1,0:T(8,128)S(1)}, f32[8,128]{1,0:T(8,128)S(1)}, u32[]{:S(2)}, u32[]{:S(2)}) collective-permute-start(f32[8,128]{1,0:T(8,128)S(1)} %get-tuple-element.19.mine_ref), channel_id=1, source_target_pairs={{0,2},{1,3},{2,0},{3,1},{4,6},{5,7},{6,4},{7,5},{8,10},{9,11},{10,... | collective-permute-start | bytes 12296 | tf_op jit(solution)/shard_map/ppermute | solution.py:309
  46.3 7.2 %collective-permute-start.4 = (f32[8,128]{1,0:T(8,128)S(1)}, f32[8,128]{1,0:T(8,128)S(1)}, u32[]{:S(2)}, u32[]{:S(2)}) collective-permute-start(f32[8,128]{1,0:T(8,128)S(1)} %get-tuple-element.19.mine_ref), channel_id=1, source_target_pairs={{0,3},{1,2},{2,1},{3,0},{4,7},{5,6},{6,5},{7,4},{8,11},{9,10},{10,... | collective-permute-start | bytes 12296 | tf_op jit(solution)/shard_map/ppermute | solution.py:309
  51.9 1.7 %collective-permute-start.3 = (f32[8,128]{1,0:T(8,128)S(1)}, f32[8,128]{1,0:T(8,128)S(1)}, u32[]{:S(2)}, u32[]{:S(2)}) collective-permute-start(f32[8,128]{1,0:T(8,128)S(1)} %get-tuple-element.19.mine_ref), channel_id=1, source_target_pairs={{0,1},{1,0},{2,3},{3,2},{4,5},{5,4},{6,7},{7,6},{8,9},{9,8},{10,11... | collective-permute-start | bytes 12296 | tf_op jit(solution)/shard_map/ppermute | solution.py:309
  53.6 5.9 %collective-permute-start.9 = (f32[264,128]{1,0:T(8,128)S(1)}, f32[264,128]{1,0:T(8,128)S(1)}, u32[]{:S(2)}, u32[]{:S(2)}) collective-permute-start(f32[264,128]{1,0:T(8,128)S(1)} %get-tuple-element.21), channel_id=1, source_target_pairs={{0,64},{4,68},{8,72},{12,76},{16,80},{20,84},{24,88},{28,92},{32,9... | collective-permute-start | bytes 405512 | tf_op jit(solution)/shard_map/ppermute | solution.py:297
  54.9 5.4 %collective-permute-start.8 = (f32[264,128]{1,0:T(8,128)S(1)}, f32[264,128]{1,0:T(8,128)S(1)}, u32[]{:S(2)}, u32[]{:S(2)}) collective-permute-start(f32[264,128]{1,0:T(8,128)S(1)} %get-tuple-element.21), channel_id=1, source_target_pairs={{0,192},{4,196},{8,200},{12,204},{16,208},{20,212},{24,216},{28,22... | collective-permute-start | bytes 405512 | tf_op jit(solution)/shard_map/ppermute | solution.py:297
  55.4 4.1 %collective-permute-start.7 = (f32[8,128]{1,0:T(8,128)S(1)}, f32[8,128]{1,0:T(8,128)S(1)}, u32[]{:S(2)}, u32[]{:S(2)}) collective-permute-start(f32[8,128]{1,0:T(8,128)S(1)} %get-tuple-element.20.refs_1_), channel_id=1, source_target_pairs={{0,128},{4,132},{8,136},{12,140},{16,144},{20,148},{24,152},{28,15... | collective-permute-start | bytes 12296 | tf_op jit(solution)/shard_map/ppermute | solution.py:297

commit v10 on v6

--- a/solution.py
+++ b/solution.py
@@ -61,20 +61,15 @@
             copy.start()
     y = my_y(workers)
     plan_copy.wait()
-    waited = set()
+    for f in range(frags):
+        for copy in copies(f):
+            copy.wait()
     for k, out_ref in zip(SENT, out_refs):
         number, cols = place(y, k, width)
         f = plan_ref[number]
-        if k // 2 not in waited:
-            waited.add(k // 2)
-            for copy in copies(f):
-                copy.wait()
         for b in range(width // BLOCK):
             at = pl.ds(pl.multiple_of(cols.start + b * BLOCK, BLOCK), BLOCK)
             out_ref[b] = coded(outer_ref[f, :, at], local_ref[f, :, at])
-    for number in range(SYNCED, frags):
-        for copy in copies(plan_ref[number]):
-            copy.wait()
 
 
 def encode(plan, local, outer, workers):
@@ -179,27 +174,36 @@
     )(parts)
 
 
-def squares_kernel(workers, *refs):
-    *quarters, out_ref = refs
-    y = my_y(workers)
-    row = lax.broadcasted_iota(jnp.int32, out_ref.shape, 0)
-    total = jnp.zeros(out_ref.shape, jnp.float32)
-    sums = {k: jnp.sum(q[...] * q[...]) for k, q in zip(HELD, quarters)}
-    for k in range(0, QUARTERS, 2):
-        number, _ = place(y, k, BLOCK)
-        total = jnp.where(row == number, sums[k] + sums[k + 1], total)
-    out_ref[...] = total
+def tile_of(y, own, other):
+    row = lax.broadcasted_iota(jnp.int32, (8, BLOCK), 0)
+    number, _ = place(y, 0, BLOCK)
+    return jnp.where(row == number, own, jnp.where(row == SYNCED - 1 - number, other, 0.0))
+
+
+def first_squares_kernel(workers, own_ref, third_ref, far_ref, out_ref):
+    own, third, far = [jnp.sum(ref[...] * ref[...]) for ref in (own_ref, third_ref, far_ref)]
+    out_ref[...] = tile_of(my_y(workers), own, far + third)
+
+
+def last_squares_kernel(workers, near_ref, first_ref, out_ref):
+    near = jnp.sum(near_ref[...] * near_ref[...])
+    out_ref[...] = first_ref[...] + tile_of(my_y(workers), near, 0.0)
 
 
 def squares(quarters, workers):
-    return pl.pallas_call(
-        lambda *refs: squares_kernel(workers, *refs),
-        out_shape=jax.ShapeDtypeStruct((8, BLOCK), jnp.float32),
-        in_specs=[VMEM] * QUARTERS,
-        out_specs=VMEM,
-        compiler_params=PARAMS,
-        name="squares",
-    )(*quarters)
+    own, near, third, far = quarters
+
+    def call(kernel, *operands):
+        return pl.pallas_call(
+            lambda *refs: kernel(workers, *refs),
+            out_shape=jax.ShapeDtypeStruct((8, BLOCK), jnp.float32),
+            in_specs=[VMEM] * len(operands),
+            out_specs=VMEM,
+            compiler_params=PARAMS,
+            name="squares",
+        )(*operands)
+
+    return call(last_squares_kernel, near, call(first_squares_kernel, own, third, far))
 
 
 def update_kernel(workers, entries, *refs):

time: 61.9 us -> 61.9 us (level)
    ppermute x3, starting transfers between devices: 5.62 us -> 6.47 us  [mp_total(): lax.ppermute(mine, 'mp', [(m, m ^ bit) for m in range(4)])]
where the time goes in v10:
time: 61.9 us; the launch traced here: 61.7 us
  blocking collectives  30 us (48%)
  starting transfers between devices  15.5 us (25%)
  waiting for transfers between devices  9.91 us (16%)
  Pallas kernels  5.51 us (9%)
  between operations  0.69 us (1%)
    all_to_all x2, blocking collectives, inside(): lax.all_to_all(array, 'replica', 0, 0, axis_index_groups=groups, tiled=True)  30 us
    ppermute x6, starting transfers between devices, along_y(): lax.ppermute(array, 'replica', [(r, r ^ k * inner) for r in range(workers)])  9.06 us
    ppermute x6, waiting for transfers between devices, along_y(): lax.ppermute(array, 'replica', [(r, r ^ k * inner) for r in range(workers)])  8.27 us
    ppermute x3, starting transfers between devices, mp_total(): lax.ppermute(mine, 'mp', [(m, m ^ bit) for m in range(4)])  6.47 us
    pallas_call x1, Pallas kernels, select(): pl.pallas_call(lambda *refs: select_kernel(workers, *refs), out_shape=(ja...  2.28 us
    pallas_call x1, Pallas kernels, encode(): pl.pallas_call(lambda *refs: encode_kernel(workers, *refs), out_shape=(pi...  1.65 us
    ppermute x3, waiting for transfers between devices, mp_total(): lax.ppermute(mine, 'mp', [(m, m ^ bit) for m in range(4)])  1.64 us
  transfers between devices with their start and end apart: 9, of which 5 were waited for; matrix products, arithmetic and copies ran while one was open for 0% of the time, Pallas kernels for 4%

profile of v10, /device:TPU:1, one launch (start us, length us, event | category | flops | bytes accessed | tf_op | source)
XLA Modules:
  0.0 61.7 jit_solution(5507674005586217611)
XLA Ops:
  0.6 1.6 %encode.1 = (f32[16,16,128]{2,1,0:T(8,128)S(1)}, f32[16,16,128]{2,1,0:T(8,128)S(1)}, f32[16,16,128]{2,1,0:T(8,128)S(1)}) custom-call(s32[4]{0:T(128)} %refs_0_.3, bf16[1,4,16,4096]{3,2,1,0:T(8,128)(2,1)} %refs_1_.3, f32[4,16,4096]{2,1,0:T(8,128)} %refs_2_.3), custom_call_target="tpu_custom_call" | custom-call | tf_op jit(solution)/shard_map/encode/pallas_call | solution.py:79
  2.3 3.8 %collective-permute-start = (f32[16,16,128]{2,1,0:T(8,128)S(1)}, f32[16,16,128]{2,1,0:T(8,128)S(1)}, u32[]{:S(2)}, u32[]{:S(2)}) collective-permute-start(f32[16,16,128]{2,1,0:T(8,128)S(1)} %get-tuple-element.11), channel_id=1, source_target_pairs={{0,128},{4,132},{8,136},{12,140},{16,144},{20,148},{24,152},{28,15... | collective-permute-start | bytes 393224 | tf_op jit(solution)/shard_map/ppermute | solution.py:273
  6.1 0.8 %collective-permute-start.1 = (f32[16,16,128]{2,1,0:T(8,128)S(1)}, f32[16,16,128]{2,1,0:T(8,128)S(1)}, u32[]{:S(2)}, u32[]{:S(2)}) collective-permute-start(f32[16,16,128]{2,1,0:T(8,128)S(1)} %get-tuple-element.12), channel_id=1, source_target_pairs={{0,192},{4,196},{8,200},{12,204},{16,208},{20,212},{24,216},{28,22... | collective-permute-start | bytes 393224 | tf_op jit(solution)/shard_map/ppermute | solution.py:273
  6.9 0.0 collective-permute-start.2
  6.9 2.3 %select.1 = (f32[16,16,128]{2,1,0:T(8,128)S(1)}, f32[4,16,2048]{2,1,0:T(8,128)S(1)}, bf16[4,16,2048]{2,1,0:T(8,128)(2,1)S(1)}, f32[4,16,2048]{2,1,0:T(8,128)S(1)}) custom-call(s32[4]{0:T(128)} %refs_0_.3, bf16[1,4,16,4096]{3,2,1,0:T(8,128)(2,1)} %refs_1_.3, f32[4,16,4096]{2,1,0:T(8,128)} %refs_2_.3, f32[4,16,4096]{2,1,0:T(8,128)} %refs_3_.1), custom_call_target="tpu_custom_call" | custom-call | flops 1000000 | bytes 4000000 | tf_op jit(solution)/shard_map/select/pallas_call | solution.py:124
  9.2 0.0 collective-permute-done.refs_1_
  9.2 4.6 %collective-permute-done.1.refs_2_ = f32[16,16,128]{2,1,0:T(8,128)S(1)} collective-permute-done((f32[16,16,128]{2,1,0:T(8,128)S(1)}, f32[16,16,128]{2,1,0:T(8,128)S(1)}, u32[]{:S(2)}, u32[]{:S(2)}) %collective-permute-start.1) | collective-permute-done | bytes 131104 | tf_op jit(solution)/shard_map/ppermute | solution.py:273
  13.8 0.0 collective-permute-done.2.refs_3_
  13.9 18.0 %all_to_all.10.refs_0_ = f32[16,16,128]{2,1,0:T(8,128)S(1)} all-to-all(f32[16,16,128]{2,1,0:T(8,128)S(1)} %add.16), channel_id=1, replica_groups={{0,4,8,12,16,20,24,28,32,36,40,44,48,52,56,60},{64,68,72,76,80,84,88,92..., dimensions={0} | all-to-all | bytes 262144 | tf_op jit(solution)/shard_map/all_to_all | solution.py:276
  31.9 12.0 %all_to_all.11.refs_0_ = f32[16,16,128]{2,1,0:T(8,128)S(1)} all-to-all(f32[16,16,128]{2,1,0:T(8,128)S(1)} %mean.1), channel_id=1, replica_groups={{0,4,8,12,16,20,24,28,32,36,40,44,48,52,56,60},{64,68,72,76,80,84,88,92..., dimensions={0} | all-to-all | bytes 262144 | tf_op jit(solution)/shard_map/all_to_all | solution.py:276
  43.9 1.9 %collective-permute-start.5 = (f32[16,16,128]{2,1,0:T(8,128)S(1)}, f32[16,16,128]{2,1,0:T(8,128)S(1)}, u32[]{:S(2)}, u32[]{:S(2)}) collective-permute-start(f32[16,16,128]{2,1,0:T(8,128)S(1)} %all_to_all.11.refs_0_), channel_id=1, source_target_pairs={{0,128},{4,132},{8,136},{12,140},{16,144},{20,148},{24,152},{28,15... | collective-permute-start | bytes 393224 | tf_op jit(solution)/shard_map/ppermute | solution.py:273
  45.8 2.6 %collective-permute-start.4 = (f32[16,16,128]{2,1,0:T(8,128)S(1)}, f32[16,16,128]{2,1,0:T(8,128)S(1)}, u32[]{:S(2)}, u32[]{:S(2)}) collective-permute-start(f32[16,16,128]{2,1,0:T(8,128)S(1)} %all_to_all.11.refs_0_), channel_id=1, source_target_pairs={{0,192},{4,196},{8,200},{12,204},{16,208},{20,212},{24,216},{28,22... | collective-permute-start | bytes 393224 | tf_op jit(solution)/shard_map/ppermute | solution.py:273
  48.4 0.0 collective-permute-start.3
  48.4 0.9 %collective-permute-done.5.refs_2_.refs_3_ = f32[16,16,128]{2,1,0:T(8,128)S(1)} collective-permute-done((f32[16,16,128]{2,1,0:T(8,128)S(1)}, f32[16,16,128]{2,1,0:T(8,128)S(1)}, u32[]{:S(2)}, u32[]{:S(2)}) %collective-permute-start.5) | collective-permute-done | bytes 131104 | tf_op jit(solution)/shard_map/ppermute | solution.py:273
  49.2 2.1 %collective-permute-done.4.refs_1_.refs_2_ = f32[16,16,128]{2,1,0:T(8,128)S(1)} collective-permute-done((f32[16,16,128]{2,1,0:T(8,128)S(1)}, f32[16,16,128]{2,1,0:T(8,128)S(1)}, u32[]{:S(2)}, u32[]{:S(2)}) %collective-permute-start.4) | collective-permute-done | bytes 131104 | tf_op jit(solution)/shard_map/ppermute | solution.py:273
  51.3 0.2 squares.2.refs_1_
  51.5 0.7 %collective-permute-done.3.refs_0_.refs_1_ = f32[16,16,128]{2,1,0:T(8,128)S(1)} collective-permute-done((f32[16,16,128]{2,1,0:T(8,128)S(1)}, f32[16,16,128]{2,1,0:T(8,128)S(1)}, u32[]{:S(2)}, u32[]{:S(2)}) %collective-permute-start.3) | collective-permute-done | bytes 131104 | tf_op jit(solution)/shard_map/ppermute | solution.py:273
  52.2 0.2 squares.3
  52.3 0.4 collective-permute-start.8
  52.7 6.1 %collective-permute-start.7 = (f32[8,128]{1,0:T(8,128)S(1)}, f32[8,128]{1,0:T(8,128)S(1)}, u32[]{:S(2)}, u32[]{:S(2)}) collective-permute-start(f32[8,128]{1,0:T(8,128)S(1)} %squares.3), channel_id=1, source_target_pairs={{0,3},{1,2},{2,1},{3,0},{4,7},{5,6},{6,5},{7,4},{8,11},{9,10},{10,... | collective-permute-start | bytes 12296 | tf_op jit(solution)/shard_map/ppermute | solution.py:289
  58.8 0.0 collective-permute-start.6
  58.8 0.0 collective-permute-done.8
  58.8 1.6 %collective-permute-done.7 = f32[8,128]{1,0:T(8,128)S(1)} collective-permute-done((f32[8,128]{1,0:T(8,128)S(1)}, f32[8,128]{1,0:T(8,128)S(1)}, u32[]{:S(2)}, u32[]{:S(2)}) %collective-permute-start.7) | collective-permute-done | bytes 4128 | tf_op jit(solution)/shard_map/ppermute | solution.py:289
  60.5 1.2 %update.1 = (f32[2,16,4096]{2,1,0:T(8,128)}, f32[2,16,4096]{2,1,0:T(8,128)}, bf16[1,2,16,4096]{3,2,1,0:T(8,128)(2,1)}) custom-call(f32[16,16,128]{2,1,0:T(8,128)S(1)} %all_to_all.11.refs_0_, f32[16,16,128]{2,1,0:T(8,128)S(1)} %collective-permute-done.3.refs_0_.refs_1_, f32[16,16,128]{2,1,0:T(8,128)S(1)} %collective-permute-done.4.refs_1_.refs_2_, ...), custom_call_target="tpu_custom_call" | custom-call | tf_op jit(solution)/shard_map/update/pallas_call | solution.py:243
  (4 shorter events, 0.1 us)
Async XLA Ops:
  2.3 6.9 %collective-permute-start = (f32[16,16,128]{2,1,0:T(8,128)S(1)}, f32[16,16,128]{2,1,0:T(8,128)S(1)}, u32[]{:S(2)}, u32[]{:S(2)}) collective-permute-start(f32[16,16,128]{2,1,0:T(8,128)S(1)} %get-tuple-element.11), channel_id=1, source_target_pairs={{0,128},{4,132},{8,136},{12,140},{16,144},{20,148},{24,152},{28,15... | collective-permute-start | bytes 393224 | tf_op jit(solution)/shard_map/ppermute | solution.py:273
  6.1 7.7 %collective-permute-start.1 = (f32[16,16,128]{2,1,0:T(8,128)S(1)}, f32[16,16,128]{2,1,0:T(8,128)S(1)}, u32[]{:S(2)}, u32[]{:S(2)}) collective-permute-start(f32[16,16,128]{2,1,0:T(8,128)S(1)} %get-tuple-element.12), channel_id=1, source_target_pairs={{0,192},{4,196},{8,200},{12,204},{16,208},{20,212},{24,216},{28,22... | collective-permute-start | bytes 393224 | tf_op jit(solution)/shard_map/ppermute | solution.py:273
  6.9 6.9 %collective-permute-start.2 = (f32[16,16,128]{2,1,0:T(8,128)S(1)}, f32[16,16,128]{2,1,0:T(8,128)S(1)}, u32[]{:S(2)}, u32[]{:S(2)}) collective-permute-start(f32[16,16,128]{2,1,0:T(8,128)S(1)} %get-tuple-element.13), channel_id=1, source_target_pairs={{0,64},{4,68},{8,72},{12,76},{16,80},{20,84},{24,88},{28,92},{32,9... | collective-permute-start | bytes 393224 | tf_op jit(solution)/shard_map/ppermute | solution.py:273
  43.9 5.3 %collective-permute-start.5 = (f32[16,16,128]{2,1,0:T(8,128)S(1)}, f32[16,16,128]{2,1,0:T(8,128)S(1)}, u32[]{:S(2)}, u32[]{:S(2)}) collective-permute-start(f32[16,16,128]{2,1,0:T(8,128)S(1)} %all_to_all.11.refs_0_), channel_id=1, source_target_pairs={{0,128},{4,132},{8,136},{12,140},{16,144},{20,148},{24,152},{28,15... | collective-permute-start | bytes 393224 | tf_op jit(solution)/shard_map/ppermute | solution.py:273
  45.8 5.5 %collective-permute-start.4 = (f32[16,16,128]{2,1,0:T(8,128)S(1)}, f32[16,16,128]{2,1,0:T(8,128)S(1)}, u32[]{:S(2)}, u32[]{:S(2)}) collective-permute-start(f32[16,16,128]{2,1,0:T(8,128)S(1)} %all_to_all.11.refs_0_), channel_id=1, source_target_pairs={{0,192},{4,196},{8,200},{12,204},{16,208},{20,212},{24,216},{28,22... | collective-permute-start | bytes 393224 | tf_op jit(solution)/shard_map/ppermute | solution.py:273
  48.4 3.8 %collective-permute-start.3 = (f32[16,16,128]{2,1,0:T(8,128)S(1)}, f32[16,16,128]{2,1,0:T(8,128)S(1)}, u32[]{:S(2)}, u32[]{:S(2)}) collective-permute-start(f32[16,16,128]{2,1,0:T(8,128)S(1)} %all_to_all.11.refs_0_), channel_id=1, source_target_pairs={{0,64},{4,68},{8,72},{12,76},{16,80},{20,84},{24,88},{28,92},{32,9... | collective-permute-start | bytes 393224 | tf_op jit(solution)/shard_map/ppermute | solution.py:273
  52.3 6.5 %collective-permute-start.8 = (f32[8,128]{1,0:T(8,128)S(1)}, f32[8,128]{1,0:T(8,128)S(1)}, u32[]{:S(2)}, u32[]{:S(2)}) collective-permute-start(f32[8,128]{1,0:T(8,128)S(1)} %squares.3), channel_id=1, source_target_pairs={{0,2},{1,3},{2,0},{3,1},{4,6},{5,7},{6,4},{7,5},{8,10},{9,11},{10,... | collective-permute-start | bytes 12296 | tf_op jit(solution)/shard_map/ppermute | solution.py:289
  52.7 7.7 %collective-permute-start.7 = (f32[8,128]{1,0:T(8,128)S(1)}, f32[8,128]{1,0:T(8,128)S(1)}, u32[]{:S(2)}, u32[]{:S(2)}) collective-permute-start(f32[8,128]{1,0:T(8,128)S(1)} %squares.3), channel_id=1, source_target_pairs={{0,3},{1,2},{2,1},{3,0},{4,7},{5,6},{6,5},{7,4},{8,11},{9,10},{10,... | collective-permute-start | bytes 12296 | tf_op jit(solution)/shard_map/ppermute | solution.py:289
  58.8 1.6 %collective-permute-start.6 = (f32[8,128]{1,0:T(8,128)S(1)}, f32[8,128]{1,0:T(8,128)S(1)}, u32[]{:S(2)}, u32[]{:S(2)}) collective-permute-start(f32[8,128]{1,0:T(8,128)S(1)} %squares.3), channel_id=1, source_target_pairs={{0,1},{1,0},{2,3},{3,2},{4,5},{5,4},{6,7},{7,6},{8,9},{9,8},{10,11... | collective-permute-start | bytes 12296 | tf_op jit(solution)/shard_map/ppermute | solution.py:289
